TPU v7x, 32 devices: a whole 2x2x4 slice. The times are simulated.
32 devices in a mesh: wide: 8 (over y, x, core), narrow: 4 (over z).
Axes of the slice: x: 2, y: 2, z: 4, core: 2. Of those that a mesh axis runs over, the one named last changes fastest.
Arguments:
- tokens: bfloat16 [32768, 768], P(('wide', 'narrow')), may hold values from -5.6 to 5.6
- cotangent: bfloat16 [32768, 768], P(('wide', 'narrow')), may hold values from -6 to 6
- qkv_w: bfloat16 [2, 768, 2304], P(None, ('wide', 'narrow'))
- out_w: bfloat16 [2, 768, 768], P(None, ('wide', 'narrow')), may hold values from -0.3125 to 0.3125
- in_w: bfloat16 [2, 768, 3072], P(None, ('wide', 'narrow')), may hold values from -0.21875 to 0.21875
- in_b: bfloat16 [2, 3072], P(None, ('wide', 'narrow')), may hold values from -3 to 3
- out2_w: bfloat16 [2, 3072, 768], P(None, ('wide', 'narrow')), may hold values from -0.109375 to 0.109375
- bias_rows: bfloat16 [2, 6, 768], P(None, None, ('wide', 'narrow')), may hold values from -3 to 3
- gain_rows: bfloat16 [2, 2, 768], P(None, None, ('wide', 'narrow')), may hold values from 0.25 to 1.75
- conv_w: bfloat16 [2, 12, 33], replicated, may hold values from -1 to 1
Outputs:
- output: bfloat16 [32768, 768], P(('wide', 'narrow'))
- grad_input: float32 [32768, 768], P(('wide', 'narrow'))
- grad_qkv_w: float32 [2, 768, 2304], P(None, ('wide', 'narrow'))
- grad_out_w: float32 [2, 768, 768], P(None, ('wide', 'narrow'))
- grad_in_w: float32 [2, 768, 3072], P(None, ('wide', 'narrow'))
- grad_in_b: float32 [2, 3072], P(None, ('wide', 'narrow'))
- grad_out2_w: float32 [2, 3072, 768], P(None, ('wide', 'narrow'))
- grad_bias_rows: float32 [2, 6, 768], P(None, None, ('wide', 'narrow'))
- grad_gain_rows: float32 [2, 2, 768], P(None, None, ('wide', 'narrow'))
- grad_conv_w: float32 [2, 12, 33], replicated
All inputs are finite; a program needn't handle non-finite values.
Results may differ from a plain program's by a relative error of at most 0.02.
Values may be sent and summed in bfloat16 or wider, within the bound.
A program may use at most 384 MiB of HBM per device.

v0:
```python
import jax
import jax.numpy as jnp
from jax import lax
from jax.sharding import PartitionSpec as P

MODEL_WIDTH = 768
HEADS = 12
HEAD_DIM = 64
LANDMARKS = 64
KSIZE = 33
NS_ITERS = 6


HIGH_ACCURACY = lax.Precision.HIGHEST
EPSILON = 1e-05


def layer_norm(values_in, gain_row, shift_row):
    center = values_in - jnp.mean(values_in, axis=-1, keepdims=True)
    spread = jnp.mean(center * center, axis=-1, keepdims=True)
    return center * lax.rsqrt(spread + EPSILON) * gain_row + shift_row


def newton(adjacent):
    identity = jnp.eye(adjacent.shape[-1], dtype=jnp.float32)
    score_scale = 1.0 / jnp.sum(adjacent * adjacent, axis=(1, 2), keepdims=True)
    pseudo_inverse = jnp.swapaxes(adjacent, 1, 2) * score_scale
    for repeat in range(NS_ITERS):
        product = jnp.einsum("hij,hjk->hik", adjacent, pseudo_inverse, precision=HIGH_ACCURACY)
        bracket = 7.0 * identity - product
        bracket = 15.0 * identity - jnp.einsum(
            "hij,hjk->hik", product, bracket, precision=HIGH_ACCURACY
        )
        bracket = 13.0 * identity - jnp.einsum(
            "hij,hjk->hik", product, bracket, precision=HIGH_ACCURACY
        )
        pseudo_inverse = 0.25 * jnp.einsum(
            "hij,hjk->hik", pseudo_inverse, bracket, precision=HIGH_ACCURACY
        )
    return pseudo_inverse


def column_softmax(scores):
    return jax.nn.softmax(scores * HEAD_DIM ** (-0.5), axis=1)


def row_softmax(scores):
    return jax.nn.softmax(scores * HEAD_DIM ** (-0.5), axis=2)


def gelu_exact(values_in):
    return jax.nn.gelu(values_in, approximate=False)


def attention_forward(inputs, qkv_full, bias_query, bias_value, kernel):
    sequence_length = inputs.shape[0]
    seg_len = sequence_length // LANDMARKS
    inputs_low = inputs.astype(jnp.bfloat16)
    mixed_rows = jnp.dot(inputs_low, qkv_full, preferred_element_type=jnp.float32)
    queries = (mixed_rows[:, :MODEL_WIDTH] + bias_query).astype(jnp.bfloat16)
    key_rows = mixed_rows[:, MODEL_WIDTH : 2 * MODEL_WIDTH].astype(jnp.bfloat16)
    value_rows = (mixed_rows[:, 2 * MODEL_WIDTH :] + bias_value).astype(jnp.bfloat16)
    query_per_head = queries.reshape(sequence_length, HEADS, HEAD_DIM)
    key_per_head = key_rows.reshape(sequence_length, HEADS, HEAD_DIM)
    value_per_head = value_rows.reshape(sequence_length, HEADS, HEAD_DIM)
    query_anchors = jnp.mean(
        query_per_head.astype(jnp.float32).reshape(LANDMARKS, seg_len, HEADS, HEAD_DIM), axis=1
    ).astype(jnp.bfloat16)
    key_anchors = jnp.mean(
        key_per_head.astype(jnp.float32).reshape(LANDMARKS, seg_len, HEADS, HEAD_DIM), axis=1
    ).astype(jnp.bfloat16)
    raw_query = jnp.einsum(
        "yfb,rfb->fry", query_per_head, key_anchors, preferred_element_type=jnp.float32
    )
    softmax_query_anchors, pull_query = jax.vjp(column_softmax, raw_query)
    unscaled_anchors = jnp.einsum(
        "xow,zow->oxz", query_anchors, key_anchors, preferred_element_type=jnp.float32
    )
    softmax_anchor_pairs, pull_land = jax.vjp(row_softmax, unscaled_anchors)
    unscaled_keys = jnp.einsum(
        "prb,irb->rpi", query_anchors, key_per_head, preferred_element_type=jnp.float32
    )
    softmax_key_anchors, pull_keys = jax.vjp(row_softmax, unscaled_keys)
    pseudo_inverse, pull_newton = jax.vjp(newton, softmax_anchor_pairs)
    reduced_key_softmax = softmax_key_anchors.astype(jnp.bfloat16)
    anchor_summary = jnp.einsum(
        "ika,aip->ikp", reduced_key_softmax, value_per_head, preferred_element_type=jnp.float32
    )
    small_product = jnp.einsum(
        "ies,isr->ier", pseudo_inverse, anchor_summary, precision=HIGH_ACCURACY
    ).astype(jnp.bfloat16)
    reduced_query_softmax = softmax_query_anchors.astype(jnp.bfloat16)
    attended_output = jnp.einsum(
        "oer,oel->rol", reduced_query_softmax, small_product, preferred_element_type=jnp.float32
    ).reshape(sequence_length, MODEL_WIDTH)
    kernel_cols = jnp.repeat(kernel, HEAD_DIM, axis=0)
    radius = KSIZE // 2
    padded = jnp.pad(value_rows, ((radius, radius), (0, 0)))
    conv_out = jnp.zeros_like(attended_output)
    for offset in range(KSIZE):
        conv_out = conv_out + kernel_cols[:, offset] * padded[
            offset : offset + sequence_length
        ].astype(jnp.float32)
    context = (attended_output + conv_out).astype(jnp.bfloat16)
    kept = (
        inputs_low,
        query_per_head,
        key_per_head,
        value_per_head,
        query_anchors,
        key_anchors,
        pull_query,
        pull_land,
        pull_keys,
        pull_newton,
        reduced_key_softmax,
        anchor_summary,
        pseudo_inverse,
        small_product,
        reduced_query_softmax,
        padded,
        kernel_cols,
    )
    return (context, kept)


def attention_backward(grad_ctx, kept, qkv_full):
    (
        inputs_low,
        query_per_head,
        key_per_head,
        value_per_head,
        query_anchors,
        key_anchors,
        pull_query,
        pull_land,
        pull_keys,
        pull_newton,
        reduced_key_softmax,
        anchor_summary,
        pseudo_inverse,
        small_product,
        reduced_query_softmax,
        padded,
        kernel_cols,
    ) = kept
    sequence_length = grad_ctx.shape[0]
    seg_len = sequence_length // LANDMARKS
    radius = KSIZE // 2
    gradient_per_head = grad_ctx.reshape(sequence_length, HEADS, HEAD_DIM)
    grad_soft_query = jnp.einsum(
        "xgs,gzs->gzx", gradient_per_head, small_product, preferred_element_type=jnp.float32
    )
    gradient_small_product = jnp.einsum(
        "ika,aip->ikp", reduced_query_softmax, gradient_per_head, preferred_element_type=jnp.float32
    )
    gradient_pseudo_inverse = jnp.einsum(
        "ulp,uap->ula", gradient_small_product, anchor_summary, precision=HIGH_ACCURACY
    )
    gradient_anchor_summary = jnp.einsum(
        "oxj,oxv->ojv", pseudo_inverse, gradient_small_product, precision=HIGH_ACCURACY
    ).astype(jnp.bfloat16)
    grad_soft_keys = jnp.einsum(
        "kgl,ikl->kgi", gradient_anchor_summary, value_per_head, preferred_element_type=jnp.float32
    )
    grad_values = jnp.einsum(
        "oer,oel->rol",
        reduced_key_softmax,
        gradient_anchor_summary,
        preferred_element_type=jnp.float32,
    ).reshape(sequence_length, MODEL_WIDTH)
    (grad_soft_land,) = pull_newton(gradient_pseudo_inverse)
    (score_query_anchors,) = pull_query(grad_soft_query)
    (score_anchor_pairs,) = pull_land(grad_soft_land)
    (score_key_anchors,) = pull_keys(grad_soft_keys)
    anchor_query32 = query_anchors.astype(jnp.float32)
    anchor_keys32 = key_anchors.astype(jnp.float32)
    gradient_query_heads = jnp.einsum(
        "xov,oxi->vxi", score_query_anchors, anchor_keys32, precision=HIGH_ACCURACY
    )
    grad_key_land = jnp.einsum(
        "qyx,xqi->yqi",
        score_query_anchors,
        query_per_head.astype(jnp.float32),
        precision=HIGH_ACCURACY,
    )
    grad_key_land = grad_key_land + jnp.einsum(
        "tez,etu->ztu", score_anchor_pairs, anchor_query32, precision=HIGH_ACCURACY
    )
    gradient_query_anchors = jnp.einsum(
        "bwo,obv->wbv", score_anchor_pairs, anchor_keys32, precision=HIGH_ACCURACY
    )
    gradient_query_anchors = gradient_query_anchors + jnp.einsum(
        "qyx,xqi->yqi", score_key_anchors, key_per_head.astype(jnp.float32), precision=HIGH_ACCURACY
    )
    gradient_key_heads = jnp.einsum(
        "xov,oxi->vxi", score_key_anchors, anchor_query32, precision=HIGH_ACCURACY
    )
    gradient_query_heads = (
        gradient_query_heads + jnp.repeat(gradient_query_anchors, seg_len, axis=0) / seg_len
    ).reshape(sequence_length, MODEL_WIDTH)
    gradient_key_heads = (
        gradient_key_heads + jnp.repeat(grad_key_land, seg_len, axis=0) / seg_len
    ).reshape(sequence_length, MODEL_WIDTH)
    grad_ctx32 = grad_ctx.astype(jnp.float32)
    grad_padded = jnp.pad(grad_ctx32, ((radius, radius), (0, 0)))
    tap_grads = []
    for offset in range(KSIZE):
        grad_values = (
            grad_values
            + kernel_cols[:, offset]
            * grad_padded[2 * radius - offset : 2 * radius - offset + sequence_length]
        )
        tap_grads.append(
            jnp.sum(
                grad_ctx32 * padded[offset : offset + sequence_length].astype(jnp.float32), axis=0
            )
        )
    grad_kernel = jnp.sum(jnp.stack(tap_grads, axis=1).reshape(HEADS, HEAD_DIM, KSIZE), axis=1)
    grad_mixed = jnp.concatenate(
        [gradient_query_heads, gradient_key_heads, grad_values], axis=1
    ).astype(jnp.bfloat16)
    grad_bias_query = jnp.sum(grad_mixed[:, :MODEL_WIDTH].astype(jnp.float32), axis=0)
    grad_bias_value = jnp.sum(grad_mixed[:, 2 * MODEL_WIDTH :].astype(jnp.float32), axis=0)
    grad_qkv = jnp.einsum("td,te->de", inputs_low, grad_mixed, preferred_element_type=jnp.float32)
    grad_inputs = jnp.einsum("te,de->td", grad_mixed, qkv_full, preferred_element_type=jnp.float32)
    return (grad_inputs, grad_qkv, grad_bias_query, grad_bias_value, grad_kernel)


def layer_forward(inputs, attention_params, feed_params, kernel):
    qkv_full, out_full, bias_full, gain_full = attention_params
    in_full, in_bias, out2_full = feed_params
    bias32 = bias_full.astype(jnp.float32)
    gain32 = gain_full.astype(jnp.float32)
    context, kept = attention_forward(inputs, qkv_full, bias32[0], bias32[1], kernel)
    projected = jnp.dot(context, out_full, preferred_element_type=jnp.float32) + bias32[2]
    normed, pull_first = jax.vjp(layer_norm, projected + inputs, gain32[0], bias32[3])
    normed_low = normed.astype(jnp.bfloat16)
    hidden = jnp.dot(normed_low, in_full, preferred_element_type=jnp.float32) + in_bias.astype(
        jnp.float32
    )
    active, pull_gelu = jax.vjp(gelu_exact, hidden)
    active_low = active.astype(jnp.bfloat16)
    branch = jnp.dot(active_low, out2_full, preferred_element_type=jnp.float32) + bias32[4]
    result, pull_second = jax.vjp(layer_norm, branch + normed, gain32[1], bias32[5])
    return (result, (kept, context, normed_low, active_low, pull_first, pull_gelu, pull_second))


def feed_backward(grad_out, saved, feed_params):
    kept, context, normed_low, active_low, pull_first, pull_gelu, pull_second = saved
    in_full, in_bias, out2_full = feed_params
    grad_sum_two, grad_gain_two, grad_shift_two = pull_second(grad_out)
    grad_branch = grad_sum_two.astype(jnp.bfloat16)
    grad_bias_branch = jnp.sum(grad_branch.astype(jnp.float32), axis=0)
    grad_out2 = jnp.einsum("tf,td->fd", active_low, grad_branch, preferred_element_type=jnp.float32)
    grad_active = jnp.einsum(
        "td,fd->tf", grad_branch, out2_full, preferred_element_type=jnp.float32
    )
    (grad_hidden,) = pull_gelu(grad_active)
    grad_hidden_low = grad_hidden.astype(jnp.bfloat16)
    grad_in_bias = jnp.sum(grad_hidden_low.astype(jnp.float32), axis=0)
    grad_in = jnp.einsum(
        "td,tf->df", normed_low, grad_hidden_low, preferred_element_type=jnp.float32
    )
    grad_normed = grad_sum_two + jnp.einsum(
        "tf,df->td", grad_hidden_low, in_full, preferred_element_type=jnp.float32
    )
    return (
        grad_normed,
        (grad_in, grad_in_bias, grad_out2),
        (grad_gain_two, grad_shift_two, grad_bias_branch),
    )


def attention_part_backward(grad_normed, saved, attention_params, feed_rest):
    kept, context, normed_low, active_low, pull_first, pull_gelu, pull_second = saved
    qkv_full, out_full, bias_full, gain_full = attention_params
    grad_gain_two, grad_shift_two, grad_bias_branch = feed_rest
    grad_pre, grad_gain_one, grad_shift_one = pull_first(grad_normed)
    grad_proj = grad_pre.astype(jnp.bfloat16)
    grad_bias_proj = jnp.sum(grad_proj.astype(jnp.float32), axis=0)
    grad_out = jnp.einsum("td,te->de", context, grad_proj, preferred_element_type=jnp.float32)
    grad_context = jnp.einsum(
        "te,de->td", grad_proj, out_full, preferred_element_type=jnp.float32
    ).astype(jnp.bfloat16)
    grad_inputs, grad_qkv, grad_bias_query, grad_bias_value, grad_kernel = attention_backward(
        grad_context, kept, qkv_full
    )
    grad_biases = jnp.stack(
        [
            grad_bias_query,
            grad_bias_value,
            grad_bias_proj,
            grad_shift_one,
            grad_bias_branch,
            grad_shift_two,
        ]
    )
    grad_gains = jnp.stack([grad_gain_one, grad_gain_two])
    return (grad_pre + grad_inputs, (grad_qkv, grad_out, grad_biases, grad_gains), grad_kernel)


def stack_layers(store, position):
    return jnp.stack([entry[position] for entry in store])


def body(tokens, cotangent, qkv_w, out_w, in_w, in_b, out2_w, bias_rows, gain_rows, conv_w):
    layers = qkv_w.shape[0]
    kernels = conv_w.astype(jnp.float32)
    current = tokens.astype(jnp.float32)
    fetched = []
    saved_all = []
    for layer_id in range(layers):
        attention_params = (
            lax.all_gather(qkv_w[layer_id], ("wide", "narrow"), axis=0, tiled=True),
            lax.all_gather(out_w[layer_id], ("wide", "narrow"), axis=0, tiled=True),
            lax.all_gather(bias_rows[layer_id], ("wide", "narrow"), axis=1, tiled=True),
            lax.all_gather(gain_rows[layer_id], ("wide", "narrow"), axis=1, tiled=True),
        )
        feed_params = (
            lax.all_gather(in_w[layer_id], ("wide", "narrow"), axis=0, tiled=True),
            lax.all_gather(in_b[layer_id], ("wide", "narrow"), axis=0, tiled=True),
            lax.all_gather(out2_w[layer_id], ("wide", "narrow"), axis=0, tiled=True),
        )
        current, saved = layer_forward(current, attention_params, feed_params, kernels[layer_id])
        fetched.append((attention_params, feed_params))
        saved_all.append(saved)
    output = current.astype(jnp.bfloat16)
    grad_current = cotangent.astype(jnp.float32)
    feed_store = [None] * layers
    attention_store = [None] * layers
    kernel_store = [None] * layers
    for layer_id in reversed(range(layers)):
        attention_params = (
            lax.all_gather(qkv_w[layer_id], ("wide", "narrow"), axis=0, tiled=True),
            lax.all_gather(out_w[layer_id], ("wide", "narrow"), axis=0, tiled=True),
            lax.all_gather(bias_rows[layer_id], ("wide", "narrow"), axis=1, tiled=True),
            lax.all_gather(gain_rows[layer_id], ("wide", "narrow"), axis=1, tiled=True),
        )
        feed_params = (
            lax.all_gather(in_w[layer_id], ("wide", "narrow"), axis=0, tiled=True),
            lax.all_gather(in_b[layer_id], ("wide", "narrow"), axis=0, tiled=True),
            lax.all_gather(out2_w[layer_id], ("wide", "narrow"), axis=0, tiled=True),
        )
        grad_normed, feed_grads, feed_rest = feed_backward(
            grad_current, saved_all[layer_id], feed_params
        )
        feed_store[layer_id] = (
            lax.psum_scatter(feed_grads[0], ("wide", "narrow"), scatter_dimension=0, tiled=True),
            lax.psum_scatter(feed_grads[1], ("wide", "narrow"), scatter_dimension=0, tiled=True),
            lax.psum_scatter(feed_grads[2], ("wide", "narrow"), scatter_dimension=0, tiled=True),
        )
        grad_current, attention_grads, grad_kernel = attention_part_backward(
            grad_normed, saved_all[layer_id], attention_params, feed_rest
        )
        kernel_store[layer_id] = grad_kernel
        attention_store[layer_id] = (
            lax.psum_scatter(
                attention_grads[0], ("wide", "narrow"), scatter_dimension=0, tiled=True
            ),
            lax.psum_scatter(
                attention_grads[1], ("wide", "narrow"), scatter_dimension=0, tiled=True
            ),
            lax.psum_scatter(
                attention_grads[2], ("wide", "narrow"), scatter_dimension=1, tiled=True
            ),
            lax.psum_scatter(
                attention_grads[3], ("wide", "narrow"), scatter_dimension=1, tiled=True
            ),
        )
    grad_qkv_w = stack_layers(attention_store, 0)
    grad_out_w = stack_layers(attention_store, 1)
    grad_bias_rows = stack_layers(attention_store, 2)
    grad_gain_rows = stack_layers(attention_store, 3)
    grad_in_w = stack_layers(feed_store, 0)
    grad_in_b = stack_layers(feed_store, 1)
    grad_out2_w = stack_layers(feed_store, 2)
    grad_conv_w = lax.psum(jnp.stack(kernel_store), ("wide", "narrow"))
    return (
        output,
        grad_current,
        grad_qkv_w,
        grad_out_w,
        grad_in_w,
        grad_in_b,
        grad_out2_w,
        grad_bias_rows,
        grad_gain_rows,
        grad_conv_w,
    )


def solution(mesh):
    placed = (
        P(("wide", "narrow"), None),
        P(("wide", "narrow"), None),
        P(None, ("wide", "narrow"), None),
        P(None, ("wide", "narrow"), None),
        P(None, ("wide", "narrow"), None),
        P(None, ("wide", "narrow")),
        P(None, ("wide", "narrow"), None),
        P(None, None, ("wide", "narrow")),
        P(None, None, ("wide", "narrow")),
        P(),
    )
    return jax.shard_map(
        body,
        mesh=mesh,
        in_specs=placed,
        out_specs=(
            P(("wide", "narrow"), None),
            P(("wide", "narrow"), None),
            P(None, ("wide", "narrow"), None),
            P(None, ("wide", "narrow"), None),
            P(None, ("wide", "narrow"), None),
            P(None, ("wide", "narrow")),
            P(None, ("wide", "narrow"), None),
            P(None, None, ("wide", "narrow")),
            P(None, None, ("wide", "narrow")),
            P(),
        ),
        check_vma=False,
    )
```

profile of v0, /device:TPU:0, one launch (start us, length us, event | category | flops | bytes accessed | tf_op | source)
XLA Modules:
  0.0 2350.6 jit_solution(7863526201652623325)
XLA Ops:
  21.2 73.7 %all-gather.1 = bf16[1,6,768]{1,0,2:T(2,128)(2,1)S(1)} all-gather(bf16[1,6,24]{1,0,2:T(2,128)(2,1)S(1)} %copy.776), channel_id=3, replica_groups=mesh['wide'=8,'narrow'=4] {'wide','narrow'}, dimensions={2}, use_global_device_ids=true | all-gather | bytes 9504 | tf_op jit(solution)/shard_map/all_gather | solution.py:317
  95.2 13.3 slice_reduce_fusion.8
  110.4 68.2 %all-gather.3 = bf16[1,2,768]{1,0,2:T(2,128)(2,1)S(1)} all-gather(bf16[1,2,24]{1,0,2:T(2,128)(2,1)S(1)} %copy.777), channel_id=5, replica_groups=mesh['wide'=8,'narrow'=4] {'wide','narrow'}, dimensions={2}, use_global_device_ids=true | all-gather | bytes 3168 | tf_op jit(solution)/shard_map/all_gather | solution.py:318
  178.9 5.1 slice_reduce_fusion.9
  184.5 39.8 %all-reduce.13 = (bf16[3072]{0:T(1024)(128)(2,1)S(1)}, bf16[3072]{0:T(1024)(128)(2,1)S(1)}) all-reduce(bf16[3072]{0:T(1024)(128)(2,1)S(1)} %dynamic-update-slice, bf16[3072]{0:T(1024)(128)(2,1)S(1)} %dynamic-update-slice.1), channel_id=7, replica_groups=mesh['wide'=8,'narrow'=4] {'wide','narrow'}, use_global_device_ids=true, to_apply=%add.4 | all-reduce | flops 6144 | bytes 24576
  225.0 70.2 %all-gather.8 = bf16[1,6,768]{1,0,2:T(2,128)(2,1)S(1)} all-gather(bf16[1,6,24]{1,0,2:T(2,128)(2,1)S(1)} %copy.778), channel_id=10, replica_groups=mesh['wide'=8,'narrow'=4] {'wide','narrow'}, dimensions={2}, use_global_device_ids=true | all-gather | bytes 9504 | tf_op jit(solution)/shard_map/all_gather | solution.py:317
  295.6 13.2 slice_reduce_fusion
  309.0 68.4 %all-gather.10 = bf16[1,2,768]{1,0,2:T(2,128)(2,1)S(1)} all-gather(bf16[1,2,24]{1,0,2:T(2,128)(2,1)S(1)} %copy.779), channel_id=12, replica_groups=mesh['wide'=8,'narrow'=4] {'wide','narrow'}, dimensions={2}, use_global_device_ids=true | all-gather | bytes 3168 | tf_op jit(solution)/shard_map/all_gather | solution.py:318
  377.7 5.1 slice_reduce_fusion.1
  385.1 6.3 fusion.38
  395.2 4.5 reshape.585
  404.7 4.4 reshape.584
  410.9 4.5 reduce_sum.1194
  415.4 4.6 reduce_sum.1195
  447.7 4.2 fusion.455
  463.5 16.2 fusion.74
  485.3 37.7 %multiply_convert_fusion.1 = (bf16[1024,3072]{1,0:T(8,128)(2,1)}, f32[1024,3072]{1,0:T(8,128)}, f32[1024,3072]{1,0:T(8,128)}) fusion(f32[3072]{0:T(1024)} %convert_element_type.609, bf16[1,768,3072]{2,1,0:T(8,128)(2,1)} %all-gather.27.cloned.1.call-done, f32[1024,768]{0,1:T(8,128)} %copy-done.49, f32[768]{0:T(1024)} %get-tuple-element.162, ...), kind=kOutput, calls=%fused_computation.93 | convolution fusion | flops 5043388416 | bytes 39348224 | tf_op jit(solution)/shard_map/dot_general | solution.py:239
  523.1 9.9 fusion.457
  535.1 7.2 fusion.34
  548.0 6.2 reshape.586
  554.1 4.4 reshape.587
  560.1 4.5 reduce_sum.1205
  565.5 5.3 reduce_sum.1204
  572.2 4.5 fusion.460
  613.4 15.3 fusion.108
  628.7 4.6 fusion.461
  634.1 38.0 %multiply_convert_fusion = (bf16[1024,3072]{1,0:T(8,128)(2,1)}, f32[1024,3072]{1,0:T(8,128)}, f32[1024,3072]{1,0:T(8,128)}) fusion(f32[3072]{0:T(1024)S(1)} %copy-done.330, bf16[1,768,3072]{2,1,0:T(8,128)(2,1)} %all-gather.35.cloned.1.call-done, f32[1024,768]{0,1:T(8,128)S(1)} %get-tuple-element.304, f32[768]{0:T(1024)S(1)} %copy-done.333, ...), kind=kOutput, calls=%fused_computation.80 | convolution fusion | flops 5043388416 | bytes 39348224 | tf_op jit(solution)/shard_map/dot_general | solution.py:239
  672.2 9.7 fusion.462
  688.2 18.1 convert_reduce_fusion
  706.4 11.4 multiply_reduce_fusion
  780.0 6.3 copy.636
  805.3 6.3 copy.641
  811.6 7.4 fusion.216
  825.4 53.4 %convert_reduce_fusion.5 = (f32[768]{0:T(1024)}, bf16[1024,768]{1,0:T(8,128)(2,1)S(1)}) fusion(f32[768]{0:T(1024)S(1)} %copy-done.240, f32[768]{0:T(1024)S(1)} %copy-done.242, f32[768]{0:T(1024)S(1)} %copy-done.244, f32[768]{0:T(1024)S(1)} %copy-done.246, f32[768]{0:T(1024)S(1)} %copy-done.248, f32[768]{0:T(1024)S(1)} %copy-done.250, ...), kind=kLoop, calls=%fused_computation.401 | loop fusion | flops 55049472 | bytes 9541632 | tf_op jit(solution)/shard_map/reduce_sum | solution.py:224
  878.9 7.9 multiply_reduce_fusion.1
  889.5 17.8 convert_reduce_fusion.1
  907.3 10.8 multiply_reduce_fusion.2
  924.9 4.3 fusion.209
  929.2 4.4 fusion.208
  940.1 4.4 fusion.159
  944.5 4.6 fusion.158
  949.0 4.6 fusion.157
  1124.6 6.3 copy.672
  1142.5 52.3 %convert_reduce_fusion.9 = (f32[768]{0:T(1024)S(1)}, bf16[1024,768]{1,0:T(8,128)(2,1)}) fusion(f32[768]{0:T(1024)S(1)} %copy-done.236, f32[768]{0:T(1024)} %get-tuple-element.201, f32[768]{0:T(1024)} %get-tuple-element.202, f32[768]{0:T(1024)} %get-tuple-element.203, f32[768]{0:T(1024)} %get-tuple-element.204, f32[768]{0:T(1024)} %get-tuple-element.205, ...), kind=kLoop, calls=%fused_computation.405 | loop fusion | flops 55049472 | bytes 9541632 | tf_op jit(solution)/shard_map/reduce_sum | solution.py:224
  1198.3 4.4 fusion.500
  1210.3 4.7 fusion.390
  1218.9 6.3 copy.677
  1225.3 6.4 fusion.214
  1234.4 8.7 convolution_bitcast_fusion
  1243.1 8.1 copy.764
  1253.1 9.3 fusion.235
  1263.8 10.1 fusion.502
  1275.4 10.2 fusion.501
  1287.4 10.6 fusion.396
  1300.0 10.6 fusion.391
  1312.4 9.0 add_add_fusion.7
  1334.2 91.9 %reduce-scatter.19.cloned.1.call-done = f32[24,768]{1,0:T(8,128)} async-done(((f32[768,768]{1,0:T(8,128)}), f32[24,768]{1,0:T(8,128)}) %reduce-scatter.19.cloned.1.call-update) | async-done | bytes 73744 | tf_op jit(solution)/shard_map/reduce_scatter | solution.py:361
  1426.1 103.3 %reduce-scatter.17.cloned.1.call-done = f32[24,768]{1,0:T(8,128)} async-done(((f32[768,768]{1,0:T(8,128)}), f32[24,768]{1,0:T(8,128)}) %reduce-scatter.17.cloned.1.call-update) | async-done | bytes 73744 | tf_op jit(solution)/shard_map/reduce_scatter | solution.py:361
  1531.0 123.2 %reduce-scatter.29.cloned.1.call-done = f32[24,2304]{1,0:T(8,128)} async-done(((f32[768,2304]{1,0:T(8,128)}), f32[24,2304]{1,0:T(8,128)}) %reduce-scatter.29.cloned.1.call-update) | async-done | bytes 221200
  1655.8 122.5 %reduce-scatter.31.cloned.1.call-done = f32[24,2304]{1,0:T(8,128)} async-done(((f32[768,2304]{1,0:T(8,128)}), f32[24,2304]{1,0:T(8,128)}) %reduce-scatter.31.cloned.1.call-update) | async-done | bytes 221200
  1780.8 139.1 %reduce-scatter.27.cloned.1.call-done = f32[96,768]{1,0:T(8,128)} async-done(((f32[3072,768]{1,0:T(8,128)}), f32[96,768]{1,0:T(8,128)}) %reduce-scatter.27.cloned.1.call-update) | async-done | bytes 294928 | tf_op jit(solution)/shard_map/reduce_scatter | solution.py:351
  1920.0 140.3 %reduce-scatter.25.cloned.1.call-done = f32[96,768]{1,0:T(8,128)} async-done(((f32[3072,768]{1,0:T(8,128)}), f32[96,768]{1,0:T(8,128)}) %reduce-scatter.25.cloned.1.call-update) | async-done | bytes 294928 | tf_op jit(solution)/shard_map/reduce_scatter | solution.py:351
  2062.1 139.5 %reduce-scatter.21.cloned.1.call-done = f32[24,3072]{1,0:T(8,128)} async-done(((f32[768,3072]{1,0:T(8,128)}), f32[24,3072]{1,0:T(8,128)}) %reduce-scatter.21.cloned.1.call-update) | async-done | bytes 294928 | tf_op jit(solution)/shard_map/reduce_scatter | solution.py:349
  2201.6 140.4 %reduce-scatter.23.cloned.1.call-done = f32[24,3072]{1,0:T(8,128)} async-done(((f32[768,3072]{1,0:T(8,128)}), f32[24,3072]{1,0:T(8,128)}) %reduce-scatter.23.cloned.1.call-update) | async-done | bytes 294928 | tf_op jit(solution)/shard_map/reduce_scatter | solution.py:349
  (1242 shorter events, 462.7 us)
Async XLA Ops:
  7.2 377.9 %all-gather.23.cloned.1.call-start = ((), (), s32[]{:S(2)}) async-start(), calls=%async_computation.14 | async-start | bytes 3649536 | tf_op jit(solution)/shard_map/all_gather | solution.py:315
  8.9 470.8 %all-gather.25.cloned.1.call-start = ((), (), s32[]{:S(2)}) async-start(), calls=%async_computation.15 | async-start | bytes 1216512 | tf_op jit(solution)/shard_map/all_gather | solution.py:316
  10.4 474.9 %all-gather.27.cloned.1.call-start = ((), (), s32[]{:S(2)}) async-start(), calls=%async_computation.16 | async-start | bytes 4866048 | tf_op jit(solution)/shard_map/all_gather | solution.py:321
  12.2 510.9 %all-gather.29.cloned.1.call-start = ((), (), s32[]{:S(2)}) async-start(), calls=%async_computation.17 | async-start | bytes 4866048 | tf_op jit(solution)/shard_map/all_gather | solution.py:323
  13.9 94.6 %copy-start.171 = (bf16[1024,768]{1,0:T(8,128)(2,1)S(1)}, bf16[1024,768]{1,0:T(8,128)(2,1)}, u32[]{:S(2)}) copy-start(bf16[1024,768]{1,0:T(8,128)(2,1)} %param.10) | copy-start | bytes 4718596
  14.0 521.1 %all-gather.31.cloned.1.call-start = ((), (), s32[]{:S(2)}) async-start(), calls=%async_computation.18 | async-start | bytes 3649536 | tf_op jit(solution)/shard_map/all_gather | solution.py:315
  14.6 614.1 %all-gather.33.cloned.1.call-start = ((), (), s32[]{:S(2)}) async-start(), calls=%async_computation.19 | async-start | bytes 1216512 | tf_op jit(solution)/shard_map/all_gather | solution.py:316
  15.1 618.7 %all-gather.35.cloned.1.call-start = ((), (), s32[]{:S(2)}) async-start(), calls=%async_computation.20 | async-start | bytes 4866048 | tf_op jit(solution)/shard_map/all_gather | solution.py:321
  15.9 656.3 %all-gather.37.cloned.1.call-start = ((), (), s32[]{:S(2)}) async-start(), calls=%async_computation.21 | async-start | bytes 4866048 | tf_op jit(solution)/shard_map/all_gather | solution.py:323
  16.6 1310.0 %all-reduce.16.cloned.1.call-start = ((), (), s32[]{:S(2)}) async-start(), calls=%async_computation.24 | async-start | bytes 204800
  16.7 585.0 %copy-start.9 = (f32[64,64]{1,0:T(8,128)}, f32[64,64]{1,0:T(8,128)S(1)}, u32[]{:S(2)}) copy-start(f32[64,64]{1,0:T(8,128)S(1)} %get-tuple-element.337) | copy-start | bytes 49156
  18.5 444.9 %copy-start.233 = (f32[768]{0:T(1024)}, f32[768]{0:T(1024)S(1)}, u32[]{:S(2)}) copy-start(f32[768]{0:T(1024)S(1)} %get-tuple-element.199) | copy-start | bytes 9220
  18.5 445.0 %copy-start.235 = (f32[768]{0:T(1024)}, f32[768]{0:T(1024)S(1)}, u32[]{:S(2)}) copy-start(f32[768]{0:T(1024)S(1)} %get-tuple-element.200) | copy-start | bytes 9220
  108.6 75.5 %copy-start.343 = (bf16[2,96]{1,0:T(2,128)(2,1)S(1)}, bf16[2,96]{1,0:T(2,128)(2,1)}, u32[]{:S(2)}) copy-start(bf16[2,96]{1,0:T(2,128)(2,1)} %param.15) | copy-start | bytes 1156
  178.9 204.5 %copy-start.170 = (bf16[1024,768]{1,0:T(8,128)(2,1)S(1)}, bf16[1024,768]{1,0:T(8,128)(2,1)}, u32[]{:S(2)}) copy-start(bf16[1024,768]{1,0:T(8,128)(2,1)} %param.11) | copy-start | bytes 4718596
  404.6 58.8 %copy-start = (bf16[1024,768]{1,0:T(8,128)(2,1)}, bf16[1024,768]{1,0:T(8,128)(2,1)S(1)}, u32[]{:S(2)}) copy-start(bf16[1024,768]{1,0:T(8,128)(2,1)S(1)} %get-tuple-element.265) | copy-start | bytes 4718596
  420.3 20.0 copy-start.164
  483.2 39.9 %copy-start.223 = (f32[1024]{0:T(1024)}, f32[1024]{0:T(1024)S(1)}, u32[]{:S(2)}) copy-start(f32[1024]{0:T(1024)S(1)} %broadcast_multiply_fusion.3) | copy-start | bytes 12292
  485.2 37.8 %copy-start.229 = (f32[1024]{0:T(1024)}, f32[1024]{0:T(1024)S(1)}, u32[]{:S(2)}) copy-start(f32[1024]{0:T(1024)S(1)} %multiply_reduce_fusion.13) | copy-start | bytes 12292
  485.3 37.8 %copy-start.318 = (f32[1024]{0:T(1024)}, f32[1024]{0:T(1024)S(1)}, u32[]{:S(2)}) copy-start(f32[1024]{0:T(1024)S(1)} %fusion.371) | copy-start | bytes 12292
  533.0 95.7 %copy-start.225 = (f32[1024]{0:T(1024)}, f32[1024]{0:T(1024)S(1)}, u32[]{:S(2)}) copy-start(f32[1024]{0:T(1024)S(1)} %broadcast_multiply_fusion.2) | copy-start | bytes 12292
  535.0 93.7 %copy-start.321 = (f32[1024]{0:T(1024)}, f32[1024]{0:T(1024)S(1)}, u32[]{:S(2)}) copy-start(f32[1024]{0:T(1024)S(1)} %fusion.372) | copy-start | bytes 12292
  544.8 68.2 %copy-start.2 = (bf16[1024,768]{1,0:T(8,128)(2,1)}, bf16[1024,768]{1,0:T(8,128)(2,1)S(1)}, u32[]{:S(2)}) copy-start(bf16[1024,768]{1,0:T(8,128)(2,1)S(1)} %get-tuple-element.263) | copy-start | bytes 4718596
  576.7 26.9 %copy-start.208 = (f32[12,1024]{1,0:T(8,128)}, f32[12,1024]{1,0:T(8,128)S(1)}, u32[]{:S(2)}) copy-start(f32[12,1024]{1,0:T(8,128)S(1)} %get-tuple-element.301) | copy-start | bytes 147460
  578.6 22.1 copy-start.216
  581.3 22.8 copy-start.212
  582.3 23.2 copy-start.22
  633.3 38.8 %copy-start.57 = (f32[1024,768]{0,1:T(8,128)}, f32[1024,768]{0,1:T(8,128)S(1)}, u32[]{:S(2)}) copy-start(f32[1024,768]{0,1:T(8,128)S(1)} %get-tuple-element.304) | copy-start | bytes 9437188
  633.4 84.4 %copy-start.227 = (f32[1024]{0:T(1024)}, f32[1024]{0:T(1024)S(1)}, u32[]{:S(2)}) copy-start(f32[1024]{0:T(1024)S(1)} %broadcast_multiply_fusion.1) | copy-start | bytes 12292
  633.8 84.0 %copy-start.324 = (f32[1024]{0:T(1024)}, f32[1024]{0:T(1024)S(1)}, u32[]{:S(2)}) copy-start(f32[1024]{0:T(1024)S(1)} %fusion.373) | copy-start | bytes 12292
  634.1 38.0 %copy-start.337 = (f32[768]{0:T(1024)S(1)}, f32[768]{0:T(1024)}, u32[]{:S(2)}) copy-start(f32[768]{0:T(1024)} %get-tuple-element.153) | copy-start | bytes 9220
  688.2 18.1 copy-start.179
  820.7 58.1 %copy-start.174 = (bf16[1024,768]{1,0:T(8,128)(2,1)}, bf16[1024,768]{1,0:T(8,128)(2,1)S(1)}, u32[]{:S(2)}) copy-start(bf16[1024,768]{1,0:T(8,128)(2,1)S(1)} %copy.645) | copy-start | bytes 4718596
  825.3 53.5 %copy-start.53 = (f32[1024,768]{0,1:T(8,128)S(1)}, f32[1024,768]{0,1:T(8,128)}, u32[]{:S(2)}) copy-start(f32[1024,768]{0,1:T(8,128)} %copy-done.52) | copy-start | bytes 9437188
  825.4 53.4 %copy-start.65 = (f32[1024,768]{0,1:T(8,128)S(1)}, f32[1024,768]{0,1:T(8,128)}, u32[]{:S(2)}) copy-start(f32[1024,768]{0,1:T(8,128)} %copy-done.64) | copy-start | bytes 9437188
  825.4 53.4 %copy-start.173 = (bf16[1024,768]{1,0:T(8,128)(2,1)S(1)}, bf16[1024,768]{1,0:T(8,128)(2,1)}, u32[]{:S(2)}) copy-start(bf16[1024,768]{1,0:T(8,128)(2,1)} %copy.644) | copy-start | bytes 4718596
  825.4 53.4 %copy-start.226 = (f32[1024]{0:T(1024)S(1)}, f32[1024]{0:T(1024)}, u32[]{:S(2)}) copy-start(f32[1024]{0:T(1024)} %copy-done.225) | copy-start | bytes 12292
  825.4 53.4 %copy-start.307 = (f32[768]{0:T(1024)S(1)}, f32[768]{0:T(1024)}, u32[]{:S(2)}) copy-start(f32[768]{0:T(1024)} %get-tuple-element.158) | copy-start | bytes 9220
  825.4 53.4 %copy-start.322 = (f32[1024]{0:T(1024)S(1)}, f32[1024]{0:T(1024)}, u32[]{:S(2)}) copy-start(f32[1024]{0:T(1024)} %copy-done.321) | copy-start | bytes 12292
  888.9 18.4 copy-start.183
  889.4 17.8 copy-start.224
  889.5 17.8 copy-start.319
  995.1 109.1 %copy-start.82 = (f32[12,64,64]{2,1,0:T(8,128)S(1)}, f32[12,64,64]{2,1,0:T(8,128)}, u32[]{:S(2)}) copy-start(f32[12,64,64]{2,1,0:T(8,128)} %copy-done.80) | copy-start | bytes 589828
  1142.4 52.4 %copy-start.316 = (f32[768]{0:T(1024)S(1)}, f32[768]{0:T(1024)}, u32[]{:S(2)}) copy-start(f32[768]{0:T(1024)} %get-tuple-element.243) | copy-start | bytes 9220
  1142.4 52.4 %copy-start.342 = (f32[768]{0:T(1024)S(1)}, f32[768]{0:T(1024)}, u32[]{:S(2)}) copy-start(f32[768]{0:T(1024)} %get-tuple-element.146) | copy-start | bytes 9220
  1142.4 52.5 %copy-start.315 = (f32[768]{0:T(1024)S(1)}, f32[768]{0:T(1024)}, u32[]{:S(2)}) copy-start(f32[768]{0:T(1024)} %get-tuple-element.241) | copy-start | bytes 9220
  1142.4 52.5 %copy-start.341 = (f32[768]{0:T(1024)S(1)}, f32[768]{0:T(1024)}, u32[]{:S(2)}) copy-start(f32[768]{0:T(1024)} %get-tuple-element.147) | copy-start | bytes 9220
  1142.4 52.5 %copy-start.317 = (f32[768]{0:T(1024)S(1)}, f32[768]{0:T(1024)}, u32[]{:S(2)}) copy-start(f32[768]{0:T(1024)} %convert_reduce_fusion.6) | copy-start | bytes 9220
  1142.4 52.5 %copy-start.314 = (f32[768]{0:T(1024)S(1)}, f32[768]{0:T(1024)}, u32[]{:S(2)}) copy-start(f32[768]{0:T(1024)} %get-tuple-element.251) | copy-start | bytes 9220
  1142.5 52.5 %copy-start.313 = (f32[768]{0:T(1024)S(1)}, f32[768]{0:T(1024)}, u32[]{:S(2)}) copy-start(f32[768]{0:T(1024)} %get-tuple-element.249) | copy-start | bytes 9220
  1142.5 52.5 %copy-start.340 = (f32[768]{0:T(1024)S(1)}, f32[768]{0:T(1024)}, u32[]{:S(2)}) copy-start(f32[768]{0:T(1024)} %get-tuple-element.148) | copy-start | bytes 9220
  1142.5 52.5 %copy-start.312 = (f32[768]{0:T(1024)S(1)}, f32[768]{0:T(1024)}, u32[]{:S(2)}) copy-start(f32[768]{0:T(1024)} %get-tuple-element.247) | copy-start | bytes 9220
  1142.5 52.5 %copy-start.329 = (f32[768]{0:T(1024)S(1)}, f32[768]{0:T(1024)}, u32[]{:S(2)}) copy-start(f32[768]{0:T(1024)} %get-tuple-element.149) | copy-start | bytes 9220
  1142.5 52.5 %copy-start.339 = (f32[768]{0:T(1024)S(1)}, f32[768]{0:T(1024)}, u32[]{:S(2)}) copy-start(f32[768]{0:T(1024)} %get-tuple-element.74) | copy-start | bytes 9220
  1142.5 52.6 %copy-start.328 = (f32[768]{0:T(1024)S(1)}, f32[768]{0:T(1024)}, u32[]{:S(2)}) copy-start(f32[768]{0:T(1024)} %get-tuple-element.76) | copy-start | bytes 9220
  1142.5 55.8 %copy-start.181 = (bf16[1024,768]{1,0:T(8,128)(2,1)S(1)}, bf16[1024,768]{1,0:T(8,128)(2,1)}, u32[]{:S(2)}) copy-start(bf16[1024,768]{1,0:T(8,128)(2,1)} %fusion.108) | copy-start | bytes 4718596
  1198.2 227.9 %reduce-scatter.19.cloned.1.call-start = ((), (), s32[]{:S(2)}) async-start(), calls=%async_computation.9 | async-start | bytes 2433024 | tf_op jit(solution)/shard_map/reduce_scatter | solution.py:361
  1202.7 326.7 %reduce-scatter.17.cloned.1.call-start = ((), (), s32[]{:S(2)}) async-start(), calls=%async_computation.8 | async-start | bytes 2433024 | tf_op jit(solution)/shard_map/reduce_scatter | solution.py:361
  1207.0 447.2 %reduce-scatter.29.cloned.1.call-start = ((), (), s32[]{:S(2)}) async-start(), calls=%async_computation.22 | async-start | bytes 7299072
  1251.2 527.1 %reduce-scatter.31.cloned.1.call-start = ((), (), s32[]{:S(2)}) async-start(), calls=%async_computation.23 | async-start | bytes 7299072
  1262.4 657.5 %reduce-scatter.27.cloned.1.call-start = ((), (), s32[]{:S(2)}) async-start(), calls=%async_computation.13 | async-start | bytes 9732096 | tf_op jit(solution)/shard_map/reduce_scatter | solution.py:351
  1274.0 786.2 %reduce-scatter.25.cloned.1.call-start = ((), (), s32[]{:S(2)}) async-start(), calls=%async_computation.12 | async-start | bytes 9732096 | tf_op jit(solution)/shard_map/reduce_scatter | solution.py:351
  1285.6 916.0 %reduce-scatter.21.cloned.1.call-start = ((), (), s32[]{:S(2)}) async-start(), calls=%async_computation.10 | async-start | bytes 9732096 | tf_op jit(solution)/shard_map/reduce_scatter | solution.py:349
  1298.1 1043.9 %reduce-scatter.23.cloned.1.call-start = ((), (), s32[]{:S(2)}) async-start(), calls=%async_computation.11 | async-start | bytes 9732096 | tf_op jit(solution)/shard_map/reduce_scatter | solution.py:349
  (312 other events, 1235.7 us)
Sparse Core Ops, SparseCore 0:
  11.4 63.4 all-gather.22
  77.7 52.9 all-gather.24
  134.1 62.9 all-gather.26
  200.3 63.5 all-gather.28
  266.5 59.7 all-gather.30
  329.0 53.0 all-gather.32
  385.4 62.4 all-gather.34
  450.7 62.3 all-gather.36
  1198.3 121.6 all-reduce.15
  1326.0 100.0 reduce-scatter.18
  1431.4 97.9 reduce-scatter.16
  1535.9 118.2 reduce-scatter.28
  1659.9 118.4 reduce-scatter.30
  1785.1 134.8 reduce-scatter.26
  1925.7 134.4 reduce-scatter.24
  2067.0 134.5 reduce-scatter.20
  2207.3 134.5 reduce-scatter.22
where the time goes:
time: 2360 us; the launch traced here: 2350 us
  waiting for transfers between devices  1000 us (42%)
  matrix products  455 us (19%)
  blocking collectives  320 us (14%)
  local copies, waits for them, and re-layouts  316 us (13%)
  other arithmetic  236 us (10%)
    reduce_scatter x2, waiting for transfers between devices, body(): lax.psum_scatter(feed_grads[0], ('wide', 'narrow'), scatter_dimension=0,...  280 us
    reduce_scatter x2, waiting for transfers between devices, body(): lax.psum_scatter(feed_grads[2], ('wide', 'narrow'), scatter_dimension=0,...  279 us
    unnamed x20, waiting for transfers between devices  248 us
    reduce_scatter x2, waiting for transfers between devices, body(): lax.psum_scatter(attention_grads[1], ('wide', 'narrow'), scatter_dimensio...  195 us
    all_gather x2, blocking collectives, body(): lax.all_gather(bias_rows[layer_id], ('wide', 'narrow'), axis=1, tiled=True)  144 us
    all_gather x2, blocking collectives, body(): lax.all_gather(gain_rows[layer_id], ('wide', 'narrow'), axis=1, tiled=True)  137 us
    unnamed x800, local copies, waits for them, and re-layouts  116 us
    reduce_sum x2, other arithmetic, attention_backward(): jnp.sum(grad_mixed[:, 2 * MODEL_WIDTH:].astype(jnp.float32), axis=0)  106 us
  transfers between devices with their start and end apart: 17, of which 8 were waited for; matrix products, arithmetic and copies ran while one was open for 19% of the time, Pallas kernels for 0%

commit v1 on v0

v1 whole, which is shorter than its diff:
```python
import functools
import jax
import jax.numpy as jnp
import numpy as np
from jax import lax
from jax.experimental import pallas as pl
from jax.experimental.pallas import tpu as pltpu
from jax.sharding import PartitionSpec as P

D = 768
HEADS = 12
HD = 64
FF = 3072
LM = 64
KSIZE = 33
RADIUS = KSIZE // 2
NS_ITERS = 6
T = 1024
SEG = T // LM
SCALE = HD ** -0.5
EPS = 1e-05
CONV_N = 256
CONV_K = 512
CONV_BLOCKS = T // CONV_N
LEAD = 128
f32 = jnp.float32
bf16 = jnp.bfloat16
AXES = ("wide", "narrow")
NN = (((1,), (0,)), ((), ()))
NT = (((1,), (1,)), ((), ()))
TN = (((0,), (0,)), ((), ()))
VMEM_LIMIT = 60 * 1024 * 1024


def dot(a, b, dims):
    return lax.dot_general(a, b, dims, preferred_element_type=f32)


def split(a):
    high = a.astype(bf16)
    return high, (a - high.astype(f32)).astype(bf16)


def dot3(a, b, dims):
    return dot(a[0], b[0], dims) + (dot(a[0], b[1], dims) + dot(a[1], b[0], dims))


def rows(start, size):
    if isinstance(start, int):
        return pl.ds(start, size)
    return pl.ds(pl.multiple_of(start, size), size)


def segment_mean():
    token = lax.broadcasted_iota(jnp.int32, (T, LM), 0)
    seg = lax.broadcasted_iota(jnp.int32, (T, LM), 1)
    return jnp.where(token // SEG == seg, 1.0 / SEG, 0.0).astype(bf16)


def segment_spread():
    token = lax.broadcasted_iota(jnp.int32, (LM, T), 1)
    seg = lax.broadcasted_iota(jnp.int32, (LM, T), 0)
    return jnp.where(token // SEG == seg, 1.0, 0.0).astype(bf16)


def eye(value):
    i = lax.broadcasted_iota(jnp.int32, (LM, LM), 0)
    j = lax.broadcasted_iota(jnp.int32, (LM, LM), 1)
    return jnp.where(i == j, value, 0.0).astype(f32)


def toeplitz(row):
    full = jnp.broadcast_to(row, (CONV_N, CONV_K))
    return pltpu.roll(full, 0, 1, stride=1, stride_axis=0).astype(bf16)


def windows(ref, base):
    return jnp.concatenate(
        [ref[rows(base, HD), CONV_N * b : CONV_N * b + CONV_K] for b in range(CONV_BLOCKS)], axis=0
    )


def stack_blocks(value):
    return jnp.concatenate(
        [value[:, CONV_N * b : CONV_N * (b + 1)] for b in range(CONV_BLOCKS)], axis=0
    )


def unstack_blocks(value):
    return jnp.concatenate(
        [value[HD * b : HD * (b + 1), :] for b in range(CONV_BLOCKS)], axis=1
    )


def norm_forward(r_ref, xhat_ref, rstd_ref, width=128):
    for c in range(0, T, width):
        r = r_ref[:, c : c + width]
        center = r - jnp.mean(r, axis=0, keepdims=True)
        rstd = lax.rsqrt(jnp.mean(center * center, axis=0, keepdims=True) + EPS)
        xhat_ref[:, c : c + width] = center * rstd
        rstd_ref[:, c : c + width] = jnp.broadcast_to(rstd, (8, width))


def attention_forward_kernel(
    n_pieces, p, starts_ref, x_ref, par_ref, conv_ref, *rest
):
    pieces = rest[:n_pieces]
    (xl_ref, mix_ref, ctx_ref, f_ref, b_ref, lm_ref, a_ref, ns_ref, small_ref, xhat_ref, rstd_ref,
     w_ref, vpad_ref, z_ref, sem) = rest[n_pieces:]
    r = pieces[0].shape[0]
    loads = []
    for i in range(n_pieces):
        copy = pltpu.make_async_copy(
            pieces[i].at[:, pl.ds(0, 4 * D)], w_ref.at[pl.ds(pl.multiple_of(starts_ref[i] * r, r), r), :], sem.at[i])
        copy.start()
        loads.append(copy)
    vpad_ref[:, 0:LEAD] = jnp.zeros((D, LEAD), bf16)
    vpad_ref[:, LEAD + T :] = jnp.zeros((D, LEAD), bf16)
    xl_ref[...] = x_ref[...].astype(bf16)
    for copy in loads:
        copy.wait()

    for part, column in ((0, p), (1, None), (2, p + 1)):

        def mix_step(i, _):
            at = rows(part * D + i * 256, 256)
            got = dot(w_ref[:, at], xl_ref[...], TN)
            if column is not None:
                got = got + par_ref[rows(i * 256, 256), column : column + 1]
            mix_ref[at, :] = got.astype(bf16)
            return 0

        lax.fori_loop(0, 3, mix_step, 0)
    vpad_ref[:, LEAD : LEAD + T] = mix_ref[2 * D :, :]
    mean = segment_mean()
    lm_ref[...] = dot(mix_ref[0 : 2 * D, :], mean, NN).astype(bf16)

    for h in range(HEADS):
        ql = lm_ref[h * HD : (h + 1) * HD, :]
        kl = lm_ref[D + h * HD : D + (h + 1) * HD, :]
        s = dot(ql, kl, TN) * SCALE
        e = jnp.exp(s - jnp.max(s, axis=1, keepdims=True))
        a = e / jnp.sum(e, axis=1, keepdims=True)
        a_ref[h] = a
        z_ref[h] = a.T / jnp.sum(a * a)

    def ns_step(k, _):
        ps, rs = [], []
        for h in range(HEADS):
            z = z_ref[h]
            ns_ref[k, 0, h] = z
            p = dot3(split(a_ref[h]), split(z), NN)
            ns_ref[k, 1, h] = p
            ps.append(split(p))
            rs.append(split(eye(7.0) - p))
        for h in range(HEADS):
            r2 = eye(15.0) - dot3(ps[h], rs[h], NN)
            ns_ref[k, 2, h] = r2
            rs[h] = split(r2)
        for h in range(HEADS):
            r3 = eye(13.0) - dot3(ps[h], rs[h], NN)
            ns_ref[k, 3, h] = r3
            rs[h] = split(r3)
        for h in range(HEADS):
            z_ref[h] = 0.25 * dot3(split(z_ref[h]), rs[h], NN)
        return 0

    lax.fori_loop(0, NS_ITERS, ns_step, 0)

    def head_step(h, _):
        base = h * HD
        q = mix_ref[rows(base, HD), :]
        k = mix_ref[rows(D + base, HD), :]
        v = mix_ref[rows(2 * D + base, HD), :]
        ql = lm_ref[rows(base, HD), :]
        kl = lm_ref[rows(D + base, HD), :]
        s = dot(kl, q, TN) * SCALE
        e = jnp.exp(s - jnp.max(s, axis=0, keepdims=True))
        f = (e / jnp.sum(e, axis=0, keepdims=True)).astype(bf16)
        f_ref[rows(base, HD), :] = f
        s = dot(ql, k, TN) * SCALE
        e = jnp.exp(s - jnp.max(s, axis=1, keepdims=True))
        b = (e / jnp.sum(e, axis=1, keepdims=True)).astype(bf16)
        b_ref[rows(base, HD), :] = b
        bv = dot(b, v, NT)
        z = z_ref[h]
        w = dot3(split(z), split(bv), NN)
        small_ref[0, h] = z
        small_ref[1, h] = bv
        small_ref[2, h] = w
        attended = dot(w.astype(bf16), f, TN)
        conv = dot(windows(vpad_ref, base), toeplitz(conv_ref[h, 0:1]), NT)
        ctx_ref[rows(base, HD), :] = (attended + unstack_blocks(conv)).astype(bf16)
        return 0

    lax.fori_loop(0, HEADS, head_step, 0)

    def out_step(i, _):
        base = i * 256
        got = dot(w_ref[:, pl.ds(pl.multiple_of(3 * D + base, 256), 256)], ctx_ref[...], TN)
        xhat_ref[rows(base, 256), :] = got + par_ref[rows(base, 256), p + 2 : p + 3] + x_ref[rows(base, 256), :]
        return 0

    lax.fori_loop(0, 3, out_step, 0)
    norm_forward(xhat_ref, xhat_ref, rstd_ref)


def vm():
    return pl.BlockSpec(memory_space=pltpu.VMEM)


def attention_forward(x, pieces, starts, par, conv, layer):
    n = len(pieces)
    sd = jax.ShapeDtypeStruct
    return pl.pallas_call(
        functools.partial(attention_forward_kernel, n, 8 * layer),
        out_shape=[
            sd((D, T), bf16), sd((3 * D, T), bf16), sd((D, T), bf16), sd((D, T), bf16), sd((D, T), bf16),
            sd((2 * D, LM), bf16), sd((HEADS, LM, LM), f32), sd((NS_ITERS, 4, HEADS, LM, LM), f32),
            sd((3, HEADS, LM, LM), f32), sd((D, T), f32), sd((8, T), f32),
        ],
        in_specs=[pl.BlockSpec(memory_space=pltpu.SMEM), vm(), vm(), vm()]
        + [pl.BlockSpec(memory_space=pl.ANY)] * n,
        out_specs=[vm()] * 11,
        scratch_shapes=[
            pltpu.VMEM((D, 4 * D), bf16),
            pltpu.VMEM((D, T + 2 * LEAD), bf16),
            pltpu.VMEM((HEADS, LM, LM), f32),
            pltpu.SemaphoreType.DMA((n,)),
        ],
        compiler_params=pltpu.CompilerParams(vmem_limit_bytes=VMEM_LIMIT),
        cost_estimate=pl.CostEstimate(flops=6_500_000_000, bytes_accessed=30_000_000, transcendentals=2_000_000),
        name="attention_forward",
    )(starts, x, par, conv, *pieces)


CHUNK = 768
STEPS = FF // CHUNK
SUB = 256


def feed_forward_kernel(n_in, n_out, p, last, in_starts, out_starts, xhat_ref, par_ref, inb_ref, *rest):
    in_pieces, rest = rest[:n_in], rest[n_in:]
    out_pieces, rest = rest[:n_out], rest[n_out:]
    (a_ref, g_ref, xhat2_ref, rstd2_ref, next_ref, w1_ref, w2_ref, hl_ref, sem1, sem2) = rest
    j = pl.program_id(0)
    r1, r2 = in_pieces[0].shape[0], out_pieces[0].shape[0]

    def load1(i):
        return pltpu.make_async_copy(
            in_pieces[i], w1_ref.at[pl.ds(pl.multiple_of(in_starts[i] * r1, r1), r1), :], sem1.at[i])

    def load2(i):
        return pltpu.make_async_copy(
            out_pieces[i], w2_ref.at[pl.ds(pl.multiple_of(out_starts[i] * r2, r2), r2), :], sem2.at[i])

    @pl.when(j == 0)
    def _():
        for i in range(n_in):
            load1(i).start()
        for i in range(n_out):
            load2(i).start()
        h = xhat_ref[...] * par_ref[:, p + 6 : p + 7] + par_ref[:, p + 3 : p + 4]
        hl_ref[...] = h.astype(bf16)
        xhat2_ref[...] = h + par_ref[:, p + 4 : p + 5]
        for i in range(n_in):
            load1(i).wait()
        for i in range(n_out):
            load2(i).wait()

    def up_step(i, _):
        base = i * SUB
        at = j * CHUNK + base
        u = dot(w1_ref[:, pl.ds(pl.multiple_of(at, SUB), SUB)], hl_ref[...], TN)
        u = u + inb_ref[rows(at, SUB), 0:1]
        cdf = 0.5 + 0.5 * lax.erf(u * (2.0 ** -0.5))
        pdf = jnp.exp(-0.5 * u * u) * ((2.0 * np.pi) ** -0.5)
        a_ref[rows(base, SUB), :] = (u * cdf).astype(bf16)
        g_ref[rows(base, SUB), :] = (cdf + u * pdf).astype(bf16)
        return 0

    lax.fori_loop(0, CHUNK // SUB, up_step, 0)

    def down_step(i, _):
        base = i * SUB
        xhat2_ref[rows(base, SUB), :] += dot(
            w2_ref[rows(j * CHUNK, CHUNK), pl.ds(pl.multiple_of(base, SUB), SUB)], a_ref[...], TN)
        return 0

    lax.fori_loop(0, D // SUB, down_step, 0)

    @pl.when(j == STEPS - 1)
    def _():
        norm_forward(xhat2_ref, xhat2_ref, rstd2_ref)
        y = xhat2_ref[...] * par_ref[:, p + 7 : p + 8] + par_ref[:, p + 5 : p + 6]
        if last:
            next_ref[...] = y.T.astype(bf16)
        else:
            next_ref[...] = y


def feed_forward(xhat, in_pieces, out_pieces, in_starts, out_starts, par, inb, layer, last):
    n1, n2 = len(in_pieces), len(out_pieces)
    sd = jax.ShapeDtypeStruct
    smem = pl.BlockSpec(memory_space=pltpu.SMEM)
    anyspec = pl.BlockSpec(memory_space=pl.ANY)
    whole = lambda *s: pl.BlockSpec(s, lambda j: (0,) * len(s))
    next_shape = (T, D) if last else (D, T)
    return pl.pallas_call(
        functools.partial(feed_forward_kernel, n1, n2, 8 * layer, last),
        grid=(STEPS,),
        out_shape=[
            sd((FF, T), bf16), sd((FF, T), bf16), sd((D, T), f32), sd((8, T), f32),
            sd(next_shape, bf16 if last else f32),
        ],
        in_specs=[smem, smem, whole(D, T), whole(D, 128), whole(FF, 1)] + [anyspec] * (n1 + n2),
        out_specs=[
            pl.BlockSpec((CHUNK, T), lambda j: (j, 0)), pl.BlockSpec((CHUNK, T), lambda j: (j, 0)),
            whole(D, T), whole(8, T), whole(*next_shape),
        ],
        scratch_shapes=[
            pltpu.VMEM((D, FF), bf16), pltpu.VMEM((FF, D), bf16), pltpu.VMEM((D, T), bf16),
            pltpu.SemaphoreType.DMA((n1,)), pltpu.SemaphoreType.DMA((n2,)),
        ],
        compiler_params=pltpu.CompilerParams(vmem_limit_bytes=VMEM_LIMIT),
        cost_estimate=pl.CostEstimate(flops=9_700_000_000, bytes_accessed=30_000_000, transcendentals=6_000_000),
        name="feed_forward",
    )(in_starts, out_starts, xhat, par, inb, *in_pieces, *out_pieces)


def norm_backward(dy_ref, xhat_ref, rstd_ref, gain, out_ref, grads_ref, gain_col, shift_col, width=128):
    total_gain = jnp.zeros((D, width), f32)
    total_shift = jnp.zeros((D, width), f32)
    for c in range(0, T, width):
        dy = dy_ref[:, c : c + width]
        xhat = xhat_ref[:, c : c + width]
        total_shift = total_shift + dy
        total_gain = total_gain + dy * xhat
        dxhat = dy * gain
        m1 = jnp.mean(dxhat, axis=0, keepdims=True)
        m2 = jnp.mean(dxhat * xhat, axis=0, keepdims=True)
        out_ref[:, c : c + width] = rstd_ref[0:1, c : c + width] * (dxhat - m1 - xhat * m2)
    grads_ref[:, gain_col : gain_col + 1] = jnp.sum(total_gain, axis=1, keepdims=True)
    grads_ref[:, shift_col : shift_col + 1] = jnp.sum(total_shift, axis=1, keepdims=True)


def lane_sum(value):
    return jnp.sum(value.astype(f32), axis=1, keepdims=True)


def permute_rows(dst_ref, src_ref, order_ref, offset, block):
    for i in range(D // block):
        dst_ref[i * block : (i + 1) * block, :] = src_ref[
            pl.ds(pl.multiple_of(order_ref[offset + i] * block, block), block), :]


def feed_backward_kernel(
    n_in, n_out, p, first, order_ref, dy_ref, xhat2_ref, rstd2_ref, xhat1_ref, rstd1_ref, par_ref, a_ref, g_ref, *rest
):
    in_pieces, rest = rest[:n_in], rest[n_in:]
    out_pieces, rest = rest[:n_out], rest[n_out:]
    (keep2_ref, send2_ref, keep1_ref, send1_ref, inb_ref, dr1_ref, cols_ref,
     w1_ref, w2_ref, hl_ref, dz_ref, du_ref, acc_ref, sem1, sem2) = rest
    j = pl.program_id(0)
    r1, r2 = in_pieces[0].shape[0], out_pieces[0].shape[0]

    def load1(i):
        return pltpu.make_async_copy(
            in_pieces[i], w1_ref.at[pl.ds(pl.multiple_of(order_ref[IN_AT + i] * r1, r1), r1), :], sem1.at[i])

    def load2(i):
        return pltpu.make_async_copy(
            out_pieces[i], w2_ref.at[pl.ds(pl.multiple_of(order_ref[IN_AT + i] * r2, r2), r2), :], sem2.at[i])

    @pl.when(j == 0)
    def _():
        for i in range(n_out):
            load2(i).start()
        for i in range(n_in):
            load1(i).start()
        if first:
            acc_ref[...] = dy_ref[...].astype(f32).T
            dy = acc_ref
        else:
            dy = dy_ref
        cols_ref[...] = jnp.zeros_like(cols_ref)
        norm_backward(dy, xhat2_ref, rstd2_ref, par_ref[:, p + 7 : p + 8], acc_ref, cols_ref, 7, 5)
        dz_ref[...] = acc_ref[...].astype(bf16)
        cols_ref[:, 4:5] = lane_sum(dz_ref[...])
        block = D // 8
        for i in range(8):
            at = pl.ds(pl.multiple_of(order_ref[ROW_AT + i] * block, block), block)
            hl_ref[i * block : (i + 1) * block, :] = (
                xhat1_ref[at, :] * par_ref[at, p + 6 : p + 7] + par_ref[at, p + 3 : p + 4]).astype(bf16)
        for i in range(n_out):
            load2(i).wait()
        for i in range(n_in):
            load1(i).wait()

    def du_step(i, _):
        base = i * SUB
        da = dot(w2_ref[rows(j * CHUNK + base, SUB), :], dz_ref[...], NN)
        du = (da * g_ref[rows(base, SUB), :].astype(f32)).astype(bf16)
        du_ref[rows(base, SUB), :] = du
        inb_ref[rows(base, SUB), :] = lane_sum(du)
        return 0

    lax.fori_loop(0, CHUNK // SUB, du_step, 0)
    half = CHUNK // 2
    core = order_ref[CORE_AT]
    keep2_ref[0] = dot(a_ref[rows(core * half, half), :], dz_ref[...], NT).astype(bf16)
    send2_ref[0] = dot(a_ref[rows((1 - core) * half, half), :], dz_ref[...], NT).astype(bf16)

    for i, out_ref in enumerate((keep1_ref, send1_ref)):
        out_ref[...] = dot(hl_ref[i * (D // 2) : (i + 1) * (D // 2), :], du_ref[...], NT).astype(bf16)

    def dh_step(i, _):
        acc_ref[rows(i * SUB, SUB), :] += dot(
            w1_ref[rows(i * SUB, SUB), rows(j * CHUNK, CHUNK)], du_ref[...], NN)
        return 0

    lax.fori_loop(0, D // SUB, dh_step, 0)

    @pl.when(j == STEPS - 1)
    def _():
        norm_backward(acc_ref, xhat1_ref, rstd1_ref, par_ref[:, p + 6 : p + 7], dr1_ref, cols_ref, 6, 3)
        cols_ref[:, 2:3] = lane_sum(dr1_ref[...].astype(bf16))


IN_AT = 0
ROW_AT = 8
KEEP_AT = 16
SEND_AT = 20
CORE_AT = 24


def feed_backward(dy, xhat2, rstd2, xhat1, rstd1, par, a, g, in_pieces, out_pieces, order, layer, first):
    n1, n2 = len(in_pieces), len(out_pieces)
    sd = jax.ShapeDtypeStruct
    anyspec = pl.BlockSpec(memory_space=pl.ANY)
    whole = lambda *s: pl.BlockSpec(s, lambda j, o: (0,) * len(s))
    chunk = pl.BlockSpec((CHUNK, T), lambda j, o: (j, 0))
    half = CHUNK // 2
    return pl.pallas_call(
        functools.partial(feed_backward_kernel, n1, n2, 8 * layer, first),
        grid_spec=pltpu.PrefetchScalarGridSpec(
            num_scalar_prefetch=1,
            grid=(STEPS,),
            in_specs=[whole(*dy.shape), whole(D, T), whole(8, T), whole(D, T), whole(8, T), whole(D, 128), chunk, chunk]
            + [anyspec] * (n1 + n2),
            out_specs=[
                pl.BlockSpec((1, half, D), lambda j, o: (o[KEEP_AT + j], 0, 0)),
                pl.BlockSpec((1, half, D), lambda j, o: (o[SEND_AT + j], 0, 0)),
                pl.BlockSpec((D // 2, CHUNK), lambda j, o: (0, j)), pl.BlockSpec((D // 2, CHUNK), lambda j, o: (0, j)),
                pl.BlockSpec((CHUNK, 1), lambda j, o: (j, 0)),
                whole(D, T), whole(D, 8),
            ],
            scratch_shapes=[
                pltpu.VMEM((D, FF), bf16), pltpu.VMEM((FF, D), bf16), pltpu.VMEM((D, T), bf16),
                pltpu.VMEM((D, T), bf16), pltpu.VMEM((CHUNK, T), bf16), pltpu.VMEM((D, T), f32),
                pltpu.SemaphoreType.DMA((n1,)), pltpu.SemaphoreType.DMA((n2,)),
            ],
        ),
        out_shape=[
            sd((STEPS, half, D), bf16), sd((STEPS, half, D), bf16), sd((D // 2, FF), bf16), sd((D // 2, FF), bf16), sd((FF, 1), f32),
            sd((D, T), f32), sd((D, 8), f32),
        ],
        compiler_params=pltpu.CompilerParams(vmem_limit_bytes=VMEM_LIMIT),
        cost_estimate=pl.CostEstimate(flops=19_400_000_000, bytes_accessed=50_000_000, transcendentals=0),
        name="feed_backward",
    )(order, dy, xhat2, rstd2, xhat1, rstd1, par, a, g, *in_pieces, *out_pieces)


def attention_backward_kernel(
    n_pieces, first, order_ref, dr1_ref, xl_ref, mix_ref, ctx_ref, f_ref, b_ref, lm_ref, a_ref, ns_ref, small_ref,
    conv_ref, *rest
):
    pieces = rest[:n_pieces]
    (keep_ref, send_ref, dx_ref, cols_ref, taps_ref,
     w_ref, dp_ref, perm_ref, dctx_ref, dmix_ref, vpad_ref, dpad_ref, dz_ref, da_ref, sem) = rest[n_pieces:]
    r = pieces[0].shape[0]
    loads = []
    for i in range(n_pieces):
        copy = pltpu.make_async_copy(
            pieces[i].at[:, pl.ds(0, 4 * D)], w_ref.at[pl.ds(pl.multiple_of(order_ref[IN_AT + i] * r, r), r), :], sem.at[i])
        copy.start()
        loads.append(copy)
    for ref in (vpad_ref, dpad_ref):
        ref[:, 0:LEAD] = jnp.zeros((D, LEAD), bf16)
        ref[:, LEAD + T :] = jnp.zeros((D, LEAD), bf16)
    vpad_ref[:, LEAD : LEAD + T] = mix_ref[2 * D :, :]
    dp_ref[...] = dr1_ref[...].astype(bf16)
    permute_rows(perm_ref, ctx_ref, order_ref, ROW_AT, D // 8)

    for i, out_ref in enumerate((keep_ref, send_ref)):
        out_ref[:, 3 * D :] = dot(perm_ref[i * (D // 2) : (i + 1) * (D // 2), :], dp_ref[...], NT).astype(bf16)
    for copy in loads:
        copy.wait()

    def dctx_step(i, _):
        got = dot(w_ref[rows(i * SUB, SUB), 3 * D :], dp_ref[...], NN).astype(bf16)
        dctx_ref[rows(i * SUB, SUB), :] = got
        dpad_ref[rows(i * SUB, SUB), LEAD : LEAD + T] = got
        return 0

    lax.fori_loop(0, D // SUB, dctx_step, 0)
    spread = segment_spread()
    flip = jnp.where(
        lax.broadcasted_iota(jnp.int32, (CONV_N, CONV_N), 0)
        + lax.broadcasted_iota(jnp.int32, (CONV_N, CONV_N), 1) == CONV_N - 1, 1.0, 0.0).astype(bf16)

    def value_step(h, _):
        base = h * HD
        dctx = dctx_ref[rows(base, HD), :]
        f = f_ref[rows(base, HD), :]
        dw = split(dot(f, dctx, NT))
        dz_ref[h] = dot3(dw, split(small_ref[1, h]), NT)
        dbv = dot3(split(small_ref[0, h]), dw, TN)
        da_ref[h] = dbv
        vw = windows(vpad_ref, base)
        dw_ = windows(dpad_ref, base)
        dv = dot(dbv.astype(bf16), b_ref[rows(base, HD), :], TN)
        conv = dot(dw_, toeplitz(conv_ref[h, 1:2]), NT)
        dmix_ref[rows(2 * D + base, HD), :] = (dv + unstack_blocks(conv)).astype(bf16)
        flipped = dot(stack_blocks(dctx), flip, NN).astype(bf16)
        g = dot(flipped, vw, TN)
        g = pltpu.roll(g, CONV_K - CONV_N + 1, 1, stride=1, stride_axis=0)
        taps_ref[h] = jnp.sum(g, axis=0, keepdims=True)
        return 0

    lax.fori_loop(0, HEADS, value_step, 0)

    def score_b_step(h, _):
        base = h * HD
        b = b_ref[rows(base, HD), :].astype(f32)
        db = dot(da_ref[h].astype(bf16), mix_ref[rows(2 * D + base, HD), :], NN)
        ds = SCALE * b * (db - jnp.sum(b * db, axis=1, keepdims=True))
        b_out = ds.astype(bf16)
        dmix_ref[rows(D + base, HD), :] = b_out
        return 0

    lax.fori_loop(0, HEADS, score_b_step, 0)

    for h in range(HEADS):
        da_ref[h] = jnp.zeros((LM, LM), f32)

    def ns_step(i, _):
        k = NS_ITERS - 1 - i
        d3, dzs, dps, d2 = [], [], [], []
        for h in range(HEADS):
            dzn = split(0.25 * dz_ref[h])
            d3.append(split(dot3(split(ns_ref[k, 0, h]), dzn, TN)))
            dz_ref[h] = dot3(dzn, split(ns_ref[k, 3, h]), NT)
        for h in range(HEADS):
            p = split(ns_ref[k, 1, h])
            d2.append(split(-dot3(p, d3[h], TN)))
            dps.append(dot3(d3[h], split(ns_ref[k, 2, h]), NT))
        for h in range(HEADS):
            p = ns_ref[k, 1, h]
            d1 = dot3(split(p), d2[h], TN)
            dp = d1 - dps[h] - dot3(d2[h], split(eye(7.0) - p), NT)
            dps[h] = split(dp)
        for h in range(HEADS):
            da_ref[h] += dot3(dps[h], split(ns_ref[k, 0, h]), NT)
            dz_ref[h] += dot3(split(a_ref[h]), dps[h], TN)
        return 0

    lax.fori_loop(0, NS_ITERS, ns_step, 0)

    def score_step(h, _):
        base = h * HD
        a = a_ref[h]
        dz0 = dz_ref[h].T
        s = 1.0 / jnp.sum(a * a)
        da = da_ref[h] + s * dz0 - (2.0 * s * s * jnp.sum(dz0 * a)) * a
        dsa = (SCALE * a * (da - jnp.sum(a * da, axis=1, keepdims=True))).astype(bf16)
        ql = lm_ref[rows(base, HD), :]
        kl = lm_ref[rows(D + base, HD), :]
        q = mix_ref[rows(base, HD), :]
        k = mix_ref[rows(D + base, HD), :]
        f = f_ref[rows(base, HD), :].astype(f32)
        df = dot(small_ref[2, h].astype(bf16), dctx_ref[rows(base, HD), :], NN)
        dsf = (SCALE * f * (df - jnp.sum(f * df, axis=0, keepdims=True))).astype(bf16)
        dsb = dmix_ref[rows(D + base, HD), :]
        dkl = dot(q, dsf, NT) + dot(ql, dsa, NN)
        dql = dot(kl, dsa, NT) + dot(k, dsb, NT)
        dq = dot(kl, dsf, NN) + dot((dql * (1.0 / SEG)).astype(bf16), spread, NN)
        dk = dot(ql, dsb, NN) + dot((dkl * (1.0 / SEG)).astype(bf16), spread, NN)
        dmix_ref[rows(base, HD), :] = dq.astype(bf16)
        dmix_ref[rows(D + base, HD), :] = dk.astype(bf16)
        return 0

    lax.fori_loop(0, HEADS, score_step, 0)
    cols_ref[...] = jnp.zeros_like(cols_ref)
    cols_ref[:, 0:1] = lane_sum(dmix_ref[0:D, :])
    cols_ref[:, 1:2] = lane_sum(dmix_ref[2 * D :, :])
    permute_rows(perm_ref, xl_ref, order_ref, ROW_AT, D // 8)

    def gqkv_step(i, _):
        at = rows(i * D, D)
        for part, out_ref in enumerate((keep_ref, send_ref)):
            out_ref[:, at] = dot(
                perm_ref[part * (D // 2) : (part + 1) * (D // 2), :], dmix_ref[at, :], NT).astype(bf16)
        return 0

    lax.fori_loop(0, 3, gqkv_step, 0)

    def dx_step(i, _):
        got = dr1_ref[rows(i * SUB, SUB), :] + dot(w_ref[rows(i * SUB, SUB), 0 : 3 * D], dmix_ref[...], NN)
        if first:
            dx_ref[:, rows(i * SUB, SUB)] = got.T
        else:
            dx_ref[rows(i * SUB, SUB), :] = got
        return 0

    lax.fori_loop(0, D // SUB, dx_step, 0)


def attention_backward(dr1, saved, conv, pieces, order, first):
    n = len(pieces)
    sd = jax.ShapeDtypeStruct
    return pl.pallas_call(
        functools.partial(attention_backward_kernel, n, first),
        out_shape=[
            sd((D // 2, 4 * D), bf16), sd((D // 2, 4 * D), bf16), sd((T, D) if first else (D, T), f32), sd((D, 8), f32),
            sd((HEADS, 1, CONV_K), f32),
        ],
        in_specs=[pl.BlockSpec(memory_space=pltpu.SMEM)] + [vm()] * 11 + [pl.BlockSpec(memory_space=pl.ANY)] * n,
        out_specs=[vm()] * 5,
        scratch_shapes=[
            pltpu.VMEM((D, 4 * D), bf16), pltpu.VMEM((D, T), bf16), pltpu.VMEM((D, T), bf16), pltpu.VMEM((D, T), bf16),
            pltpu.VMEM((3 * D, T), bf16), pltpu.VMEM((D, T + 2 * LEAD), bf16), pltpu.VMEM((D, T + 2 * LEAD), bf16),
            pltpu.VMEM((HEADS, LM, LM), f32), pltpu.VMEM((HEADS, LM, LM), f32), pltpu.SemaphoreType.DMA((n,)),
        ],
        compiler_params=pltpu.CompilerParams(vmem_limit_bytes=VMEM_LIMIT),
        cost_estimate=pl.CostEstimate(flops=15_000_000_000, bytes_accessed=40_000_000, transcendentals=0),
        name="attention_backward",
    )(order, dr1, *saved, conv, *pieces)


class Ring:
    def __init__(self, wide, narrow):
        self.wide, self.narrow = wide, narrow
        self.bits = wide.bit_length() - 1
        up = list(range(1, self.bits))
        self.gather_order = (up, up[::-1])
        self.scatter_order = (up[::-1], up)
        self.exact = wide == 8

    def pairs(self, flip):
        n = self.narrow
        out = []
        for w in range(self.wide):
            for z in range(n):
                to_w, to_z = flip(w, z)
                out.append((w * n + z, to_w * n + to_z))
        return out

    def narrow_pairs(self, k):
        return self.pairs(lambda w, z: (w, z ^ k))

    def step_pairs(self, order, s):
        return self.pairs(lambda w, z: (w ^ (1 << order[w & 1][s]), z))

    def core_pairs(self):
        return self.pairs(lambda w, z: (w ^ 1, z))

    def gathered(self, w):
        out = []
        for other in (0, 1):
            v = w ^ other
            for code in range(self.wide // 2):
                t = v
                for s in range(self.bits - 1):
                    if code >> s & 1:
                        t ^= 1 << self.gather_order[v & 1][s]
                out.append(t)
        return out

    def slots(self, w):
        out = []
        for other in (0, 1):
            v = w ^ other
            for code in range(self.wide // 2):
                t = v
                for s in range(self.bits - 1):
                    if code >> (self.bits - 2 - s) & 1:
                        t ^= 1 << self.scatter_order[v & 1][s]
                out.append(t)
        return out

    def table(self):
        out = np.zeros((self.wide, 32), np.int32)
        for w in range(self.wide):
            if self.exact:
                got, slots = self.gathered(w), self.slots(w)
                out[w, IN_AT : IN_AT + 8] = got
                out[w, ROW_AT : ROW_AT + 8] = slots
                for slot in range(4):
                    out[w, KEEP_AT + (slots[slot] >> 1)] = slot
                    out[w, SEND_AT + (slots[4 + slot] >> 1)] = slot
                out[w, CORE_AT] = w & 1
            else:
                out[w, ROW_AT : ROW_AT + 8] = range(8)
                out[w, KEEP_AT : KEEP_AT + 4] = range(4)
                out[w, SEND_AT : SEND_AT + 4] = range(4)
        return out

    def mine(self, table):
        return lax.dynamic_index_in_dim(jnp.asarray(table), lax.axis_index("wide"), 0, keepdims=False)

    def gather(self, shard):
        z = lax.axis_index("narrow")
        parts = [shard] + [lax.ppermute(shard, AXES, self.narrow_pairs(k)) for k in range(1, self.narrow)]
        bit = 1
        while bit < self.narrow:
            swap = (z & bit) != 0
            parts = [jnp.where(swap, parts[k ^ bit], parts[k]) for k in range(self.narrow)]
            bit *= 2
        held = [jnp.concatenate(parts, axis=0)]
        for s in range(self.bits - 1):
            pairs = self.step_pairs(self.gather_order, s)
            held = held + [lax.ppermute(h, AXES, pairs) for h in held]
        pairs = self.core_pairs()
        return held + [lax.ppermute(h, AXES, pairs) for h in held]

    def join(self, pieces):
        inverse = np.stack([np.argsort(self.gathered(w)) for w in range(self.wide)]).astype(np.int32)
        stacked = jnp.stack(pieces)
        return jnp.take(stacked, self.mine(inverse), axis=0).reshape(-1, stacked.shape[-1])

    def pieces(self, shard):
        got = self.gather(shard)
        return got if self.exact else [self.join(got)]

    def scatter(self, keep, send):
        half = self.wide // 2
        if not self.exact:
            slots = np.stack([self.slots(w) for w in range(self.wide)]).astype(np.int32)
            whole = jnp.concatenate([keep, send], axis=0)
            whole = whole.reshape(self.wide, -1, whole.shape[-1])
            whole = jnp.take(whole, self.mine(slots), axis=0)
            keep, send = whole[:half], whole[half:]
        total = keep.astype(f32) + lax.ppermute(send, AXES, self.core_pairs()).astype(f32)
        for s in range(self.bits - 1):
            half //= 2
            away = total[half:].astype(bf16)
            total = total[:half] + lax.ppermute(away, AXES, self.step_pairs(self.scatter_order, s)).astype(f32)
        total = total[0]
        size = total.shape[0] // self.narrow
        z = lax.axis_index("narrow")
        own = lax.dynamic_slice_in_dim(total, z * size, size, axis=0)
        low = total.astype(bf16)
        for k in range(1, self.narrow):
            part = lax.dynamic_slice_in_dim(low, (z ^ k) * size, size, axis=0)
            own = own + lax.ppermute(part, AXES, self.narrow_pairs(k)).astype(f32)
        return own

    def total(self, value):
        bit = 1
        while bit < self.narrow:
            value = value + lax.ppermute(value, AXES, self.narrow_pairs(bit))
            bit *= 2
        for s in range(self.bits - 1):
            value = value + lax.ppermute(value, AXES, self.pairs(lambda w, z: (w ^ (2 << s), z)))
        return value + lax.ppermute(value, AXES, self.core_pairs())


def natural_halves(keep, send):
    both = jnp.stack([keep, send], axis=1)
    both = both.reshape(2, -1, both.shape[-1])
    return both[0], both[1]


def conv_rows(conv):
    at = LEAD - RADIUS
    tail = CONV_K - at - KSIZE
    both = jnp.stack([conv, conv[:, ::-1]], axis=1)
    return jnp.pad(both.astype(f32), ((0, 0), (0, 0), (at, tail)))


def body(ring, tokens, cotangent, qkv_w, out_w, in_w, in_b, out2_w, bias_rows, gain_rows, conv_w):
    layers = qkv_w.shape[0]
    size = qkv_w.shape[1]
    order = ring.mine(ring.table())
    columns = jnp.concatenate([bias_rows, gain_rows], axis=1)
    columns = columns.transpose(2, 0, 1).reshape(size, 8 * layers)
    hidden = in_b.reshape(layers, size, -1).transpose(1, 0, 2).reshape(size, -1)
    per = hidden.shape[1] // layers
    small = jnp.concatenate([columns, hidden], axis=1)
    small = jnp.pad(small, ((0, 0), (0, 128 - small.shape[1])))
    attention, feed_in, feed_out = [], [], []
    for layer in range(layers):
        parts = [qkv_w[layer], out_w[layer]] + ([small] if layer == 0 else [])
        attention.append(ring.gather(jnp.concatenate(parts, axis=1)))
        feed_in.append(ring.pieces(in_w[layer]))
        feed_out.append(ring.pieces(out2_w[layer]))
    par = ring.join([piece[:, 4 * D :] for piece in attention[0]]).astype(f32)
    if not ring.exact:
        attention = [[ring.join(pieces)] for pieces in attention]

    x = tokens.T.astype(f32)
    kept = []
    for layer in range(layers):
        conv = conv_rows(conv_w[layer])
        at = 8 * layers + per * layer
        inb = par[:, at : at + per].reshape(FF, 1)
        *saved, xhat1, rstd1 = attention_forward(x, attention[layer], order, par, conv, layer)
        a, g, xhat2, rstd2, x = feed_forward(
            xhat1, feed_in[layer], feed_out[layer], order, order, par, inb, layer, layer == layers - 1)
        kept.append((saved, xhat1, rstd1, a, g, xhat2, rstd2, conv))
    output = x
    dy = cotangent
    results = [None] * layers
    for layer in reversed(range(layers)):
        saved, xhat1, rstd1, a, g, xhat2, rstd2, conv = kept[layer]
        keep2, send2, keep1, send1, inb, dr1, cols = feed_backward(
            dy, xhat2, rstd2, xhat1, rstd1, par, a, g, feed_in[layer], feed_out[layer], order, layer,
            layer == layers - 1)
        if not ring.exact:
            keep2, send2 = natural_halves(keep2, send2)
        grad_out2 = ring.scatter(keep2.reshape(ring.wide // 2, -1, D), send2.reshape(ring.wide // 2, -1, D))
        grad_in = ring.scatter(keep1.reshape(ring.wide // 2, -1, FF), send1.reshape(ring.wide // 2, -1, FF))
        keep, send, dy, cols2, taps = attention_backward(dr1, saved, conv, attention[layer], order, layer == 0)
        grad_att = ring.scatter(keep.reshape(ring.wide // 2, -1, 4 * D), send.reshape(ring.wide // 2, -1, 4 * D))
        at = LEAD - RADIUS
        taps = taps[:, 0, at : at + KSIZE]
        flat = jnp.concatenate(
            [cols2[:, :2].T.reshape(-1), cols[:, 2:].T.reshape(-1), inb.reshape(-1), taps.reshape(-1)])
        flat = jnp.pad(flat, (0, -flat.shape[0] % 1024)).reshape(-1, 128)
        flat = ring.total(flat).reshape(-1)
        rest = flat[8 * D :]
        here = lax.axis_index("wide") * ring.narrow + lax.axis_index("narrow")
        mine = lax.dynamic_slice_in_dim(flat[: 8 * D].reshape(8, D), here * size, size, axis=1)
        results[layer] = (
            grad_att[:, : 3 * D], grad_att[:, 3 * D :], grad_in,
            lax.dynamic_slice_in_dim(rest[:FF], here * in_b.shape[1], in_b.shape[1], axis=0),
            grad_out2, mine[:6], mine[6:], rest[FF : FF + HEADS * KSIZE].reshape(HEADS, KSIZE))
    grads = [jnp.stack([results[layer][i] for layer in range(layers)]) for i in range(8)]
    return (output, dy, *grads)


def solution(mesh):
    ring = Ring(mesh.shape["wide"], mesh.shape["narrow"])
    rows3 = P(None, AXES, None)
    columns3 = P(None, None, AXES)
    weights = (rows3, rows3, rows3, P(None, AXES), rows3, columns3, columns3, P())
    return jax.shard_map(
        functools.partial(body, ring),
        mesh=mesh,
        in_specs=(P(AXES, None), P(AXES, None)) + weights,
        out_specs=(P(AXES, None), P(AXES, None)) + weights,
        check_vma=False,
    )
```

time: 2360 us -> 767 us (0.33)
  waiting for transfers between devices: 1000 us -> 211 us
  matrix products: 455 us -> 0 us
  Pallas kernels: 0 us -> 350 us
  blocking collectives: 320 us -> 0 us
  local copies, waits for them, and re-layouts: 316 us -> 21.1 us
  other arithmetic: 236 us -> 38.6 us
  starting transfers between devices: 1.08 us -> 134 us
    reduce_scatter x6 -> x0, waiting for transfers between devices: 754 us -> none  [the longest x2 280 us: body(): lax.psum_scatter(feed_grads[0], ('wide', 'narrow'), scatter_dimension=0,...]
    dot_general x199 -> x0, matrix products: 431 us -> none  [the longest x2 75.8 us: layer_forward(): jnp.dot(normed_low, in_full, preferred_element_type=jnp.float32)]
    pallas_call x0 -> x8, Pallas kernels: none -> 350 us  [the longest x2 125 us: attention_backward(): pl.pallas_call(functools.partial(attention_backward_kernel, n, first), ou...]
    all_gather x4 -> x0, blocking collectives: 280 us -> none  [the longest x2 144 us: body(): lax.all_gather(bias_rows[layer_id], ('wide', 'narrow'), axis=1, tiled=True)]
    unnamed x20 -> x0, waiting for transfers between devices: 248 us -> none
    ppermute x0 -> x106, waiting for transfers between devices: none -> 211 us  [the longest x12 75.6 us: scatter(): lax.ppermute(away, AXES, self.step_pairs(self.scatter_order, s)).astype(f32)]
    reduce_sum x34 -> x0, other arithmetic: 176 us -> none  [the longest x2 106 us: attention_backward(): jnp.sum(grad_mixed[:, 2 * MODEL_WIDTH:].astype(jnp.float32), axis=0)]
    ppermute x0 -> x106, starting transfers between devices: none -> 134 us  [the longest x18 47.1 us: gather(): lax.ppermute(shard, AXES, self.narrow_pairs(k))]
  transfers between devices with their start and end apart: 17 -> 106, of which waited for: 8 -> 36; matrix products, arithmetic and copies ran while one was open for 19% -> 7% of each run, Pallas kernels for 0% -> 28%
where the time goes in v1:
time: 767 us; the launch traced here: 757 us
  Pallas kernels  350 us (46%)
  waiting for transfers between devices  211 us (28%)
  starting transfers between devices  134 us (17%)
  other arithmetic  38.6 us (5%)
  local copies, waits for them, and re-layouts  21.1 us (3%)
    pallas_call x2, Pallas kernels, attention_backward(): pl.pallas_call(functools.partial(attention_backward_kernel, n, first), ou...  125 us
    pallas_call x2, Pallas kernels, feed_backward(): pl.pallas_call(functools.partial(feed_backward_kernel, n1, n2, 8 * layer,...  86.1 us
    pallas_call x2, Pallas kernels, attention_forward(): pl.pallas_call(functools.partial(attention_forward_kernel, n, 8 * layer),...  77.6 us
    ppermute x12, waiting for transfers between devices, scatter(): lax.ppermute(away, AXES, self.step_pairs(self.scatter_order, s)).astype(f32)  75.6 us
    ppermute x18, waiting for transfers between devices, gather(): held = held + [lax.ppermute(h, AXES, pairs) for h in held]  72.1 us
    pallas_call x2, Pallas kernels, feed_forward(): pl.pallas_call(functools.partial(feed_forward_kernel, n1, n2, 8 * layer,...  61.4 us
    ppermute x18, starting transfers between devices, gather(): lax.ppermute(shard, AXES, self.narrow_pairs(k))  47.1 us
    ppermute x18, waiting for transfers between devices, scatter(): own = own + lax.ppermute(part, AXES, self.narrow_pairs(k)).astype(f32)  36.3 us
  transfers between devices with their start and end apart: 106, of which 36 were waited for; matrix products, arithmetic and copies ran while one was open for 7% of the time, Pallas kernels for 28%

profile of v1, /device:TPU:0, one launch (start us, length us, event | category | flops | bytes accessed | tf_op | source)
XLA Modules:
  0.0 757.0 jit_solution(7983698912786250584)
XLA Ops:
  2.4 5.0 collective-permute-start.40
  8.0 2.4 collective-permute-start.11
  13.6 2.1 convert_bitcast_fusion.x_ref
  22.1 5.4 collective-permute-done.41
  27.5 2.7 collective-permute-start.50
  30.2 4.2 collective-permute-done.11
  34.4 2.4 collective-permute-start.52
  36.7 5.1 collective-permute-start.21
  43.1 5.5 collective-permute-start.22
  48.7 4.1 collective-permute-done.51
  52.8 2.7 collective-permute-start
  56.5 3.2 collective-permute-start.2
  59.7 3.2 collective-permute-start.30
  62.9 9.3 %collective-permute-start.31 = (bf16[24,3072]{1,0:T(8,128)(2,1)S(1)}, bf16[24,3072]{1,0:T(8,128)(2,1)S(1)}, u32[]{:S(2)}, u32[]{:S(2)}) collective-permute-start(bf16[24,3072]{1,0:T(8,128)(2,1)S(1)} %pad_maximum_fusion.10), channel_id=1, source_target_pairs={{0,2},{1,3},{2,0},{3,1},{4,6},{5,7},{6,4},{7,5},{8,10},{9,11},{10,... | collective-permute-start | bytes 442376 | tf_op jit(solution)/shard_map/ppermute | solution.py:714
  72.4 1.8 collective-permute-start.32
  74.2 3.0 collective-permute-done.1
  80.5 3.4 collective-permute-done.31
  86.9 6.6 collective-permute-done.13.rest_1_
  97.4 8.8 %collective-permute-done.23.rest_9_ = bf16[384,768]{1,0:T(8,128)(2,1)} collective-permute-done((bf16[384,768]{1,0:T(8,128)(2,1)S(1)}, bf16[384,768]{1,0:T(8,128)(2,1)}, u32[]{:S(2)}, u32[]{:S(2)}) %collective-permute-start.23) | collective-permute-done | bytes 589856 | tf_op jit(solution)/shard_map/ppermute | solution.py:723
  109.2 10.1 %collective-permute-done.3.rest_1_ = bf16[96,3200]{1,0:T(8,128)(2,1)S(1)} collective-permute-done((bf16[96,3200]{1,0:T(8,128)(2,1)S(1)}, bf16[96,3200]{1,0:T(8,128)(2,1)S(1)}, u32[]{:S(2)}, u32[]{:S(2)}) %collective-permute-start.3) | collective-permute-done | bytes 614432 | tf_op jit(solution)/shard_map/ppermute | solution.py:723
  119.4 12.5 %collective-permute-done.33.rest_1_ = bf16[96,3072]{1,0:T(8,128)(2,1)S(1)} collective-permute-done((bf16[96,3072]{1,0:T(8,128)(2,1)S(1)}, bf16[96,3072]{1,0:T(8,128)(2,1)S(1)}, u32[]{:S(2)}, u32[]{:S(2)}) %collective-permute-start.33) | collective-permute-done | bytes 589856 | tf_op jit(solution)/shard_map/ppermute | solution.py:723
  134.0 7.7 %collective-permute-done.5.rest_3_ = bf16[96,3200]{1,0:T(8,128)(2,1)S(1)} collective-permute-done((bf16[96,3200]{1,0:T(8,128)(2,1)S(1)}, bf16[96,3200]{1,0:T(8,128)(2,1)S(1)}, u32[]{:S(2)}, u32[]{:S(2)}) %collective-permute-start.5) | collective-permute-done | bytes 614432 | tf_op jit(solution)/shard_map/ppermute | solution.py:723
  141.8 6.4 collective-permute-done.43.rest_1_
  152.4 11.8 %collective-permute-done.53.rest_9_ = bf16[384,768]{1,0:T(8,128)(2,1)S(1)} collective-permute-done((bf16[384,768]{1,0:T(8,128)(2,1)S(1)}, bf16[384,768]{1,0:T(8,128)(2,1)S(1)}, u32[]{:S(2)}, u32[]{:S(2)}) %collective-permute-start.53) | collective-permute-done | bytes 589856 | tf_op jit(solution)/shard_map/ppermute | solution.py:723
  172.3 4.8 collective-permute-done.25.rest_11_
  177.6 38.8 %attention_forward.2 = (bf16[768,1024]{1,0:T(8,128)(2,1)}, bf16[2304,1024]{1,0:T(8,128)(2,1)}, bf16[768,1024]{1,0:T(8,128)(2,1)}, bf16[768,1024]{1,0:T(8,128)(2,...) custom-call(s32[32]{0:T(128)} %fusion.33.starts_ref.in_starts.out_st, ...), custom_call_target="tpu_custom_call" | custom-call | flops 6499999744 | bytes 30000000 | tf_op jit(solution)/shard_map/attention_forward/pallas_call | solution.py:215
  219.4 30.7 %feed_forward.2 = (bf16[3072,1024]{1,0:T(8,128)(2,1)}, bf16[3072,1024]{1,0:T(8,128)(2,1)}, f32[768,1024]{1,0:T(8,128)}, f32[8,1024]{1,0:T(8,128)}, f32[768,1024]{1,0:T(8,128)}) custom-call(s32[32]{0:T(128)} %fusion.33.starts_ref.in_starts.out_starts.order_ref, s32[32]{0:T(128)} %fusion.33.starts_ref.in_starts.out_starts.order_ref, ...), custom_call_target="tpu_custom_call" | custom-call | flops 9699999744 | bytes 30000000 | tf_op jit(solution)/shard_map/feed_forward/pallas_call | solution.py:309
  251.8 38.9 %attention_forward.3 = (bf16[768,1024]{1,0:T(8,128)(2,1)}, bf16[2304,1024]{1,0:T(8,128)(2,1)}, bf16[768,1024]{1,0:T(8,128)(2,1)}, bf16[768,1024]{1,0:T(8,128)(2,...) custom-call(s32[32]{0:T(128)} %fusion.33.starts_ref.in_starts.out_st, ...), custom_call_target="tpu_custom_call" | custom-call | flops 6499999744 | bytes 30000000 | tf_op jit(solution)/shard_map/attention_forward/pallas_call | solution.py:215
  291.7 30.7 %feed_forward.3 = (bf16[3072,1024]{1,0:T(8,128)(2,1)}, bf16[3072,1024]{1,0:T(8,128)(2,1)}, f32[768,1024]{1,0:T(8,128)}, f32[8,1024]{1,0:T(8,128)}, bf16[1024,768]{1,0:T(8,128)(2,1)}) custom-call(s32[32]{0:T(128)} %fusion.33.starts_ref.in_starts.out_starts.order_ref, s32[32]{0:T(128)} %fusion.33.starts_ref.in_starts.out_starts.order_ref, ...), custom_call_target="tpu_custom_call" | custom-call | flops 9699999744 | bytes 30000000 | tf_op jit(solution)/shard_map/feed_forward/pallas_call | solution.py:309
  322.4 42.9 %feed_backward.2 = (bf16[4,384,768]{2,1,0:T(8,128)(2,1)}, bf16[4,384,768]{2,1,0:T(8,128)(2,1)}, bf16[384,3072]{1,0:T(8,128)(2,1)}, bf16[384,3072]{1,0:T(8,128)(2...) custom-call(s32[32]{0:T(128)} %fusion.33.starts_ref.in_starts.out_starts.order_ref, ...), custom_call_target="tpu_custom_call" | custom-call | flops 19399999488 | bytes 50000000 | tf_op jit(solution)/shard_map/feed_backward/pallas_call | solution.py:444
  365.3 62.1 %attention_backward.2 = (bf16[384,3072]{1,0:T(8,128)(2,1)}, bf16[384,3072]{1,0:T(8,128)(2,1)}, f32[768,1024]{1,0:T(8,128)}, f32[768,8]{1,0:T(8,128)}, f32[12,1,512]{2,1,0:T(1,128)}) custom-call(s32[32]{0:T(128)} %fusion.33.starts_ref.in_starts.out_starts.order_ref, f32[768,1024]{1,0:T(8,128)} %get-tuple-element.75.dr1_ref, ...), custom_call_target="tpu_custom_call" | custom-call | flops 15000000512 | bytes 40000000 | tf_op jit(solution)/shard_map/attention_backward/pallas_call | solution.py:622
  431.2 43.2 %feed_backward.3 = (bf16[4,384,768]{2,1,0:T(8,128)(2,1)}, bf16[4,384,768]{2,1,0:T(8,128)(2,1)}, bf16[384,3072]{1,0:T(8,128)(2,1)}, bf16[384,3072]{1,0:T(8,128)(2...) custom-call(s32[32]{0:T(128)} %fusion.33.starts_ref.in_starts.out_starts.order_ref, ...), custom_call_target="tpu_custom_call" | custom-call | flops 19399999488 | bytes 50000000 | tf_op jit(solution)/shard_map/feed_backward/pallas_call | solution.py:444
  474.4 62.7 %attention_backward.3 = (bf16[384,3072]{1,0:T(8,128)(2,1)}, bf16[384,3072]{1,0:T(8,128)(2,1)}, f32[1024,768]{1,0:T(8,128)}, f32[768,8]{1,0:T(8,128)}, f32[12,1,512]{2,1,0:T(1,128)}) custom-call(s32[32]{0:T(128)} %fusion.33.starts_ref.in_starts.out_starts.order_ref, f32[768,1024]{1,0:T(8,128)} %get-tuple-element.91.dr1_ref, ...), custom_call_target="tpu_custom_call" | custom-call | flops 15000000512 | bytes 40000000 | tf_op jit(solution)/shard_map/attention_backward/pallas_call | solution.py:622
  541.1 2.0 collective-permute-start.84
  546.1 3.3 collective-permute-start.85
  566.5 2.5 convert_add_fusion.2
  570.7 2.5 convert_add_fusion.3
  574.9 2.5 convert_add_fusion
  579.1 2.5 convert_add_fusion.1
  583.3 2.2 convert_add_fusion.4
  591.1 7.0 collective-permute-done.61
  601.4 15.8 %collective-permute-done.79 = bf16[2,96,3072]{2,1,0:T(8,128)(2,1)} collective-permute-done((bf16[2,96,3072]{2,1,0:T(8,128)(2,1)S(1)}, bf16[2,96,3072]{2,1,0:T(8,128)(2,1)}, u32[]{:S(2)}, u32[]{:S(2)}) %collective-permute-start.79) | collective-permute-done | bytes 1179680 | tf_op jit(solution)/shard_map/ppermute | solution.py:748
  620.3 15.8 %collective-permute-done.73 = bf16[2,96,3072]{2,1,0:T(8,128)(2,1)} collective-permute-done((bf16[2,96,3072]{2,1,0:T(8,128)(2,1)S(1)}, bf16[2,96,3072]{2,1,0:T(8,128)(2,1)}, u32[]{:S(2)}, u32[]{:S(2)}) %collective-permute-start.73) | collective-permute-done | bytes 1179680 | tf_op jit(solution)/shard_map/ppermute | solution.py:748
  639.2 15.8 %collective-permute-done.101 = bf16[2,384,768]{2,1,0:T(8,128)(2,1)} collective-permute-done((bf16[2,384,768]{2,1,0:T(8,128)(2,1)}, bf16[2,384,768]{2,1,0:T(8,128)(2,1)}, u32[]{:S(2)}, u32[]{:S(2)}) %collective-permute-start.101) | collective-permute-done | bytes 1179680 | tf_op jit(solution)/shard_map/ppermute | solution.py:748
  658.1 15.8 %collective-permute-done.95 = bf16[2,384,768]{2,1,0:T(8,128)(2,1)S(1)} collective-permute-done((bf16[2,384,768]{2,1,0:T(8,128)(2,1)S(1)}, bf16[2,384,768]{2,1,0:T(8,128)(2,1)S(1)}, u32[]{:S(2)}, u32[]{:S(2)}) %collective-permute-start.95) | collective-permute-done | bytes 1179680 | tf_op jit(solution)/shard_map/ppermute | solution.py:748
  676.6 2.7 collective-permute-start.71
  679.4 2.0 collective-permute-start.70
  683.8 2.6 collective-permute-start.65
  686.6 3.5 collective-permute-done.96
  690.1 2.4 collective-permute-start.64
  693.6 4.8 collective-permute-done.70
  698.4 3.3 collective-permute-start.83
  701.8 6.5 collective-permute-start.81
  708.4 3.7 collective-permute-done.64
  712.1 2.3 collective-permute-start.77
  714.5 2.2 collective-permute-start.75
  716.6 8.1 %collective-permute-done.82 = bf16[24,3072]{1,0:T(8,128)(2,1)S(1)} collective-permute-done((bf16[24,3072]{1,0:T(8,128)(2,1)S(1)}, bf16[24,3072]{1,0:T(8,128)(2,1)S(1)}, u32[]{:S(2)}, u32[]{:S(2)}) %collective-permute-start.82) | collective-permute-done | bytes 147488 | tf_op jit(solution)/shard_map/ppermute | solution.py:756
  724.7 2.3 collective-permute-start.105
  727.9 2.1 collective-permute-start.103
  730.0 7.4 collective-permute-done.76
  737.3 2.3 collective-permute-start.99
  740.6 2.2 collective-permute-start.97
  742.7 7.2 collective-permute-done.104
  750.7 5.1 collective-permute-done.98
  (428 shorter events, 109.8 us)
Async XLA Ops:
  7.4 20.1 %collective-permute-start.41 = (bf16[24,3072]{1,0:T(8,128)(2,1)}, bf16[24,3072]{1,0:T(8,128)(2,1)S(1)}, u32[]{:S(2)}, u32[]{:S(2)}) collective-permute-start(bf16[24,3072]{1,0:T(8,128)(2,1)} %get-tuple-element.208), channel_id=1, source_target_pairs={{0,2},{1,3},{2,0},{3,1},{4,6},{5,7},{6,4},{7,5},{8,10},{9,11},{10,... | collective-permute-start | bytes 442376 | tf_op jit(solution)/shard_map/ppermute | solution.py:714
  7.4 22.8 %collective-permute-start.42 = (bf16[24,3072]{1,0:T(8,128)(2,1)}, bf16[24,3072]{1,0:T(8,128)(2,1)S(1)}, u32[]{:S(2)}, u32[]{:S(2)}) collective-permute-start(bf16[24,3072]{1,0:T(8,128)(2,1)} %get-tuple-element.208), channel_id=1, source_target_pairs={{0,1},{1,0},{2,3},{3,2},{4,5},{5,4},{6,7},{7,6},{8,9},{9,8},{10,11... | collective-permute-start | bytes 442376 | tf_op jit(solution)/shard_map/ppermute | solution.py:714
  8.0 26.4 %collective-permute-start.11 = (bf16[24,3072]{1,0:T(8,128)(2,1)}, bf16[24,3072]{1,0:T(8,128)(2,1)S(1)}, u32[]{:S(2)}, u32[]{:S(2)}) collective-permute-start(bf16[24,3072]{1,0:T(8,128)(2,1)} %get-tuple-element.209), channel_id=1, source_target_pairs={{0,2},{1,3},{2,0},{3,1},{4,6},{5,7},{6,4},{7,5},{8,10},{9,11},{10,... | collective-permute-start | bytes 442376 | tf_op jit(solution)/shard_map/ppermute | solution.py:714
  10.3 26.4 %collective-permute-start.10 = (bf16[24,3072]{1,0:T(8,128)(2,1)}, bf16[24,3072]{1,0:T(8,128)(2,1)S(1)}, u32[]{:S(2)}, u32[]{:S(2)}) collective-permute-start(bf16[24,3072]{1,0:T(8,128)(2,1)} %get-tuple-element.209), channel_id=1, source_target_pairs={{0,3},{1,2},{2,1},{3,0},{4,7},{5,6},{6,5},{7,4},{8,11},{9,10},{10,... | collective-permute-start | bytes 442376 | tf_op jit(solution)/shard_map/ppermute | solution.py:714
  19.3 22.6 %collective-permute-start.12 = (bf16[24,3072]{1,0:T(8,128)(2,1)}, bf16[24,3072]{1,0:T(8,128)(2,1)S(1)}, u32[]{:S(2)}, u32[]{:S(2)}) collective-permute-start(bf16[24,3072]{1,0:T(8,128)(2,1)} %get-tuple-element.209), channel_id=1, source_target_pairs={{0,1},{1,0},{2,3},{3,2},{4,5},{5,4},{6,7},{7,6},{8,9},{9,8},{10,11... | collective-permute-start | bytes 442376 | tf_op jit(solution)/shard_map/ppermute | solution.py:714
  30.2 22.6 %collective-permute-start.51 = (bf16[96,768]{1,0:T(8,128)(2,1)}, bf16[96,768]{1,0:T(8,128)(2,1)S(1)}, u32[]{:S(2)}, u32[]{:S(2)}) collective-permute-start(bf16[96,768]{1,0:T(8,128)(2,1)} %get-tuple-element.202), channel_id=1, source_target_pairs={{0,2},{1,3},{2,0},{3,1},{4,6},{5,7},{6,4},{7,5},{8,10},{9,11},{10,... | collective-permute-start | bytes 442376 | tf_op jit(solution)/shard_map/ppermute | solution.py:714
  34.4 21.1 %collective-permute-start.52 = (bf16[96,768]{1,0:T(8,128)(2,1)}, bf16[96,768]{1,0:T(8,128)(2,1)S(1)}, u32[]{:S(2)}, u32[]{:S(2)}) collective-permute-start(bf16[96,768]{1,0:T(8,128)(2,1)} %get-tuple-element.202), channel_id=1, source_target_pairs={{0,1},{1,0},{2,3},{3,2},{4,5},{5,4},{6,7},{7,6},{8,9},{9,8},{10,11... | collective-permute-start | bytes 442376 | tf_op jit(solution)/shard_map/ppermute | solution.py:714
  36.7 19.7 %collective-permute-start.21 = (bf16[96,768]{1,0:T(8,128)(2,1)}, bf16[96,768]{1,0:T(8,128)(2,1)S(1)}, u32[]{:S(2)}, u32[]{:S(2)}) collective-permute-start(bf16[96,768]{1,0:T(8,128)(2,1)} %get-tuple-element.203), channel_id=1, source_target_pairs={{0,2},{1,3},{2,0},{3,1},{4,6},{5,7},{6,4},{7,5},{8,10},{9,11},{10,... | collective-permute-start | bytes 442376 | tf_op jit(solution)/shard_map/ppermute | solution.py:714
  41.9 17.8 %collective-permute-start.20 = (bf16[96,768]{1,0:T(8,128)(2,1)}, bf16[96,768]{1,0:T(8,128)(2,1)S(1)}, u32[]{:S(2)}, u32[]{:S(2)}) collective-permute-start(bf16[96,768]{1,0:T(8,128)(2,1)} %get-tuple-element.203), channel_id=1, source_target_pairs={{0,3},{1,2},{2,1},{3,0},{4,7},{5,6},{6,5},{7,4},{8,11},{9,10},{10,... | collective-permute-start | bytes 442376 | tf_op jit(solution)/shard_map/ppermute | solution.py:714
  43.1 19.8 %collective-permute-start.22 = (bf16[96,768]{1,0:T(8,128)(2,1)}, bf16[96,768]{1,0:T(8,128)(2,1)S(1)}, u32[]{:S(2)}, u32[]{:S(2)}) collective-permute-start(bf16[96,768]{1,0:T(8,128)(2,1)} %get-tuple-element.203), channel_id=1, source_target_pairs={{0,1},{1,0},{2,3},{3,2},{4,5},{5,4},{6,7},{7,6},{8,9},{9,8},{10,11... | collective-permute-start | bytes 442376 | tf_op jit(solution)/shard_map/ppermute | solution.py:714
  52.8 19.6 %collective-permute-start = (bf16[24,3200]{1,0:T(8,128)(2,1)S(1)}, bf16[24,3200]{1,0:T(8,128)(2,1)S(1)}, u32[]{:S(2)}, u32[]{:S(2)}) collective-permute-start(bf16[24,3200]{1,0:T(8,128)(2,1)S(1)} %pad_maximum_fusion.9), channel_id=1, source_target_pairs={{0,3},{1,2},{2,1},{3,0},{4,7},{5,6},{6,5},{7,4},{8,11},{9,10},{10,... | collective-permute-start | bytes 460808 | tf_op jit(solution)/shard_map/ppermute | solution.py:714
  55.5 21.7 %collective-permute-start.1 = (bf16[24,3200]{1,0:T(8,128)(2,1)S(1)}, bf16[24,3200]{1,0:T(8,128)(2,1)S(1)}, u32[]{:S(2)}, u32[]{:S(2)}) collective-permute-start(bf16[24,3200]{1,0:T(8,128)(2,1)S(1)} %pad_maximum_fusion.9), channel_id=1, source_target_pairs={{0,2},{1,3},{2,0},{3,1},{4,6},{5,7},{6,4},{7,5},{8,10},{9,11},{10,... | collective-permute-start | bytes 460808 | tf_op jit(solution)/shard_map/ppermute | solution.py:714
  56.5 22.2 %collective-permute-start.2 = (bf16[24,3200]{1,0:T(8,128)(2,1)S(1)}, bf16[24,3200]{1,0:T(8,128)(2,1)S(1)}, u32[]{:S(2)}, u32[]{:S(2)}) collective-permute-start(bf16[24,3200]{1,0:T(8,128)(2,1)S(1)} %pad_maximum_fusion.9), channel_id=1, source_target_pairs={{0,1},{1,0},{2,3},{3,2},{4,5},{5,4},{6,7},{7,6},{8,9},{9,8},{10,11... | collective-permute-start | bytes 460808 | tf_op jit(solution)/shard_map/ppermute | solution.py:714
  59.7 20.8 %collective-permute-start.30 = (bf16[24,3072]{1,0:T(8,128)(2,1)S(1)}, bf16[24,3072]{1,0:T(8,128)(2,1)S(1)}, u32[]{:S(2)}, u32[]{:S(2)}) collective-permute-start(bf16[24,3072]{1,0:T(8,128)(2,1)S(1)} %pad_maximum_fusion.10), channel_id=1, source_target_pairs={{0,3},{1,2},{2,1},{3,0},{4,7},{5,6},{6,5},{7,4},{8,11},{9,10},{10,... | collective-permute-start | bytes 442376 | tf_op jit(solution)/shard_map/ppermute | solution.py:714
  62.9 21.0 %collective-permute-start.31 = (bf16[24,3072]{1,0:T(8,128)(2,1)S(1)}, bf16[24,3072]{1,0:T(8,128)(2,1)S(1)}, u32[]{:S(2)}, u32[]{:S(2)}) collective-permute-start(bf16[24,3072]{1,0:T(8,128)(2,1)S(1)} %pad_maximum_fusion.10), channel_id=1, source_target_pairs={{0,2},{1,3},{2,0},{3,1},{4,6},{5,7},{6,4},{7,5},{8,10},{9,11},{10,... | collective-permute-start | bytes 442376 | tf_op jit(solution)/shard_map/ppermute | solution.py:714
  83.9 22.3 %collective-permute-start.23 = (bf16[384,768]{1,0:T(8,128)(2,1)S(1)}, bf16[384,768]{1,0:T(8,128)(2,1)}, u32[]{:S(2)}, u32[]{:S(2)}) collective-permute-start(bf16[384,768]{1,0:T(8,128)(2,1)S(1)} %pad_maximum_fusion.2.rest_8_), channel_id=1, source_target_pairs={{0,8},{1,9},{2,10},{3,11},{4,20},{5,21},{6,22},{7,23},{8,0},{9,1},... | collective-permute-start | bytes 1769480 | tf_op jit(solution)/shard_map/ppermute | solution.py:723
  85.4 22.1 %collective-permute-start.24 = (bf16[384,768]{1,0:T(8,128)(2,1)S(1)}, bf16[384,768]{1,0:T(8,128)(2,1)S(1)}, u32[]{:S(2)}, u32[]{:S(2)}) collective-permute-start(bf16[384,768]{1,0:T(8,128)(2,1)S(1)} %pad_maximum_fusion.2.rest_8_), channel_id=1, source_target_pairs={{0,16},{1,17},{2,18},{3,19},{4,12},{5,13},{6,14},{7,15},{8,24},{9,... | collective-permute-start | bytes 1769480 | tf_op jit(solution)/shard_map/ppermute | solution.py:723
  95.0 24.2 %collective-permute-start.3 = (bf16[96,3200]{1,0:T(8,128)(2,1)S(1)}, bf16[96,3200]{1,0:T(8,128)(2,1)S(1)}, u32[]{:S(2)}, u32[]{:S(2)}) collective-permute-start(bf16[96,3200]{1,0:T(8,128)(2,1)S(1)} %pad_maximum_fusion.rest_0_), channel_id=1, source_target_pairs={{0,8},{1,9},{2,10},{3,11},{4,20},{5,21},{6,22},{7,23},{8,0},{9,1},... | collective-permute-start | bytes 1843208 | tf_op jit(solution)/shard_map/ppermute | solution.py:723
  95.8 36.1 %collective-permute-start.33 = (bf16[96,3072]{1,0:T(8,128)(2,1)S(1)}, bf16[96,3072]{1,0:T(8,128)(2,1)S(1)}, u32[]{:S(2)}, u32[]{:S(2)}) collective-permute-start(bf16[96,3072]{1,0:T(8,128)(2,1)S(1)} %pad_maximum_fusion.3.rest_0_), channel_id=1, source_target_pairs={{0,8},{1,9},{2,10},{3,11},{4,20},{5,21},{6,22},{7,23},{8,0},{9,1},... | collective-permute-start | bytes 1769480 | tf_op jit(solution)/shard_map/ppermute | solution.py:723
  106.2 27.2 %collective-permute-start.34 = (bf16[96,3072]{1,0:T(8,128)(2,1)S(1)}, bf16[96,3072]{1,0:T(8,128)(2,1)S(1)}, u32[]{:S(2)}, u32[]{:S(2)}) collective-permute-start(bf16[96,3072]{1,0:T(8,128)(2,1)S(1)} %pad_maximum_fusion.3.rest_0_), channel_id=1, source_target_pairs={{0,16},{1,17},{2,18},{3,19},{4,12},{5,13},{6,14},{7,15},{8,24},{9,... | collective-permute-start | bytes 1769480 | tf_op jit(solution)/shard_map/ppermute | solution.py:723
  107.6 25.8 %collective-permute-start.36 = (bf16[96,3072]{1,0:T(8,128)(2,1)S(1)}, bf16[96,3072]{1,0:T(8,128)(2,1)S(1)}, u32[]{:S(2)}, u32[]{:S(2)}) collective-permute-start(bf16[96,3072]{1,0:T(8,128)(2,1)S(1)} %pad_maximum_fusion.3.rest_0_), channel_id=1, source_target_pairs={{0,4},{1,5},{2,6},{3,7},{4,0},{5,1},{6,2},{7,3},{8,12},{9,13},{10,... | collective-permute-start | bytes 1769480 | tf_op jit(solution)/shard_map/ppermute | solution.py:725
  107.6 25.9 %collective-permute-start.4 = (bf16[96,3200]{1,0:T(8,128)(2,1)S(1)}, bf16[96,3200]{1,0:T(8,128)(2,1)S(1)}, u32[]{:S(2)}, u32[]{:S(2)}) collective-permute-start(bf16[96,3200]{1,0:T(8,128)(2,1)S(1)} %pad_maximum_fusion.rest_0_), channel_id=1, source_target_pairs={{0,16},{1,17},{2,18},{3,19},{4,12},{5,13},{6,14},{7,15},{8,24},{9,... | collective-permute-start | bytes 1843208 | tf_op jit(solution)/shard_map/ppermute | solution.py:723
  119.3 22.5 %collective-permute-start.5 = (bf16[96,3200]{1,0:T(8,128)(2,1)S(1)}, bf16[96,3200]{1,0:T(8,128)(2,1)S(1)}, u32[]{:S(2)}, u32[]{:S(2)}) collective-permute-start(bf16[96,3200]{1,0:T(8,128)(2,1)S(1)} %collective-permute-done.3.rest_1_), channel_id=1, source_target_pairs={{0,16},{1,17},{2,18},{3,19},{4,12},{5,13},{6,14},{7,15},{8,24},{9,... | collective-permute-start | bytes 1843208 | tf_op jit(solution)/shard_map/ppermute | solution.py:723
  133.5 17.6 %collective-permute-start.7 = (bf16[96,3200]{1,0:T(8,128)(2,1)S(1)}, bf16[96,3200]{1,0:T(8,128)(2,1)S(1)}, u32[]{:S(2)}, u32[]{:S(2)}) collective-permute-start(bf16[96,3200]{1,0:T(8,128)(2,1)S(1)} %collective-permute-done.3.rest_1_), channel_id=1, source_target_pairs={{0,4},{1,5},{2,6},{3,7},{4,0},{5,1},{6,2},{7,3},{8,12},{9,13},{10,... | collective-permute-start | bytes 1843208 | tf_op jit(solution)/shard_map/ppermute | solution.py:725
  151.6 19.1 %collective-permute-start.15 = (bf16[96,3072]{1,0:T(8,128)(2,1)}, bf16[96,3072]{1,0:T(8,128)(2,1)}, u32[]{:S(2)}, u32[]{:S(2)}) collective-permute-start(bf16[96,3072]{1,0:T(8,128)(2,1)} %collective-permute-done.13.rest_1_), channel_id=1, source_target_pairs={{0,16},{1,17},{2,18},{3,19},{4,12},{5,13},{6,14},{7,15},{8,24},{9,... | collective-permute-start | bytes 1769480 | tf_op jit(solution)/shard_map/ppermute | solution.py:723
  170.8 46.7 %collective-permute-start.35 = (bf16[96,3072]{1,0:T(8,128)(2,1)}, bf16[96,3072]{1,0:T(8,128)(2,1)}, u32[]{:S(2)}, u32[]{:S(2)}) collective-permute-start(bf16[96,3072]{1,0:T(8,128)(2,1)} %copy-done.38), channel_id=1, source_target_pairs={{0,16},{1,17},{2,18},{3,19},{4,12},{5,13},{6,14},{7,15},{8,24},{9,... | collective-permute-start | bytes 1769480 | tf_op jit(solution)/shard_map/ppermute | solution.py:723
  171.7 46.2 %collective-permute-start.37 = (bf16[96,3072]{1,0:T(8,128)(2,1)}, bf16[96,3072]{1,0:T(8,128)(2,1)}, u32[]{:S(2)}, u32[]{:S(2)}) collective-permute-start(bf16[96,3072]{1,0:T(8,128)(2,1)} %copy-done.38), channel_id=1, source_target_pairs={{0,4},{1,5},{2,6},{3,7},{4,0},{5,1},{6,2},{7,3},{8,12},{9,13},{10,... | collective-permute-start | bytes 1769480 | tf_op jit(solution)/shard_map/ppermute | solution.py:725
  172.2 44.2 %collective-permute-start.28 = (bf16[384,768]{1,0:T(8,128)(2,1)}, bf16[384,768]{1,0:T(8,128)(2,1)S(1)}, u32[]{:S(2)}, u32[]{:S(2)}) collective-permute-start(bf16[384,768]{1,0:T(8,128)(2,1)} %copy-done.36), channel_id=1, source_target_pairs={{0,4},{1,5},{2,6},{3,7},{4,0},{5,1},{6,2},{7,3},{8,12},{9,13},{10,... | collective-permute-start | bytes 1769480 | tf_op jit(solution)/shard_map/ppermute | solution.py:725
  177.1 40.9 %collective-permute-start.19 = (bf16[96,3072]{1,0:T(8,128)(2,1)}, bf16[96,3072]{1,0:T(8,128)(2,1)S(1)}, u32[]{:S(2)}, u32[]{:S(2)}) collective-permute-start(bf16[96,3072]{1,0:T(8,128)(2,1)} %collective-permute-done.15.rest_3_), channel_id=1, source_target_pairs={{0,4},{1,5},{2,6},{3,7},{4,0},{5,1},{6,2},{7,3},{8,12},{9,13},{10,... | collective-permute-start | bytes 1769480 | tf_op jit(solution)/shard_map/ppermute | solution.py:725
  177.3 42.1 %collective-permute-start.29 = (bf16[384,768]{1,0:T(8,128)(2,1)}, bf16[384,768]{1,0:T(8,128)(2,1)}, u32[]{:S(2)}, u32[]{:S(2)}) collective-permute-start(bf16[384,768]{1,0:T(8,128)(2,1)} %collective-permute-done.25.rest_11_), channel_id=1, source_target_pairs={{0,4},{1,5},{2,6},{3,7},{4,0},{5,1},{6,2},{7,3},{8,12},{9,13},{10,... | collective-permute-start | bytes 1769480 | tf_op jit(solution)/shard_map/ppermute | solution.py:725
  216.4 34.3 %collective-permute-start.45 = (bf16[96,3072]{1,0:T(8,128)(2,1)S(1)}, bf16[96,3072]{1,0:T(8,128)(2,1)}, u32[]{:S(2)}, u32[]{:S(2)}) collective-permute-start(bf16[96,3072]{1,0:T(8,128)(2,1)S(1)} %copy-done.43), channel_id=1, source_target_pairs={{0,16},{1,17},{2,18},{3,19},{4,12},{5,13},{6,14},{7,15},{8,24},{9,... | collective-permute-start | bytes 1769480 | tf_op jit(solution)/shard_map/ppermute | solution.py:723
  217.5 33.3 %collective-permute-start.47 = (bf16[96,3072]{1,0:T(8,128)(2,1)S(1)}, bf16[96,3072]{1,0:T(8,128)(2,1)}, u32[]{:S(2)}, u32[]{:S(2)}) collective-permute-start(bf16[96,3072]{1,0:T(8,128)(2,1)S(1)} %copy-done.43), channel_id=1, source_target_pairs={{0,4},{1,5},{2,6},{3,7},{4,0},{5,1},{6,2},{7,3},{8,12},{9,13},{10,... | collective-permute-start | bytes 1769480 | tf_op jit(solution)/shard_map/ppermute | solution.py:725
  217.9 32.2 %collective-permute-start.38 = (bf16[96,3072]{1,0:T(8,128)(2,1)S(1)}, bf16[96,3072]{1,0:T(8,128)(2,1)}, u32[]{:S(2)}, u32[]{:S(2)}) collective-permute-start(bf16[96,3072]{1,0:T(8,128)(2,1)S(1)} %copy-done.40), channel_id=1, source_target_pairs={{0,4},{1,5},{2,6},{3,7},{4,0},{5,1},{6,2},{7,3},{8,12},{9,13},{10,... | collective-permute-start | bytes 1769480 | tf_op jit(solution)/shard_map/ppermute | solution.py:725
  218.0 33.2 %collective-permute-start.55 = (bf16[384,768]{1,0:T(8,128)(2,1)S(1)}, bf16[384,768]{1,0:T(8,128)(2,1)}, u32[]{:S(2)}, u32[]{:S(2)}) collective-permute-start(bf16[384,768]{1,0:T(8,128)(2,1)S(1)} %copy-done.48), channel_id=1, source_target_pairs={{0,16},{1,17},{2,18},{3,19},{4,12},{5,13},{6,14},{7,15},{8,24},{9,... | collective-permute-start | bytes 1769480 | tf_op jit(solution)/shard_map/ppermute | solution.py:723
  219.4 32.0 %collective-permute-start.39 = (bf16[96,3072]{1,0:T(8,128)(2,1)}, bf16[96,3072]{1,0:T(8,128)(2,1)}, u32[]{:S(2)}, u32[]{:S(2)}) collective-permute-start(bf16[96,3072]{1,0:T(8,128)(2,1)} %collective-permute-done.35.rest_3_), channel_id=1, source_target_pairs={{0,4},{1,5},{2,6},{3,7},{4,0},{5,1},{6,2},{7,3},{8,12},{9,13},{10,... | collective-permute-start | bytes 1769480 | tf_op jit(solution)/shard_map/ppermute | solution.py:725
  250.1 40.5 %collective-permute-start.57 = (bf16[384,768]{1,0:T(8,128)(2,1)S(1)}, bf16[384,768]{1,0:T(8,128)(2,1)S(1)}, u32[]{:S(2)}, u32[]{:S(2)}) collective-permute-start(bf16[384,768]{1,0:T(8,128)(2,1)S(1)} %copy-done.48), channel_id=1, source_target_pairs={{0,4},{1,5},{2,6},{3,7},{4,0},{5,1},{6,2},{7,3},{8,12},{9,13},{10,... | collective-permute-start | bytes 1769480 | tf_op jit(solution)/shard_map/ppermute | solution.py:725
  250.7 39.9 %collective-permute-start.48 = (bf16[96,3072]{1,0:T(8,128)(2,1)S(1)}, bf16[96,3072]{1,0:T(8,128)(2,1)}, u32[]{:S(2)}, u32[]{:S(2)}) collective-permute-start(bf16[96,3072]{1,0:T(8,128)(2,1)S(1)} %copy-done.45), channel_id=1, source_target_pairs={{0,4},{1,5},{2,6},{3,7},{4,0},{5,1},{6,2},{7,3},{8,12},{9,13},{10,... | collective-permute-start | bytes 1769480 | tf_op jit(solution)/shard_map/ppermute | solution.py:725
  250.8 39.9 %collective-permute-start.58 = (bf16[384,768]{1,0:T(8,128)(2,1)S(1)}, bf16[384,768]{1,0:T(8,128)(2,1)S(1)}, u32[]{:S(2)}, u32[]{:S(2)}) collective-permute-start(bf16[384,768]{1,0:T(8,128)(2,1)S(1)} %copy-done.50), channel_id=1, source_target_pairs={{0,4},{1,5},{2,6},{3,7},{4,0},{5,1},{6,2},{7,3},{8,12},{9,13},{10,... | collective-permute-start | bytes 1769480 | tf_op jit(solution)/shard_map/ppermute | solution.py:725
  251.2 39.4 %collective-permute-start.49 = (bf16[96,3072]{1,0:T(8,128)(2,1)}, bf16[96,3072]{1,0:T(8,128)(2,1)}, u32[]{:S(2)}, u32[]{:S(2)}) collective-permute-start(bf16[96,3072]{1,0:T(8,128)(2,1)} %collective-permute-done.45.rest_3_), channel_id=1, source_target_pairs={{0,4},{1,5},{2,6},{3,7},{4,0},{5,1},{6,2},{7,3},{8,12},{9,13},{10,... | collective-permute-start | bytes 1769480 | tf_op jit(solution)/shard_map/ppermute | solution.py:725
  251.3 39.4 %collective-permute-start.59 = (bf16[384,768]{1,0:T(8,128)(2,1)}, bf16[384,768]{1,0:T(8,128)(2,1)}, u32[]{:S(2)}, u32[]{:S(2)}) collective-permute-start(bf16[384,768]{1,0:T(8,128)(2,1)} %collective-permute-done.55.rest_11_), channel_id=1, source_target_pairs={{0,4},{1,5},{2,6},{3,7},{4,0},{5,1},{6,2},{7,3},{8,12},{9,13},{10,... | collective-permute-start | bytes 1769480 | tf_op jit(solution)/shard_map/ppermute | solution.py:725
  431.2 112.0 %collective-permute-start.89 = (f32[80,128]{1,0:T(8,128)}, f32[80,128]{1,0:T(8,128)}, u32[]{:S(2)}, u32[]{:S(2)}) collective-permute-start(f32[80,128]{1,0:T(8,128)} %fusion.17), channel_id=1, source_target_pairs={{0,1},{1,0},{2,3},{3,2},{4,5},{5,4},{6,7},{7,6},{8,9},{9,8},{10,11... | collective-permute-start | bytes 122888 | tf_op jit(solution)/shard_map/ppermute | solution.py:762
  563.1 18.7 %collective-permute-start.100 = (bf16[4,384,768]{2,1,0:T(8,128)(2,1)}, bf16[4,384,768]{2,1,0:T(8,128)(2,1)}, u32[]{:S(2)}, u32[]{:S(2)}) collective-permute-start(bf16[4,384,768]{2,1,0:T(8,128)(2,1)} %get-tuple-element.121), channel_id=1, source_target_pairs={{0,4},{1,5},{2,6},{3,7},{4,0},{5,1},{6,2},{7,3},{8,12},{9,13},{10,... | collective-permute-start | bytes 7077896 | tf_op jit(solution)/shard_map/ppermute | solution.py:744
  566.3 20.3 %collective-permute-start.94 = (bf16[4,384,768]{2,1,0:T(8,128)(2,1)}, bf16[4,384,768]{2,1,0:T(8,128)(2,1)S(1)}, u32[]{:S(2)}, u32[]{:S(2)}) collective-permute-start(bf16[4,384,768]{2,1,0:T(8,128)(2,1)} %get-tuple-element.119), channel_id=1, source_target_pairs={{0,4},{1,5},{2,6},{3,7},{4,0},{5,1},{6,2},{7,3},{8,12},{9,13},{10,... | collective-permute-start | bytes 7077896 | tf_op jit(solution)/shard_map/ppermute | solution.py:744
  569.2 19.3 %collective-permute-start.67 = (bf16[2,96,3072]{2,1,0:T(8,128)(2,1)S(1)}, bf16[2,96,3072]{2,1,0:T(8,128)(2,1)}, u32[]{:S(2)}, u32[]{:S(2)}) collective-permute-start(bf16[2,96,3072]{2,1,0:T(8,128)(2,1)S(1)} %slice.454), channel_id=1, source_target_pairs={{0,16},{1,17},{2,18},{3,19},{4,12},{5,13},{6,14},{7,15},{8,24},{9,... | collective-permute-start | bytes 3538952 | tf_op jit(solution)/shard_map/ppermute | solution.py:748
  573.4 24.8 %collective-permute-start.61 = (bf16[2,96,3072]{2,1,0:T(8,128)(2,1)S(1)}, bf16[2,96,3072]{2,1,0:T(8,128)(2,1)}, u32[]{:S(2)}, u32[]{:S(2)}) collective-permute-start(bf16[2,96,3072]{2,1,0:T(8,128)(2,1)S(1)} %slice.455), channel_id=1, source_target_pairs={{0,16},{1,17},{2,18},{3,19},{4,12},{5,13},{6,14},{7,15},{8,24},{9,... | collective-permute-start | bytes 3538952 | tf_op jit(solution)/shard_map/ppermute | solution.py:748
  577.6 39.6 %collective-permute-start.79 = (bf16[2,96,3072]{2,1,0:T(8,128)(2,1)S(1)}, bf16[2,96,3072]{2,1,0:T(8,128)(2,1)}, u32[]{:S(2)}, u32[]{:S(2)}) collective-permute-start(bf16[2,96,3072]{2,1,0:T(8,128)(2,1)S(1)} %slice.452), channel_id=1, source_target_pairs={{0,16},{1,17},{2,18},{3,19},{4,12},{5,13},{6,14},{7,15},{8,24},{9,... | collective-permute-start | bytes 3538952 | tf_op jit(solution)/shard_map/ppermute | solution.py:748
  581.8 54.3 %collective-permute-start.73 = (bf16[2,96,3072]{2,1,0:T(8,128)(2,1)S(1)}, bf16[2,96,3072]{2,1,0:T(8,128)(2,1)}, u32[]{:S(2)}, u32[]{:S(2)}) collective-permute-start(bf16[2,96,3072]{2,1,0:T(8,128)(2,1)S(1)} %slice.453), channel_id=1, source_target_pairs={{0,16},{1,17},{2,18},{3,19},{4,12},{5,13},{6,14},{7,15},{8,24},{9,... | collective-permute-start | bytes 3538952 | tf_op jit(solution)/shard_map/ppermute | solution.py:748
  586.6 68.5 %collective-permute-start.101 = (bf16[2,384,768]{2,1,0:T(8,128)(2,1)}, bf16[2,384,768]{2,1,0:T(8,128)(2,1)}, u32[]{:S(2)}, u32[]{:S(2)}) collective-permute-start(bf16[2,384,768]{2,1,0:T(8,128)(2,1)} %slice.450), channel_id=1, source_target_pairs={{0,16},{1,17},{2,18},{3,19},{4,12},{5,13},{6,14},{7,15},{8,24},{9,... | collective-permute-start | bytes 3538952 | tf_op jit(solution)/shard_map/ppermute | solution.py:748
  588.5 85.4 %collective-permute-start.95 = (bf16[2,384,768]{2,1,0:T(8,128)(2,1)S(1)}, bf16[2,384,768]{2,1,0:T(8,128)(2,1)S(1)}, u32[]{:S(2)}, u32[]{:S(2)}) collective-permute-start(bf16[2,384,768]{2,1,0:T(8,128)(2,1)S(1)} %slice.451), channel_id=1, source_target_pairs={{0,16},{1,17},{2,18},{3,19},{4,12},{5,13},{6,14},{7,15},{8,24},{9,... | collective-permute-start | bytes 3538952 | tf_op jit(solution)/shard_map/ppermute | solution.py:748
  598.2 77.6 %collective-permute-start.68 = (bf16[1,96,3072]{2,1,0:T(8,128)(2,1)S(1)}, bf16[1,96,3072]{2,1,0:T(8,128)(2,1)S(1)}, u32[]{:S(2)}, u32[]{:S(2)}) collective-permute-start(bf16[1,96,3072]{2,1,0:T(8,128)(2,1)S(1)} %slice.460), channel_id=1, source_target_pairs={{0,8},{1,9},{2,10},{3,11},{4,20},{5,21},{6,22},{7,23},{8,0},{9,1},... | collective-permute-start | bytes 1769480 | tf_op jit(solution)/shard_map/ppermute | solution.py:748
  617.1 59.4 %collective-permute-start.62 = (bf16[1,96,3072]{2,1,0:T(8,128)(2,1)S(1)}, bf16[1,96,3072]{2,1,0:T(8,128)(2,1)S(1)}, u32[]{:S(2)}, u32[]{:S(2)}) collective-permute-start(bf16[1,96,3072]{2,1,0:T(8,128)(2,1)S(1)} %slice.461), channel_id=1, source_target_pairs={{0,8},{1,9},{2,10},{3,11},{4,20},{5,21},{6,22},{7,23},{8,0},{9,1},... | collective-permute-start | bytes 1769480 | tf_op jit(solution)/shard_map/ppermute | solution.py:748
  636.1 43.3 %collective-permute-start.80 = (bf16[1,96,3072]{2,1,0:T(8,128)(2,1)S(1)}, bf16[1,96,3072]{2,1,0:T(8,128)(2,1)S(1)}, u32[]{:S(2)}, u32[]{:S(2)}) collective-permute-start(bf16[1,96,3072]{2,1,0:T(8,128)(2,1)S(1)} %slice.458), channel_id=1, source_target_pairs={{0,8},{1,9},{2,10},{3,11},{4,20},{5,21},{6,22},{7,23},{8,0},{9,1},... | collective-permute-start | bytes 1769480 | tf_op jit(solution)/shard_map/ppermute | solution.py:748
  655.1 26.7 %collective-permute-start.74 = (bf16[1,96,3072]{2,1,0:T(8,128)(2,1)S(1)}, bf16[1,96,3072]{2,1,0:T(8,128)(2,1)S(1)}, u32[]{:S(2)}, u32[]{:S(2)}) collective-permute-start(bf16[1,96,3072]{2,1,0:T(8,128)(2,1)S(1)} %slice.459), channel_id=1, source_target_pairs={{0,8},{1,9},{2,10},{3,11},{4,20},{5,21},{6,22},{7,23},{8,0},{9,1},... | collective-permute-start | bytes 1769480 | tf_op jit(solution)/shard_map/ppermute | solution.py:748
  679.4 19.0 %collective-permute-start.70 = (bf16[24,3072]{1,0:T(8,128)(2,1)S(1)}, bf16[24,3072]{1,0:T(8,128)(2,1)S(1)}, u32[]{:S(2)}, u32[]{:S(2)}) collective-permute-start(bf16[24,3072]{1,0:T(8,128)(2,1)S(1)} %get-tuple-element.191), channel_id=1, source_target_pairs={{0,2},{1,3},{2,0},{3,1},{4,6},{5,7},{6,4},{7,5},{8,10},{9,11},{10,... | collective-permute-start | bytes 442376 | tf_op jit(solution)/shard_map/ppermute | solution.py:756
  681.7 20.0 %collective-permute-start.69 = (bf16[24,3072]{1,0:T(8,128)(2,1)S(1)}, bf16[24,3072]{1,0:T(8,128)(2,1)S(1)}, u32[]{:S(2)}, u32[]{:S(2)}) collective-permute-start(bf16[24,3072]{1,0:T(8,128)(2,1)S(1)} %get-tuple-element.189), channel_id=1, source_target_pairs={{0,1},{1,0},{2,3},{3,2},{4,5},{5,4},{6,7},{7,6},{8,9},{9,8},{10,11... | collective-permute-start | bytes 442376 | tf_op jit(solution)/shard_map/ppermute | solution.py:756
  683.8 18.0 %collective-permute-start.65 = (bf16[24,3072]{1,0:T(8,128)(2,1)S(1)}, bf16[24,3072]{1,0:T(8,128)(2,1)S(1)}, u32[]{:S(2)}, u32[]{:S(2)}) collective-permute-start(bf16[24,3072]{1,0:T(8,128)(2,1)S(1)} %get-tuple-element.187), channel_id=1, source_target_pairs={{0,3},{1,2},{2,1},{3,0},{4,7},{5,6},{6,5},{7,4},{8,11},{9,10},{10,... | collective-permute-start | bytes 442376 | tf_op jit(solution)/shard_map/ppermute | solution.py:756
  690.1 21.9 %collective-permute-start.64 = (bf16[24,3072]{1,0:T(8,128)(2,1)S(1)}, bf16[24,3072]{1,0:T(8,128)(2,1)S(1)}, u32[]{:S(2)}, u32[]{:S(2)}) collective-permute-start(bf16[24,3072]{1,0:T(8,128)(2,1)S(1)} %get-tuple-element.188), channel_id=1, source_target_pairs={{0,2},{1,3},{2,0},{3,1},{4,6},{5,7},{6,4},{7,5},{8,10},{9,11},{10,... | collective-permute-start | bytes 442376 | tf_op jit(solution)/shard_map/ppermute | solution.py:756
  692.8 21.6 %collective-permute-start.63 = (bf16[24,3072]{1,0:T(8,128)(2,1)S(1)}, bf16[24,3072]{1,0:T(8,128)(2,1)S(1)}, u32[]{:S(2)}, u32[]{:S(2)}) collective-permute-start(bf16[24,3072]{1,0:T(8,128)(2,1)S(1)} %get-tuple-element.186), channel_id=1, source_target_pairs={{0,1},{1,0},{2,3},{3,2},{4,5},{5,4},{6,7},{7,6},{8,9},{9,8},{10,11... | collective-permute-start | bytes 442376 | tf_op jit(solution)/shard_map/ppermute | solution.py:756
  701.7 23.0 %collective-permute-start.82 = (bf16[24,3072]{1,0:T(8,128)(2,1)S(1)}, bf16[24,3072]{1,0:T(8,128)(2,1)S(1)}, u32[]{:S(2)}, u32[]{:S(2)}) collective-permute-start(bf16[24,3072]{1,0:T(8,128)(2,1)S(1)} %get-tuple-element.185), channel_id=1, source_target_pairs={{0,2},{1,3},{2,0},{3,1},{4,6},{5,7},{6,4},{7,5},{8,10},{9,11},{10,... | collective-permute-start | bytes 442376 | tf_op jit(solution)/shard_map/ppermute | solution.py:756
  701.8 25.2 %collective-permute-start.81 = (bf16[24,3072]{1,0:T(8,128)(2,1)S(1)}, bf16[24,3072]{1,0:T(8,128)(2,1)S(1)}, u32[]{:S(2)}, u32[]{:S(2)}) collective-permute-start(bf16[24,3072]{1,0:T(8,128)(2,1)S(1)} %get-tuple-element.183), channel_id=1, source_target_pairs={{0,1},{1,0},{2,3},{3,2},{4,5},{5,4},{6,7},{7,6},{8,9},{9,8},{10,11... | collective-permute-start | bytes 442376 | tf_op jit(solution)/shard_map/ppermute | solution.py:756
  714.3 23.0 %collective-permute-start.76 = (bf16[24,3072]{1,0:T(8,128)(2,1)S(1)}, bf16[24,3072]{1,0:T(8,128)(2,1)S(1)}, u32[]{:S(2)}, u32[]{:S(2)}) collective-permute-start(bf16[24,3072]{1,0:T(8,128)(2,1)S(1)} %get-tuple-element.182), channel_id=1, source_target_pairs={{0,2},{1,3},{2,0},{3,1},{4,6},{5,7},{6,4},{7,5},{8,10},{9,11},{10,... | collective-permute-start | bytes 442376 | tf_op jit(solution)/shard_map/ppermute | solution.py:756
  714.5 25.2 %collective-permute-start.75 = (bf16[24,3072]{1,0:T(8,128)(2,1)S(1)}, bf16[24,3072]{1,0:T(8,128)(2,1)S(1)}, u32[]{:S(2)}, u32[]{:S(2)}) collective-permute-start(bf16[24,3072]{1,0:T(8,128)(2,1)S(1)} %get-tuple-element.180), channel_id=1, source_target_pairs={{0,1},{1,0},{2,3},{3,2},{4,5},{5,4},{6,7},{7,6},{8,9},{9,8},{10,11... | collective-permute-start | bytes 442376 | tf_op jit(solution)/shard_map/ppermute | solution.py:756
  727.0 23.0 %collective-permute-start.104 = (bf16[96,768]{1,0:T(8,128)(2,1)S(1)}, bf16[96,768]{1,0:T(8,128)(2,1)S(1)}, u32[]{:S(2)}, u32[]{:S(2)}) collective-permute-start(bf16[96,768]{1,0:T(8,128)(2,1)S(1)} %get-tuple-element.179), channel_id=1, source_target_pairs={{0,2},{1,3},{2,0},{3,1},{4,6},{5,7},{6,4},{7,5},{8,10},{9,11},{10,... | collective-permute-start | bytes 442376 | tf_op jit(solution)/shard_map/ppermute | solution.py:756
  727.9 22.1 %collective-permute-start.103 = (bf16[96,768]{1,0:T(8,128)(2,1)S(1)}, bf16[96,768]{1,0:T(8,128)(2,1)S(1)}, u32[]{:S(2)}, u32[]{:S(2)}) collective-permute-start(bf16[96,768]{1,0:T(8,128)(2,1)S(1)} %get-tuple-element.177), channel_id=1, source_target_pairs={{0,1},{1,0},{2,3},{3,2},{4,5},{5,4},{6,7},{7,6},{8,9},{9,8},{10,11... | collective-permute-start | bytes 442376 | tf_op jit(solution)/shard_map/ppermute | solution.py:756
  (98 other events, 1731.1 us)

commit v2 on v1

v2 whole, which is shorter than its diff:
```python
import functools
import jax
import jax.numpy as jnp
import numpy as np
from jax import lax
from jax.experimental import pallas as pl
from jax.experimental.pallas import tpu as pltpu
from jax.sharding import PartitionSpec as P

D = 768
HEADS = 12
HD = 64
FF = 3072
LM = 64
KSIZE = 33
RADIUS = KSIZE // 2
NS_ITERS = 6
T = 1024
SEG = T // LM
SCALE = HD ** -0.5
EPS = 1e-05
CONV_N = 256
CONV_K = 512
CONV_BLOCKS = T // CONV_N
LEAD = 128
f32 = jnp.float32
bf16 = jnp.bfloat16
AXES = ("wide", "narrow")
NN = (((1,), (0,)), ((), ()))
NT = (((1,), (1,)), ((), ()))
TN = (((0,), (0,)), ((), ()))
VMEM_LIMIT = 60 * 1024 * 1024


def dot(a, b, dims):
    return lax.dot_general(a, b, dims, preferred_element_type=f32)


def split(a):
    high = a.astype(bf16)
    return high, (a - high.astype(f32)).astype(bf16)


def dot3(a, b, dims):
    return dot(a[0], b[0], dims) + (dot(a[0], b[1], dims) + dot(a[1], b[0], dims))


def rows(start, size):
    if isinstance(start, int):
        return pl.ds(start, size)
    return pl.ds(pl.multiple_of(start, size), size)


def segment_mean():
    token = lax.broadcasted_iota(jnp.int32, (T, LM), 0)
    seg = lax.broadcasted_iota(jnp.int32, (T, LM), 1)
    return jnp.where(token // SEG == seg, 1.0 / SEG, 0.0).astype(bf16)


def segment_spread():
    token = lax.broadcasted_iota(jnp.int32, (LM, T), 1)
    seg = lax.broadcasted_iota(jnp.int32, (LM, T), 0)
    return jnp.where(token // SEG == seg, 1.0, 0.0).astype(bf16)


def eye(value):
    i = lax.broadcasted_iota(jnp.int32, (LM, LM), 0)
    j = lax.broadcasted_iota(jnp.int32, (LM, LM), 1)
    return jnp.where(i == j, value, 0.0).astype(f32)


def toeplitz(row):
    full = jnp.broadcast_to(row, (CONV_N, CONV_K))
    return pltpu.roll(full, 0, 1, stride=1, stride_axis=0).astype(bf16)


def windows(ref, base):
    return jnp.concatenate(
        [ref[rows(base, HD), CONV_N * b : CONV_N * b + CONV_K] for b in range(CONV_BLOCKS)], axis=0
    )


def stack_blocks(value):
    return jnp.concatenate(
        [value[:, CONV_N * b : CONV_N * (b + 1)] for b in range(CONV_BLOCKS)], axis=0
    )


def unstack_blocks(value):
    return jnp.concatenate(
        [value[HD * b : HD * (b + 1), :] for b in range(CONV_BLOCKS)], axis=1
    )


def norm_forward(r_ref, xhat_ref, rstd_ref, width=128):
    for c in range(0, T, width):
        r = r_ref[:, c : c + width]
        center = r - jnp.mean(r, axis=0, keepdims=True)
        rstd = lax.rsqrt(jnp.mean(center * center, axis=0, keepdims=True) + EPS)
        xhat_ref[:, c : c + width] = center * rstd
        rstd_ref[:, c : c + width] = jnp.broadcast_to(rstd, (8, width))


def vm():
    return pl.BlockSpec(memory_space=pltpu.VMEM)


def anywhere(n):
    return [pl.BlockSpec(memory_space=pl.ANY)] * n


def whole(*s):
    return pl.BlockSpec(s, lambda *_: (0,) * len(s))


def sd(*s, t=f32):
    return jax.ShapeDtypeStruct(s, t)


def loader(pieces, dst, sem, columns=None):
    r = pieces[0].shape[0]
    order = Order(len(pieces))
    out = []
    for i, piece in enumerate(pieces):
        src = piece if columns is None else piece.at[:, pl.ds(*columns)]
        at = rows(order.target(i) * r, r)
        out.append(pltpu.make_async_copy(src, dst.at[at, :], sem.at[i]))
    return out


def call(kernel, name, out_shape, in_specs, out_specs, scratch, args, lanes, flops, size, grid=None, trans=0):
    identity, lanes = lanes
    ins, outs = len(args), len(out_shape)
    lane_args = [a for lane in lanes for a in lane.args]
    lane_outs = [o for lane in lanes for o in lane.outs]
    lane_scratch = [o for lane in lanes for o in lane.scratch]

    def run(*refs):
        refs = list(refs)

        def take(n):
            got = refs[:n]
            del refs[:n]
            return got

        own = take(ins)
        lane_in = [take(len(lane.args)) for lane in lanes]
        own += take(outs)
        lane_out = [take(len(lane.outs)) for lane in lanes]
        own += take(len(scratch))
        for lane, a, o in zip(lanes, lane_in, lane_out):
            lane.bind(a, o, take(len(lane.scratch)))

        def hook(i):
            if lanes and i == 0:
                near = Near()
                names = sorted({p for lane in lanes for p in lane.partners})
                barrier = pltpu.get_barrier_semaphore()
                for p in names:
                    pl.semaphore_signal(barrier, inc=1, device_id=near.at(p), device_id_type=pl.DeviceIdType.MESH)
                pl.semaphore_wait(barrier, len(names))
            for lane in lanes:
                lane.turn(i)

        kernel(*own, hook=hook)

    params = {"collective_id": identity, "has_side_effects": True} if lanes else {}
    got = pl.pallas_call(
        run,
        out_shape=list(out_shape) + [o for o, _ in lane_outs],
        in_specs=list(in_specs) + [spec for lane in lanes for spec in lane.specs],
        out_specs=list(out_specs) + [spec for _, spec in lane_outs],
        scratch_shapes=list(scratch) + lane_scratch,
        **({} if grid is None else {"grid": grid}),
        compiler_params=pltpu.CompilerParams(vmem_limit_bytes=VMEM_LIMIT, **params),
        cost_estimate=pl.CostEstimate(flops=flops, bytes_accessed=size, transcendentals=trans),
        name=name,
    )(*args, *lane_args)
    own, rest = list(got[:outs]), list(got[outs:])
    for lane in lanes:
        n = len(lane.outs)
        lane.done(rest[:n])
        rest = rest[n:]
    return own


class Near:
    def __init__(self):
        self.w, self.z = lax.axis_index("wide"), lax.axis_index("narrow")

    def over(self, k):
        z = self.z
        if k == 1:
            return z + 1 - 2 * (z % 2)
        if k == 2:
            return z + 2 - 4 * (z // 2)
        return 3 - z

    def at(self, name):
        w, core = self.w, self.w % 2
        if name[0] == "z":
            return (w, self.over(int(name[1])))
        if name == "core":
            return (w + 1 - 2 * core, self.z)
        step = {"a": 2 + 2 * core, "b": 4 - 2 * core, "x": 2, "y": 4}[name]
        return (w + step - 2 * step * ((w // step) % 2), self.z)


def remote(src, dst, send, recv, name):
    return pltpu.make_async_remote_copy(
        src_ref=src, dst_ref=dst, send_sem=send, recv_sem=recv, device_id=Near().at(name),
        device_id_type=pl.DeviceIdType.MESH)


DMA = pltpu.SemaphoreType.DMA
ANY = pl.BlockSpec(memory_space=pl.ANY)


class Move:
    def __init__(self, source, name, start, wait):
        self.chained = isinstance(source, Move)
        self.source, self.name, self.start, self.wait = source, name, start, wait
        self.shape = source.shape
        self.args = [] if self.chained else [source]
        self.specs = [ANY] * len(self.args)
        self.outs = [(sd(*self.shape, t=bf16), ANY)]
        self.scratch = [DMA((2,))]
        self.partners = [name]

    def bind(self, args, outs, scratch):
        self.src = self.source.dst if self.chained else args[0]
        self.dst, self.sem = outs[0], scratch[0]

    def copy(self):
        return remote(self.src, self.dst, self.sem.at[0], self.sem.at[1], self.name)

    def turn(self, i):
        if i == self.wait:
            self.copy().wait()
        if i == self.start:
            self.copy().start()

    def done(self, got):
        self.value = got[0]


class Spread:
    def __init__(self, shard, start, wait):
        self.start, self.wait = start, wait
        self.args, self.specs = [shard], [ANY]
        self.outs = [(sd(4, *shard.shape, t=bf16), ANY)]
        self.scratch = [DMA((7,))]
        self.partners = ["z1", "z2", "z3"]

    def bind(self, args, outs, scratch):
        self.src, self.dst, self.sem = args[0], outs[0], scratch[0]

    def copies(self):
        z = lax.axis_index("narrow")
        out = [pltpu.make_async_copy(self.src, self.dst.at[z], self.sem.at[6])]
        for k in (1, 2, 3):
            out.append(remote(self.src, self.dst.at[z], self.sem.at[2 * k - 2], self.sem.at[2 * k - 1], f"z{k}"))
        return out

    def turn(self, i):
        if i == self.wait:
            for copy in self.copies():
                copy.wait()
        if i == self.start:
            for copy in self.copies():
                copy.start()

    def done(self, got):
        value = got[0]
        self.value = value.reshape(-1, value.shape[-1])


def strips(columns):
    width = 384 if columns % 384 == 0 else columns
    return [slice(c, c + width) for c in range(0, columns, width)]


class ReduceFirst:
    def __init__(self, keep, send, turns, chained=False, columns=None):
        self.turns, self.chained, self.at = turns, chained, columns
        rows4 = D // 2 if columns is not None else send.shape[0]
        self.columns = columns.stop - columns.start if columns is not None else send.shape[1]
        self.r = r = rows4 // 4
        self.partners = ["core", "b"]
        shape = (r, self.columns)
        self.args = [] if columns is not None else [keep, send]
        self.specs = [ANY] * len(self.args)
        self.outs = [] if chained else [(sd(*shape, t=bf16), whole(*shape)), (sd(*shape), whole(*shape))]
        self.scratch = [pltpu.VMEM((2 * r, self.columns), bf16), pltpu.VMEM((2 * r, self.columns), bf16),
                        pltpu.VMEM((4 * r, self.columns), bf16), DMA((5,))]
        if chained:
            self.scratch += [pltpu.VMEM(shape, bf16), pltpu.VMEM(shape, f32)]
        if columns is None:
            self.scratch += [pltpu.VMEM((4 * r, self.columns), bf16)]

    def bind(self, args, outs, scratch):
        self.away1, self.got1, self.got0, self.sem = scratch[:4]
        rest = scratch[4:]
        if self.chained:
            self.away2, self.own2 = rest[:2]
            rest = rest[2:]
        else:
            self.away2, self.own2 = outs
        if self.at is None:
            self.keep_from, self.send = args
            self.keep = rest[0]

    def use(self, keep, send):
        self.keep, self.send = keep.at[:, self.at], send.at[:, self.at]

    def load(self):
        return pltpu.make_async_copy(self.keep_from, self.keep, self.sem.at[4])

    def first(self):
        return remote(self.send, self.got0, self.sem.at[0], self.sem.at[1], "core")

    def second(self):
        return remote(self.away1, self.got1, self.sem.at[2], self.sem.at[3], "b")

    def turn(self, i):
        r = self.r
        if i == self.turns[0]:
            self.first().start()
            if self.at is None:
                self.load().start()
        if i == self.turns[1]:
            if self.at is None:
                self.load().wait()
            self.first().wait()
            for at in strips(self.columns):
                self.away1[:, at] = self.keep[2 * r :, at] + self.got0[2 * r :, at]
            self.second().start()
        if i == self.turns[2]:
            self.second().wait()
            for at in strips(self.columns):
                for k, out in ((0, self.own2), (1, self.away2)):
                    block = slice(k * r, (k + 1) * r)
                    value = self.keep[block, at].astype(f32) + self.got0[block, at].astype(f32)
                    out[:, at] = (value + self.got1[block, at].astype(f32)).astype(out.dtype)

    def done(self, got):
        self.value = got


class ReduceLast:
    def __init__(self, away, own, turns, inside=None):
        self.turns, self.inside = turns, inside
        r, columns = (inside.r, inside.columns) if inside else away.shape
        size = r // 4
        self.r, self.columns, self.size = r, columns, size
        self.partners = ["a", "z1", "z2", "z3"]
        self.args = [] if inside else [away, own]
        self.specs = [] if inside else [ANY, whole(r, columns)]
        self.outs = [(sd(size, columns), whole(size, columns))]
        self.scratch = [pltpu.VMEM((r, columns), bf16), pltpu.VMEM((4, size, columns), bf16),
                        pltpu.VMEM((4, size, columns), bf16), pltpu.VMEM((4, size, columns), f32), DMA((8,))]

    def bind(self, args, outs, scratch):
        self.got2, self.parts, self.got3, self.sums, self.sem = scratch
        self.out = outs[0]
        self.away, self.own = (self.inside.away2, self.inside.own2) if self.inside else args

    def third(self):
        return remote(self.away, self.got2, self.sem.at[0], self.sem.at[1], "a")

    def last(self):
        near = Near()
        return [
            remote(self.parts.at[near.over(k)], self.got3.at[near.z], self.sem.at[2 * k], self.sem.at[2 * k + 1], f"z{k}")
            for k in (1, 2, 3)]

    def turn(self, i):
        if i == self.turns[0]:
            self.third().start()
        if i == self.turns[1]:
            self.third().wait()
            for at in strips(self.columns):
                for k in range(4):
                    block = slice(k * self.size, (k + 1) * self.size)
                    self.sums[k, :, at] = self.own[block, at]
                whole_block = self.got2[:, at].astype(f32)
                for k in range(4):
                    value = self.sums[k, :, at] + whole_block[k * self.size : (k + 1) * self.size]
                    self.sums[k, :, at] = value
                    self.parts[k, :, at] = value.astype(bf16)
            for copy in self.last():
                copy.start()
        if i == self.turns[2]:
            for copy in self.last():
                copy.wait()
            near = Near()
            for at in strips(self.columns):
                value = self.sums[near.z, :, at]
                for k in (1, 2, 3):
                    value = value + self.got3[near.over(k), :, at].astype(f32)
                self.out[:, at] = value

    def done(self, got):
        self.value = got[0]


SMALL = 24


class Total:
    def __init__(self, sums, taps, turns):
        self.turns = turns
        self.args = [sums, *taps]
        self.specs = [whole(*a.shape) for a in self.args]
        shape = (SMALL, D + 128)
        self.outs = [(sd(*shape), whole(*shape))]
        self.scratch = [pltpu.VMEM((5, *shape), f32), pltpu.VMEM((5, *shape), f32), DMA((10,))]
        self.partners = ["core", "x", "y", "z1", "z2"]

    def bind(self, args, outs, scratch):
        self.small, self.out = args, outs[0]
        self.held, self.got, self.sem = scratch

    def copy(self, s):
        return remote(self.held.at[s], self.got.at[s], self.sem.at[2 * s], self.sem.at[2 * s + 1], self.partners[s])

    def turn(self, i):
        for s in range(6):
            if i == self.turns[s]:
                if s:
                    self.copy(s - 1).wait()
                    value = self.held[s - 1] + self.got[s - 1]
                    if s < 5:
                        self.held[s] = value
                    else:
                        self.out[...] = value
                else:
                    self.held[0, :, 0:D] = self.small[0][...].T[0:SMALL, :]
                    self.held[0, 0:HEADS, D:] = self.small[1][...]
                    self.held[0, HEADS : 2 * HEADS, D:] = self.small[2][...]
                if s < 5:
                    self.copy(s).start()

    def done(self, got):
        self.value = got[0]


CHUNK = 768
STEPS = FF // CHUNK
SUB = 256


def flip(t, stride):
    return t + stride - 2 * stride * ((t // stride) % 2)


class Order:
    def __init__(self, n):
        self.exact = n == 8
        self.core = 0
        if self.exact:
            self.w = lax.axis_index("wide")
            self.core = self.w % 2

    def target(self, i):
        if not self.exact:
            return i
        other, code = i // 4, i % 4
        t = self.w + other * (1 - 2 * self.core)
        core = t % 2
        if code % 2:
            t = flip(t, 2 + 2 * core)
        if code // 2:
            t = flip(t, 4 - 2 * core)
        return t

    def slot(self, j, other):
        if not self.exact:
            return j
        plane = self.w // 2
        core = self.core if other == 0 else 1 - self.core
        dx, dy = (j + plane) % 2, (j // 2 + plane // 2) % 2
        return dx * (1 + core) + dy * (2 - core)


def exchange(lanes, turns):
    def kernel(hook):
        for i in range(turns):
            hook(i)

    call(kernel, "exchange", [], [], [], [], (), lanes, 0, 10_000_000)


def project_kernel(n, p, x_ref, *rest, hook):
    if p:
        par_ref, *rest = rest
    pieces, rest = rest[:n], rest[n:]
    if p:
        xl_ref, mix_ref, lm_ref, w_ref, sem = rest
        loads = []
    else:
        xl_ref, mix_ref, lm_ref, par_ref, w_ref, sem, low_ref, low_sem = rest
        loads = loader(pieces, low_ref, low_sem, (4 * D, 128))
    loads += loader(pieces, w_ref, sem, (0, 3 * D))
    for copy in loads:
        copy.start()
    xl_ref[...] = x_ref[...].astype(bf16)
    hook(0)
    for copy in loads:
        copy.wait()
    if not p:
        par_ref[...] = low_ref[...].astype(f32)
    for part, column in ((0, p), (1, None), (2, p + 1)):

        def mix_step(i, _):
            at = rows(part * D + i * 256, 256)
            got = dot(w_ref[:, at], xl_ref[...], TN)
            if column is not None:
                got = got + par_ref[rows(i * 256, 256), column : column + 1]
            mix_ref[at, :] = got.astype(bf16)
            return 0

        lax.fori_loop(0, 3, mix_step, 0)
        hook(part + 1)
    lm_ref[...] = dot(mix_ref[0 : 2 * D, :], segment_mean(), NN).astype(bf16)
    hook(4)


def project(x, pieces, par, layer, lanes=(None, ())):
    n = len(pieces)
    first = layer == 0
    got = call(
        functools.partial(project_kernel, n, 8 * layer), "project",
        [sd(D, T, t=bf16), sd(3 * D, T, t=bf16), sd(2 * D, LM, t=bf16)] + [sd(D, 128)] * first,
        [vm()] + [vm()] * (not first) + anywhere(n), [vm()] * (3 + first),
        [pltpu.VMEM((D, 3 * D), bf16), DMA((n,))] + [pltpu.VMEM((D, 128), bf16), DMA((n,))] * first,
        (x, *([] if first else [par]), *pieces), lanes, 3_800_000_000, 14_000_000)
    return got if first else [*got, par]


def attend_kernel(n, p, x_ref, mix_ref, lm_ref, par_ref, conv_ref, *rest, hook):
    pieces = rest[:n]
    (ctx_ref, f_ref, b_ref, a_ref, ns_ref, small_ref, xhat_ref, rstd_ref,
     w_ref, vpad_ref, z_ref, sem) = rest[n:]
    loads = loader(pieces, w_ref, sem, (3 * D, D))
    for copy in loads:
        copy.start()
    vpad_ref[:, 0:LEAD] = jnp.zeros((D, LEAD), bf16)
    vpad_ref[:, LEAD + T :] = jnp.zeros((D, LEAD), bf16)
    vpad_ref[:, LEAD : LEAD + T] = mix_ref[2 * D :, :]
    hook(0)
    for h in range(HEADS):
        ql = lm_ref[h * HD : (h + 1) * HD, :]
        kl = lm_ref[D + h * HD : D + (h + 1) * HD, :]
        s = dot(ql, kl, TN) * SCALE
        e = jnp.exp(s - jnp.max(s, axis=1, keepdims=True))
        a = e / jnp.sum(e, axis=1, keepdims=True)
        a_ref[h] = a
        z_ref[h] = a.T / jnp.sum(a * a)

    def ns_step(k, _):
        ps, rs = [], []
        for h in range(HEADS):
            z = z_ref[h]
            ns_ref[k, 0, h] = z
            p = dot3(split(a_ref[h]), split(z), NN)
            ns_ref[k, 1, h] = p
            ps.append(split(p))
            rs.append(split(eye(7.0) - p))
        for h in range(HEADS):
            r2 = eye(15.0) - dot3(ps[h], rs[h], NN)
            ns_ref[k, 2, h] = r2
            rs[h] = split(r2)
        for h in range(HEADS):
            r3 = eye(13.0) - dot3(ps[h], rs[h], NN)
            ns_ref[k, 3, h] = r3
            rs[h] = split(r3)
        for h in range(HEADS):
            z_ref[h] = 0.25 * dot3(split(z_ref[h]), rs[h], NN)
        return 0

    lax.fori_loop(0, NS_ITERS, ns_step, 0)
    hook(1)

    def head_step(h, _):
        base = h * HD
        q = mix_ref[rows(base, HD), :]
        k = mix_ref[rows(D + base, HD), :]
        v = mix_ref[rows(2 * D + base, HD), :]
        ql = lm_ref[rows(base, HD), :]
        kl = lm_ref[rows(D + base, HD), :]
        s = dot(kl, q, TN) * SCALE
        e = jnp.exp(s - jnp.max(s, axis=0, keepdims=True))
        f = (e / jnp.sum(e, axis=0, keepdims=True)).astype(bf16)
        f_ref[rows(base, HD), :] = f
        s = dot(ql, k, TN) * SCALE
        e = jnp.exp(s - jnp.max(s, axis=1, keepdims=True))
        b = (e / jnp.sum(e, axis=1, keepdims=True)).astype(bf16)
        b_ref[rows(base, HD), :] = b
        bv = dot(b, v, NT)
        z = z_ref[h]
        w = dot3(split(z), split(bv), NN)
        small_ref[0, h] = z
        small_ref[1, h] = bv
        small_ref[2, h] = w
        attended = dot(w.astype(bf16), f, TN)
        conv = dot(windows(vpad_ref, base), toeplitz(conv_ref[h, 0:1]), NT)
        ctx_ref[rows(base, HD), :] = (attended + unstack_blocks(conv)).astype(bf16)
        return 0

    lax.fori_loop(0, HEADS // 2, head_step, 0)
    hook(2)
    lax.fori_loop(HEADS // 2, HEADS, head_step, 0)
    hook(3)
    for copy in loads:
        copy.wait()

    def out_step(i, _):
        base = i * 256
        got = dot(w_ref[:, rows(base, 256)], ctx_ref[...], TN)
        xhat_ref[rows(base, 256), :] = got + par_ref[rows(base, 256), p + 2 : p + 3] + x_ref[rows(base, 256), :]
        return 0

    lax.fori_loop(0, 3, out_step, 0)
    norm_forward(xhat_ref, xhat_ref, rstd_ref)
    hook(4)


def attend(x, mix, lm, pieces, par, conv, layer, lanes=(None, ())):
    n = len(pieces)
    return call(
        functools.partial(attend_kernel, n, 8 * layer), "attend",
        [
            sd(D, T, t=bf16), sd(D, T, t=bf16), sd(D, T, t=bf16), sd(HEADS, LM, LM),
            sd(NS_ITERS, 4, HEADS, LM, LM), sd(3, HEADS, LM, LM), sd(D, T), sd(8, T),
        ],
        [vm()] * 5 + anywhere(n), [vm()] * 8,
        [
            pltpu.VMEM((D, D), bf16), pltpu.VMEM((D, T + 2 * LEAD), bf16), pltpu.VMEM((HEADS, LM, LM), f32),
            pltpu.SemaphoreType.DMA((n,)),
        ],
        (x, mix, lm, par, conv, *pieces), lanes, 3_000_000_000, 30_000_000, trans=2_000_000)


def up_kernel(n, p, xhat_ref, par_ref, inb_ref, *rest, hook):
    pieces, (a_ref, g_ref, w_ref, hl_ref, sem) = rest[:n], rest[n:]
    j = pl.program_id(0)

    @pl.when(j == 0)
    def _():
        loads = loader(pieces, w_ref, sem)
        for copy in loads:
            copy.start()
        hook(0)
        h = xhat_ref[...] * par_ref[:, p + 6 : p + 7] + par_ref[:, p + 3 : p + 4]
        hl_ref[...] = h.astype(bf16)
        for copy in loads:
            copy.wait()

    def up_step(i, _):
        base = i * SUB
        at = j * CHUNK + base
        u = dot(w_ref[:, pl.ds(pl.multiple_of(at, SUB), SUB)], hl_ref[...], TN)
        u = u + inb_ref[rows(at, SUB), 0:1]
        cdf = 0.5 + 0.5 * lax.erf(u * (2.0 ** -0.5))
        pdf = jnp.exp(-0.5 * u * u) * ((2.0 * np.pi) ** -0.5)
        a_ref[rows(base, SUB), :] = (u * cdf).astype(bf16)
        g_ref[rows(base, SUB), :] = (cdf + u * pdf).astype(bf16)
        return 0

    lax.fori_loop(0, CHUNK // SUB, up_step, 0)
    for i in range(STEPS):

        @pl.when(j == i)
        def _():
            hook(i + 1)


def up(xhat, pieces, par, inb, layer, lanes=(None, ())):
    n = len(pieces)
    chunk = pl.BlockSpec((CHUNK, T), lambda j: (j, 0))
    return call(
        functools.partial(up_kernel, n, 8 * layer), "up",
        [sd(FF, T, t=bf16), sd(FF, T, t=bf16)],
        [whole(D, T), whole(D, 128), whole(FF, 1)] + anywhere(n), [chunk, chunk],
        [pltpu.VMEM((D, FF), bf16), pltpu.VMEM((D, T), bf16), pltpu.SemaphoreType.DMA((n,))],
        (xhat, par, inb, *pieces), lanes, 4_900_000_000, 24_000_000, (STEPS,), 6_000_000)


def down_kernel(n, p, last, xhat_ref, par_ref, a_ref, *rest, hook):
    pieces, (xhat2_ref, rstd2_ref, next_ref, w_ref, sem) = rest[:n], rest[n:]
    j = pl.program_id(0)

    @pl.when(j == 0)
    def _():
        loads = loader(pieces, w_ref, sem)
        for copy in loads:
            copy.start()
        hook(0)
        h = xhat_ref[...] * par_ref[:, p + 6 : p + 7] + par_ref[:, p + 3 : p + 4]
        xhat2_ref[...] = h + par_ref[:, p + 4 : p + 5]
        for copy in loads:
            copy.wait()

    def down_step(i, _):
        base = i * SUB
        xhat2_ref[rows(base, SUB), :] += dot(
            w_ref[rows(j * CHUNK, CHUNK), pl.ds(pl.multiple_of(base, SUB), SUB)], a_ref[...], TN)
        return 0

    lax.fori_loop(0, D // SUB, down_step, 0)

    @pl.when(j == STEPS - 1)
    def _():
        norm_forward(xhat2_ref, xhat2_ref, rstd2_ref)
        y = xhat2_ref[...] * par_ref[:, p + 7 : p + 8] + par_ref[:, p + 5 : p + 6]
        if last:
            next_ref[...] = y.T.astype(bf16)
        else:
            next_ref[...] = y
    for i in range(STEPS):

        @pl.when(j == i)
        def _():
            hook(i + 1)


def down(xhat, a, pieces, par, layer, last, lanes=(None, ())):
    n = len(pieces)
    next_shape = (T, D) if last else (D, T)
    return call(
        functools.partial(down_kernel, n, 8 * layer, last), "down",
        [sd(D, T), sd(8, T), sd(*next_shape, t=bf16 if last else f32)],
        [whole(D, T), whole(D, 128), pl.BlockSpec((CHUNK, T), lambda j: (j, 0))] + anywhere(n),
        [whole(D, T), whole(8, T), whole(*next_shape)],
        [pltpu.VMEM((FF, D), bf16), pltpu.SemaphoreType.DMA((n,))],
        (xhat, par, a, *pieces), lanes, 4_900_000_000, 24_000_000, (STEPS,))


def norm_backward(dy_ref, xhat_ref, rstd_ref, gain, out_ref, grads_ref, gain_col, shift_col, width=128):
    total_gain = jnp.zeros((D, width), f32)
    total_shift = jnp.zeros((D, width), f32)
    for c in range(0, T, width):
        dy = dy_ref[:, c : c + width]
        xhat = xhat_ref[:, c : c + width]
        total_shift = total_shift + dy
        total_gain = total_gain + dy * xhat
        dxhat = dy * gain
        m1 = jnp.mean(dxhat, axis=0, keepdims=True)
        m2 = jnp.mean(dxhat * xhat, axis=0, keepdims=True)
        out_ref[:, c : c + width] = rstd_ref[0:1, c : c + width] * (dxhat - m1 - xhat * m2)
    grads_ref[:, gain_col : gain_col + 1] = jnp.sum(total_gain, axis=1, keepdims=True)
    grads_ref[:, shift_col : shift_col + 1] = jnp.sum(total_shift, axis=1, keepdims=True)


def lane_sum(value):
    return jnp.sum(value.astype(f32), axis=1, keepdims=True)


def permute_rows(dst_ref, src_ref, order, block):
    for i in range(D // block):
        dst_ref[i * block : (i + 1) * block, :] = src_ref[
            rows(order.target(i) * block, block), :]


def hidden_kernel(n, p, first, sums_in, dy_ref, xhat_ref, rstd_ref, par_ref, a_ref, g_ref, *rest, hook):
    order = Order(n)
    pieces, (keep_ref, send_ref, du_ref, dr_ref, cols_ref, w_ref, dz_ref, inb_ref, sem) = rest[:n], rest[n:]
    j = pl.program_id(0)

    @pl.when(j == 0)
    def _():
        loads = loader(pieces, w_ref, sem)
        for copy in loads:
            copy.start()
        hook(0)
        if first:
            dr_ref[...] = dy_ref[...].astype(f32).T
            dy = dr_ref
        else:
            dy = dy_ref
        cols_ref[...] = sums_in[...]
        norm_backward(dy, xhat_ref, rstd_ref, par_ref[:, p + 7 : p + 8], dr_ref, cols_ref, p + 7, p + 5)
        dz_ref[...] = dr_ref[...].astype(bf16)
        cols_ref[:, p + 4 : p + 5] = lane_sum(dz_ref[...])
        for copy in loads:
            copy.wait()

    def du_step(i, _):
        base = i * SUB
        da = dot(w_ref[rows(j * CHUNK + base, SUB), :], dz_ref[...], NN)
        du = (da * g_ref[rows(base, SUB), :].astype(f32)).astype(bf16)
        du_ref[rows(base, SUB), :] = du
        inb_ref[rows(base, SUB), :] = lane_sum(du)
        return 0

    lax.fori_loop(0, CHUNK // SUB, du_step, 0)
    half = CHUNK // 2
    core = order.core

    def own(start):
        return a_ref[rows(start, half), :]

    keep_ref[order.slot(j, 0)] = dot(own(core * half), dz_ref[...], NT).astype(bf16)
    send_ref[order.slot(j, 1)] = dot(own((1 - core) * half), dz_ref[...], NT).astype(bf16)
    for i in range(STEPS):

        @pl.when(j == i)
        def _():
            column = 2 * 8 + p // 2 + i
            cols_ref[:, column : column + 1] = inb_ref[...]
            hook(i + 1)


def hidden(sums, dy, xhat, rstd, par, a, g, pieces, layer, first, lanes=(None, ())):
    n = len(pieces)
    chunk = pl.BlockSpec((CHUNK, T), lambda j: (j, 0))
    half = CHUNK // 2
    return call(
        functools.partial(hidden_kernel, n, 8 * layer, first), "hidden",
        [
            sd(STEPS, half, D, t=bf16), sd(STEPS, half, D, t=bf16), sd(FF, T, t=bf16), sd(D, T), sd(D, 128),
        ],
        [whole(D, 128), whole(*dy.shape), whole(D, T), whole(8, T), whole(D, 128), chunk, chunk] + anywhere(n),
        [
            whole(STEPS, half, D), whole(STEPS, half, D), chunk, whole(D, T), whole(D, 128),
        ],
        [pltpu.VMEM((FF, D), bf16), pltpu.VMEM((D, T), bf16), pltpu.VMEM((CHUNK, 1), f32), pltpu.SemaphoreType.DMA((n,))],
        (sums, dy, xhat, rstd, par, a, g, *pieces), lanes, 9_700_000_000, 40_000_000, (STEPS,))


def inner_kernel(n, p, sums_in, du_ref, dr_ref, xhat_ref, rstd_ref, par_ref, *rest, hook):
    order = Order(n)
    pieces, (keep_ref, send_ref, out_ref, cols_ref, w_ref, hl_ref, acc_ref, sem) = rest[:n], rest[n:]
    j = pl.program_id(0)

    @pl.when(j == 0)
    def _():
        loads = loader(pieces, w_ref, sem)
        for copy in loads:
            copy.start()
        hook(0)
        block = D // 8
        for i in range(8):
            at = rows(order.target(i) * block, block)
            hl_ref[i * block : (i + 1) * block, :] = (
                xhat_ref[at, :] * par_ref[at, p + 6 : p + 7] + par_ref[at, p + 3 : p + 4]).astype(bf16)
        acc_ref[...] = dr_ref[...]
        for copy in loads:
            copy.wait()

    for i, ref in enumerate((keep_ref, send_ref)):
        ref[...] = dot(hl_ref[i * (D // 2) : (i + 1) * (D // 2), :], du_ref[...], NT).astype(bf16)

    def dh_step(i, _):
        acc_ref[rows(i * SUB, SUB), :] += dot(
            w_ref[rows(i * SUB, SUB), rows(j * CHUNK, CHUNK)], du_ref[...], NN)
        return 0

    lax.fori_loop(0, D // SUB, dh_step, 0)

    @pl.when(j == STEPS - 1)
    def _():
        cols_ref[...] = sums_in[...]
        norm_backward(acc_ref, xhat_ref, rstd_ref, par_ref[:, p + 6 : p + 7], out_ref, cols_ref, p + 6, p + 3)
        cols_ref[:, p + 2 : p + 3] = lane_sum(out_ref[...].astype(bf16))
    for i in range(STEPS):

        @pl.when(j == i)
        def _():
            hook(i + 1)


def inner(sums, du, dr, xhat, rstd, par, pieces, layer, lanes=(None, ())):
    n = len(pieces)
    return call(
        functools.partial(inner_kernel, n, 8 * layer), "inner",
        [sd(D // 2, FF, t=bf16), sd(D // 2, FF, t=bf16), sd(D, T), sd(D, 128)],
        [whole(D, 128), pl.BlockSpec((CHUNK, T), lambda j: (j, 0)), whole(D, T), whole(D, T), whole(8, T), whole(D, 128)]
        + anywhere(n),
        [
            pl.BlockSpec((D // 2, CHUNK), lambda j: (0, j)), pl.BlockSpec((D // 2, CHUNK), lambda j: (0, j)),
            whole(D, T), whole(D, 128),
        ],
        [pltpu.VMEM((D, FF), bf16), pltpu.VMEM((D, T), bf16), pltpu.VMEM((D, T), f32), pltpu.SemaphoreType.DMA((n,))],
        (sums, du, dr, xhat, rstd, par, *pieces), lanes, 9_700_000_000, 35_000_000, (STEPS,))


def values_kernel(n, p, sums_in, dr1_ref, v_ref, ctx_ref, f_ref, b_ref, small_ref, conv_ref, *rest, hook):
    order = Order(n)
    pieces = rest[:n]
    (keep_ref, send_ref, dctx_ref, dv_ref, dz_ref, dbv_ref, taps_ref, cols_ref,
     w_ref, dp_ref, perm_ref, vpad_ref, dpad_ref, sem) = rest[n:]
    loads = loader(pieces, w_ref, sem, (3 * D, D))
    for copy in loads:
        copy.start()
    for ref in (vpad_ref, dpad_ref):
        ref[:, 0:LEAD] = jnp.zeros((D, LEAD), bf16)
        ref[:, LEAD + T :] = jnp.zeros((D, LEAD), bf16)
    vpad_ref[:, LEAD : LEAD + T] = v_ref[...]
    dp_ref[...] = dr1_ref[...].astype(bf16)
    permute_rows(perm_ref, ctx_ref, order, D // 8)
    hook(0)
    for i, ref in enumerate((keep_ref, send_ref)):
        ref[...] = dot(perm_ref[i * (D // 2) : (i + 1) * (D // 2), :], dp_ref[...], NT).astype(bf16)
    for copy in loads:
        copy.wait()

    def dctx_step(i, _):
        got = dot(w_ref[rows(i * SUB, SUB), :], dp_ref[...], NN).astype(bf16)
        dctx_ref[rows(i * SUB, SUB), :] = got
        dpad_ref[rows(i * SUB, SUB), LEAD : LEAD + T] = got
        return 0

    lax.fori_loop(0, D // SUB, dctx_step, 0)
    hook(1)
    flip = jnp.where(
        lax.broadcasted_iota(jnp.int32, (CONV_N, CONV_N), 0)
        + lax.broadcasted_iota(jnp.int32, (CONV_N, CONV_N), 1) == CONV_N - 1, 1.0, 0.0).astype(bf16)

    def value_step(h, _):
        base = h * HD
        dctx = dctx_ref[rows(base, HD), :]
        f = f_ref[rows(base, HD), :]
        dw = split(dot(f, dctx, NT))
        dz_ref[h] = dot3(dw, split(small_ref[1, h]), NT)
        dbv = dot3(split(small_ref[0, h]), dw, TN).astype(bf16)
        dbv_ref[h] = dbv
        dv = dot(dbv, b_ref[rows(base, HD), :], TN)
        conv = dot(windows(dpad_ref, base), toeplitz(conv_ref[h, 1:2]), NT)
        dv_ref[rows(base, HD), :] = (dv + unstack_blocks(conv)).astype(bf16)
        flipped = dot(stack_blocks(dctx), flip, NN).astype(bf16)
        g = dot(flipped, windows(vpad_ref, base), TN)
        g = pltpu.roll(g, CONV_K - CONV_N + 1 - (LEAD - RADIUS), 1, stride=1, stride_axis=0)
        taps_ref[pl.ds(h, 1), :] = jnp.sum(g[:, 0:128], axis=0, keepdims=True)
        return 0

    lax.fori_loop(0, HEADS // 2, value_step, 0)
    hook(2)
    lax.fori_loop(HEADS // 2, HEADS, value_step, 0)
    cols_ref[...] = sums_in[...]
    cols_ref[:, p + 1 : p + 2] = lane_sum(dv_ref[...])
    hook(3)
    hook(4)


def values(sums, dr1, mix, ctx, f, b, small, conv, pieces, layer, lanes=(None, ())):
    n = len(pieces)
    return call(
        functools.partial(values_kernel, n, 8 * layer), "values",
        [
            sd(D // 2, D, t=bf16), sd(D // 2, D, t=bf16), sd(D, T, t=bf16), sd(D, T, t=bf16),
            sd(HEADS, LM, LM), sd(HEADS, LM, LM, t=bf16), sd(HEADS, 128), sd(D, 128),
        ],
        [whole(D, 128), whole(D, T), pl.BlockSpec((D, T), lambda *_: (2, 0)), whole(D, T), whole(D, T), whole(D, T),
         whole(*small.shape), whole(*conv.shape)] + anywhere(n),
        [whole(D // 2, D), whole(D // 2, D), whole(D, T), whole(D, T), whole(HEADS, LM, LM), whole(HEADS, LM, LM),
         whole(HEADS, 128), whole(D, 128)],
        [
            pltpu.VMEM((D, D), bf16), pltpu.VMEM((D, T), bf16), pltpu.VMEM((D, T), bf16),
            pltpu.VMEM((D, T + 2 * LEAD), bf16), pltpu.VMEM((D, T + 2 * LEAD), bf16), pltpu.SemaphoreType.DMA((n,)),
        ],
        (sums, dr1, mix, ctx, f, b, small, conv, *pieces), lanes, 5_000_000_000, 25_000_000, (1,))


def scores_kernel(p, sums_in, mix_ref, dctx_ref, f_ref, b_ref, lm_ref, a_ref, ns_ref, small_ref, dz0_ref, dbv_ref,
                  dqk_ref, cols_ref, dz_ref, da_ref, *, hook):
    hook(0)
    spread = segment_spread()
    for h in range(HEADS):
        da_ref[h] = jnp.zeros((LM, LM), f32)
        dz_ref[h] = dz0_ref[h]

    def ns_step(i, _):
        k = NS_ITERS - 1 - i
        d3, dzs, dps, d2 = [], [], [], []
        for h in range(HEADS):
            dzn = split(0.25 * dz_ref[h])
            d3.append(split(dot3(split(ns_ref[k, 0, h]), dzn, TN)))
            dz_ref[h] = dot3(dzn, split(ns_ref[k, 3, h]), NT)
        for h in range(HEADS):
            p = split(ns_ref[k, 1, h])
            d2.append(split(-dot3(p, d3[h], TN)))
            dps.append(dot3(d3[h], split(ns_ref[k, 2, h]), NT))
        for h in range(HEADS):
            p = ns_ref[k, 1, h]
            d1 = dot3(split(p), d2[h], TN)
            dp = d1 - dps[h] - dot3(d2[h], split(eye(7.0) - p), NT)
            dps[h] = split(dp)
        for h in range(HEADS):
            da_ref[h] += dot3(dps[h], split(ns_ref[k, 0, h]), NT)
            dz_ref[h] += dot3(split(a_ref[h]), dps[h], TN)
        return 0

    lax.fori_loop(0, NS_ITERS // 2, ns_step, 0)
    hook(1)
    lax.fori_loop(NS_ITERS // 2, NS_ITERS, ns_step, 0)
    hook(2)

    def score_step(h, _):
        base = h * HD
        a = a_ref[h]
        dz0 = dz_ref[h].T
        s = 1.0 / jnp.sum(a * a)
        da = da_ref[h] + s * dz0 - (2.0 * s * s * jnp.sum(dz0 * a)) * a
        dsa = (SCALE * a * (da - jnp.sum(a * da, axis=1, keepdims=True))).astype(bf16)
        ql = lm_ref[rows(base, HD), :]
        kl = lm_ref[rows(D + base, HD), :]
        q = mix_ref[rows(base, HD), :]
        k = mix_ref[rows(D + base, HD), :]
        f = f_ref[rows(base, HD), :].astype(f32)
        df = dot(small_ref[2, h].astype(bf16), dctx_ref[rows(base, HD), :], NN)
        dsf = (SCALE * f * (df - jnp.sum(f * df, axis=0, keepdims=True))).astype(bf16)
        b = b_ref[rows(base, HD), :].astype(f32)
        db = dot(dbv_ref[h], mix_ref[rows(2 * D + base, HD), :], NN)
        dsb = (SCALE * b * (db - jnp.sum(b * db, axis=1, keepdims=True))).astype(bf16)
        dkl = dot(q, dsf, NT) + dot(ql, dsa, NN)
        dql = dot(kl, dsa, NT) + dot(k, dsb, NT)
        dq = dot(kl, dsf, NN) + dot((dql * (1.0 / SEG)).astype(bf16), spread, NN)
        dk = dot(ql, dsb, NN) + dot((dkl * (1.0 / SEG)).astype(bf16), spread, NN)
        dqk_ref[rows(base, HD), :] = dq.astype(bf16)
        dqk_ref[rows(D + base, HD), :] = dk.astype(bf16)
        return 0

    lax.fori_loop(0, HEADS // 2, score_step, 0)
    hook(3)
    lax.fori_loop(HEADS // 2, HEADS, score_step, 0)
    cols_ref[...] = sums_in[...]
    cols_ref[:, p : p + 1] = lane_sum(dqk_ref[0:D, :])
    hook(4)


def scores(sums, mix, dctx, f, b, lm, a, ns, small, dz0, dbv, layer, lanes=(None, ())):
    return call(
        functools.partial(scores_kernel, 8 * layer), "scores", [sd(2 * D, T, t=bf16), sd(D, 128)], [vm()] * 11,
        [vm()] * 2, [pltpu.VMEM((HEADS, LM, LM), f32), pltpu.VMEM((HEADS, LM, LM), f32)],
        (sums, mix, dctx, f, b, lm, a, ns, small, dz0, dbv), lanes, 3_000_000_000, 30_000_000)


def inputs_kernel(n, first, tail, dr1_ref, xl_ref, dqk_ref, dv_ref, *rest, hook):
    order = Order(n)
    pieces, (keep_ref, send_ref, dx_ref, w_ref, perm_ref, sem) = rest[:n], rest[n:]
    loads = loader(pieces, w_ref, sem, (0, 3 * D))
    for copy in loads:
        copy.start()
    permute_rows(perm_ref, xl_ref, order, D // 8)
    for lane in tail:
        lane.use(keep_ref, send_ref)
    hook(0)
    for i in range(3):
        d = dqk_ref[i * D : (i + 1) * D, :] if i < 2 else dv_ref[...]
        for part, ref in enumerate((send_ref, keep_ref)):
            mine = perm_ref[(1 - part) * (D // 2) : (2 - part) * (D // 2), :]
            ref[:, i * D : (i + 1) * D] = dot(mine, d, NT).astype(bf16)
        hook(i + 1)
    for copy in loads:
        copy.wait()

    def dx_step(i, _):
        at = rows(i * SUB, SUB)
        got = dr1_ref[at, :] + dot(w_ref[at, 0 : 2 * D], dqk_ref[...], NN)
        got = got + dot(w_ref[at, 2 * D :], dv_ref[...], NN)
        if first:
            dx_ref[:, at] = got.T
        else:
            dx_ref[at, :] = got
        return 0

    for i in range(D // SUB):
        dx_step(i, 0)
        hook(i + 4)
    for i in range(7, TURNS):
        hook(i)


TURNS = 16


def inputs(dr1, xl, dqk, dv, pieces, first, lanes=(None, ()), tail=()):
    n = len(pieces)
    return call(
        functools.partial(inputs_kernel, n, first, tail), "inputs",
        [sd(D // 2, 3 * D, t=bf16), sd(D // 2, 3 * D, t=bf16), sd(*((T, D) if first else (D, T)))],
        [vm()] * 4 + anywhere(n), [vm()] * 3,
        [pltpu.VMEM((D, 3 * D), bf16), pltpu.VMEM((D, T), bf16), pltpu.SemaphoreType.DMA((n,))],
        (dr1, xl, dqk, dv, *pieces), lanes, 7_400_000_000, 25_000_000)


class Ring:
    def __init__(self, wide, narrow):
        self.wide, self.narrow = wide, narrow
        self.bits = wide.bit_length() - 1
        up = list(range(1, self.bits))
        self.gather_order = (up, up[::-1])
        self.scatter_order = (up[::-1], up)
        self.exact = wide == 8 and narrow == 4

    def pairs(self, flip):
        n = self.narrow
        out = []
        for w in range(self.wide):
            for z in range(n):
                to_w, to_z = flip(w, z)
                out.append((w * n + z, to_w * n + to_z))
        return out

    def narrow_pairs(self, k):
        return self.pairs(lambda w, z: (w, z ^ k))

    def step_pairs(self, order, s):
        return self.pairs(lambda w, z: (w ^ (1 << order[w & 1][s]), z))

    def core_pairs(self):
        return self.pairs(lambda w, z: (w ^ 1, z))

    def gathered(self, w):
        out = []
        for other in (0, 1):
            v = w ^ other
            for code in range(self.wide // 2):
                t = v
                for s in range(self.bits - 1):
                    if code >> s & 1:
                        t ^= 1 << self.gather_order[v & 1][s]
                out.append(t)
        return out

    def slots(self, w):
        out = []
        for other in (0, 1):
            v = w ^ other
            for code in range(self.wide // 2):
                t = v
                for s in range(self.bits - 1):
                    if code >> (self.bits - 2 - s) & 1:
                        t ^= 1 << self.scatter_order[v & 1][s]
                out.append(t)
        return out

    def mine(self, table):
        return lax.dynamic_index_in_dim(jnp.asarray(table), lax.axis_index("wide"), 0, keepdims=False)

    def gather(self, shard):
        z = lax.axis_index("narrow")
        parts = [shard] + [lax.ppermute(shard, AXES, self.narrow_pairs(k)) for k in range(1, self.narrow)]
        yield []
        bit = 1
        while bit < self.narrow:
            swap = (z & bit) != 0
            parts = [jnp.where(swap, parts[k ^ bit], parts[k]) for k in range(self.narrow)]
            bit *= 2
        held = [jnp.concatenate(parts, axis=0)]
        got = held
        for s in range(self.bits - 1):
            pairs = self.step_pairs(self.gather_order, s)
            fresh, got = got, [lax.ppermute(h, AXES, pairs) for h in held]
            held = held + got
            yield fresh
        other = [lax.ppermute(h, AXES, self.core_pairs()) for h in held]
        yield got
        held = held + other
        return held if self.exact else [self.join(held)]

    def join(self, pieces):
        inverse = np.stack([np.argsort(self.gathered(w)) for w in range(self.wide)]).astype(np.int32)
        stacked = jnp.stack(pieces)
        return jnp.take(stacked, self.mine(inverse), axis=0).reshape(-1, stacked.shape[-1])

    def scatter(self, keep, send):
        half = self.wide // 2
        if not self.exact:
            slots = np.stack([self.slots(w) for w in range(self.wide)]).astype(np.int32)
            whole = jnp.concatenate([keep, send], axis=0)
            whole = whole.reshape(self.wide, -1, whole.shape[-1])
            whole = jnp.take(whole, self.mine(slots), axis=0)
            keep, send = whole[:half], whole[half:]
        got = lax.ppermute(send, AXES, self.core_pairs())
        yield [send]
        total = keep.astype(f32) + got.astype(f32)
        for s in range(self.bits - 1):
            half //= 2
            away = total[half:].astype(bf16)
            got = lax.ppermute(away, AXES, self.step_pairs(self.scatter_order, s))
            yield [away]
            total = total[:half] + got.astype(f32)
        total = total[0]
        size = total.shape[0] // self.narrow
        z = lax.axis_index("narrow")
        own = lax.dynamic_slice_in_dim(total, z * size, size, axis=0)
        low = total.astype(bf16)
        parts = [lax.dynamic_slice_in_dim(low, (z ^ k) * size, size, axis=0) for k in range(1, self.narrow)]
        got = [lax.ppermute(parts[k - 1], AXES, self.narrow_pairs(k)) for k in range(1, self.narrow)]
        yield parts
        for part in got:
            own = own + part.astype(f32)
        return own

    def sum(self, keep, send):
        blocks = self.wide // 2
        return finish(self.scatter(
            keep.reshape(blocks, -1, keep.shape[-1]), send.reshape(blocks, -1, send.shape[-1])))

    def total(self, value):
        bit = 1
        while bit < self.narrow:
            value = value + lax.ppermute(value, AXES, self.narrow_pairs(bit))
            bit *= 2
        for s in range(self.bits - 1):
            value = value + lax.ppermute(value, AXES, self.pairs(lambda w, z: (w ^ (2 << s), z)))
        return value + lax.ppermute(value, AXES, self.core_pairs())


def natural_halves(keep, send):
    both = jnp.stack([keep, send], axis=1)
    both = both.reshape(2, -1, both.shape[-1])
    return both[0], both[1]


def conv_rows(conv):
    at = LEAD - RADIUS
    tail = CONV_K - at - KSIZE
    both = jnp.stack([conv, conv[:, ::-1]], axis=1)
    return jnp.pad(both.astype(f32), ((0, 0), (0, 0), (at, tail)))


def finish(steps):
    while True:
        try:
            next(steps)
        except StopIteration as end:
            return end.value


def small_outputs(ring, total, size, hidden_size):
    layers = total.shape[0] // (8 + STEPS)
    here = lax.axis_index("wide") * ring.narrow + lax.axis_index("narrow")
    lines = total[: 8 * layers, :D].reshape(layers, 8, D)
    lines = lax.dynamic_slice_in_dim(lines, here * size, size, axis=2)
    inb = total[8 * layers :, :D].reshape(layers, FF)
    inb = lax.dynamic_slice_in_dim(inb, here * hidden_size, hidden_size, axis=1)
    taps = total[:, D : D + KSIZE].reshape(layers, HEADS, KSIZE)
    return lines[:, :6], lines[:, 6:], inb, taps


def small_shard(in_b, bias_rows, gain_rows):
    layers, size = bias_rows.shape[0], bias_rows.shape[2]
    columns = jnp.concatenate([bias_rows, gain_rows], axis=1).transpose(2, 0, 1).reshape(size, 8 * layers)
    inner_bias = in_b.reshape(layers, size, -1).transpose(1, 0, 2).reshape(size, -1)
    small = jnp.concatenate([columns, inner_bias], axis=1)
    return jnp.pad(small, ((0, 0), (0, 128 - small.shape[1])))


def gather_all(ring, attention_shards, in_w, out2_w):
    layers = in_w.shape[0]
    return (
        [finish(ring.gather(shard)) for shard in attention_shards],
        [finish(ring.gather(in_w[layer])) for layer in range(layers)],
        [finish(ring.gather(out2_w[layer])) for layer in range(layers)],
    )


class Plan:
    def __init__(self):
        self.count = 0

    def lanes(self, *lanes):
        self.count += 1
        return (self.count, list(lanes))


def pieces_of(block, a, b, c):
    return [block, a.value] + [m.value for m in b] + [m.value for m in c]


def body(ring, tokens, cotangent, qkv_w, out_w, in_w, in_b, out2_w, bias_rows, gain_rows, conv_w):
    layers = qkv_w.shape[0]
    size = qkv_w.shape[1]
    small = small_shard(in_b, bias_rows, gain_rows)
    shards = [
        jnp.concatenate([qkv_w[layer], out_w[layer]] + ([small] if layer == 0 else []), axis=1)
        for layer in range(layers)]
    plan = Plan()
    none = (None, ())
    on = ring.exact and layers == 2
    x = tokens.T.astype(f32)
    conv = [conv_rows(conv_w[layer]) for layer in range(layers)]
    lanes = {name: [none] * layers for name in ("project", "attend", "up", "down")}

    if on:
        spread = Spread(shards[0], 0, 1)
        exchange(plan.lanes(spread), 2)
        u1 = spread.value
        a1 = Move(u1, "a", 0, 1)
        b1 = [Move(u1, "b", 1, 2), Move(a1, "b", 1, 2)]
        c1 = [Move(u1, "core", 0, 3), Move(a1, "core", 1, 3)] + [Move(b, "core", 2, 3) for b in b1]
        s2, s3 = Spread(in_w[0], 0, 3), Spread(out2_w[0], 0, 3)
        exchange(plan.lanes(a1, *b1, *c1, s2, s3), 4)
        att = [pieces_of(u1, a1, b1, c1), None]
        win, wout = [None, None], [None, None]
    else:
        att, win, wout = gather_all(ring, shards, in_w, out2_w)

    kept = []
    par = None
    for layer in range(layers):
        final = layer == layers - 1
        if on and layer == 0:
            u2, u3 = s2.value, s3.value
            a2, a3 = Move(u2, "a", 0, 4), Move(u3, "a", 0, 4)
            c2, c3 = [Move(u2, "core", 0, 4)], [Move(u3, "core", 0, 4)]
            lanes["project"][0] = plan.lanes(a2, c2[0], a3, c3[0])
        if on and layer == 1:
            b5 = [Move(u5, "b", 0, 4), Move(a5.value, "b", 0, 4)]
            c5 = [Move(u5, "core", 0, 4), Move(a5.value, "core", 0, 4)]
            lanes["project"][1] = plan.lanes(*b5, *c5)
        xl, mix, lm, par = project(x, att[layer], par, layer, lanes["project"][layer])
        if on and layer == 0:
            b2 = [Move(u2, "b", 0, 1), Move(a2.value, "b", 0, 1)]
            b3 = [Move(u3, "b", 1, 3), Move(a3.value, "b", 1, 3)]
            c2 += [Move(a2.value, "core", 0, 1)] + [Move(b, "core", 1, 4) for b in b2]
            c3 += [Move(a3.value, "core", 0, 1)] + [Move(b, "core", 3, 4) for b in b3]
            s4 = Spread(shards[1], 0, 4)
            lanes["attend"][0] = plan.lanes(*b2, *b3, *c2[1:], *c3[1:], s4)
        if on and layer == 1:
            b6 = [Move(u6, "b", 0, 2), Move(a6.value, "b", 0, 2)]
            c6 = [Move(u6, "core", 0, 1), Move(a6.value, "core", 0, 1)] + [Move(b, "core", 2, 4) for b in b6]
            c5 += [Move(b.value, "core", 0, 4) for b in b5]
            lanes["attend"][1] = plan.lanes(*b6, *c6, *c5[2:])
        ctx, f, b, a, ns, sm, xhat1, rstd1 = attend(
            x, mix, lm, att[layer], par, conv[layer], layer, lanes["attend"][layer])
        if on and layer == 0:
            win[0], wout[0] = pieces_of(u2, a2, b2, c2), pieces_of(u3, a3, b3, c3)
            u4 = s4.value
            a4 = Move(u4, "a", 0, 1)
            b4 = [Move(u4, "b", 1, 4), Move(a4, "b", 1, 4)]
            c4 = [Move(u4, "core", 0, 1), Move(a4, "core", 1, 4)]
            s5, s6 = Spread(in_w[1], 0, 4), Spread(out2_w[1], 0, 4)
            lanes["up"][0] = plan.lanes(a4, *b4, *c4, s5, s6)
        if on and layer == 1:
            win[1], wout[1] = pieces_of(u5, a5, b5, c5), pieces_of(u6, a6, b6, c6)
        at = 8 * layers + FF // D * layer
        inb = par[:, at : at + FF // D].reshape(FF, 1)
        act, slope = up(xhat1, win[layer], par, inb, layer, lanes["up"][layer])
        if on and layer == 0:
            c4 += [Move(b.value, "core", 0, 4) for b in b4]
            u5, u6 = s5.value, s6.value
            a5, a6 = Move(u5, "a", 0, 4), Move(u6, "a", 0, 4)
            lanes["down"][0] = plan.lanes(*c4[2:], a5, a6)
        xhat2, rstd2, x = down(xhat1, act, wout[layer], par, layer, final, lanes["down"][layer])
        if on and layer == 0:
            att[1] = pieces_of(u4, a4, b4, c4)
        kept.append((xl, mix, lm, ctx, f, b, a, ns, sm, xhat1, rstd1, act, slope, xhat2, rstd2))
    output = x

    dy = cotangent
    sums = jnp.zeros((D, 128), f32)
    taps = [None] * layers
    grads = [[None] * 4 for _ in range(layers)]
    waiting = []

    def sum_first(keep, send, turns, layer, place, **more):
        lane = ReduceFirst(keep, send, turns, **more)
        waiting.append((lane, layer, place))
        return lane

    def sum_last(turns, chained=False):
        lane, layer, place = waiting.pop(0)
        if chained:
            last = ReduceLast(None, None, turns, inside=lane)
        else:
            last = ReduceLast(*lane.value, turns)
        ends.append((last, layer, place))
        return last

    ends = []
    halves = None
    for layer in reversed(range(layers)):
        xl, mix, lm, ctx, f, b, a, ns, sm, xhat1, rstd1, act, slope, xhat2, rstd2 = kept[layer]
        lane = plan.lanes(sum_first(*halves, (0, 1, 4), 1, 0)) if on and halves else none
        keep, send, du, dr2, sums = hidden(
            sums, dy, xhat2, rstd2, par, act, slope, wout[layer], layer, layer == layers - 1, lane)
        if on:
            out2 = (keep.reshape(-1, D), send.reshape(-1, D))
            lane = [sum_last((0, 1, 4))] if waiting else []
            lane = plan.lanes(*lane, sum_first(*out2, (0, 1, 4), layer, 3))
        else:
            keep, send = natural_halves(keep, send)
            grads[layer][3] = ring.sum(keep, send)
        keep, send, dr1, sums = inner(sums, du, dr2, xhat1, rstd1, par, win[layer], layer, lane)
        if on:
            lane = plan.lanes(sum_last((0, 1, 4)), sum_first(keep, send, (0, 1, 4), layer, 2))
        else:
            grads[layer][2] = ring.sum(keep, send)
        keep, send, dctx, dv, dz, dbv, taps[layer], sums = values(
            sums, dr1, mix, ctx, f, b, sm, conv[layer], att[layer], layer, lane)
        if on:
            last = sum_last((0, 1, 4))
            lead = sum_first(keep, send, (0, 1, 2), layer, 1, chained=True)
            lane = plan.lanes(last, lead, sum_last((2, 3, 4), chained=True))
        else:
            grads[layer][1] = ring.sum(keep, send)
        dqk, sums = scores(sums, mix, dctx, f, b, lm, a, ns, sm, dz, dbv, layer, lane)
        tail = []
        if on and layer == 0:
            turns = [(1, 4, 7), (2, 5, 9), (3, 6, 11)]
            lane = []
            for part in range(3):
                lead = ReduceFirst(
                    None, None, turns[part], chained=True, columns=slice(part * D, (part + 1) * D))
                after = turns[part][2]
                last = ReduceLast(None, None, (after, after + 2, after + 4), inside=lead)
                tail.append(lead)
                ends.append((last, 0, part))
                lane += [lead, last]
            total = Total(sums, taps, (0, 1, 2, 3, 4, 5))
            lane = plan.lanes(*lane, total)
        else:
            lane = none
        keep, send, dy = inputs(dr1, xl, dqk, dv, att[layer], layer == 0, lane, tuple(tail))
        halves = (keep, send)
        if not on:
            grads[layer][0] = ring.sum(keep, send)
    if on:
        qkv = [None] * 3
        for lane, layer, place in ends:
            if layer == 0 and lane.columns == D and lane.inside is not None and lane.inside.at is not None:
                qkv[place] = lane.value
            else:
                grads[layer][place] = lane.value
        grads[0][0] = jnp.concatenate(qkv, axis=1)
        total = total.value
    else:
        flat = jnp.concatenate([sums.T[:SMALL], jnp.concatenate(taps, axis=0)], axis=1)
        total = ring.total(flat)
    gbias, ggain, ginb, gtaps = small_outputs(ring, total, size, in_b.shape[1])
    stacked = [jnp.stack([grads[layer][i] for layer in range(layers)]) for i in range(4)]
    return (output, dy, stacked[0], stacked[1], stacked[2], ginb, stacked[3], gbias, ggain, gtaps)


def solution(mesh):
    ring = Ring(mesh.shape["wide"], mesh.shape["narrow"])
    rows3 = P(None, AXES, None)
    columns3 = P(None, None, AXES)
    weights = (rows3, rows3, rows3, P(None, AXES), rows3, columns3, columns3, P())
    return jax.shard_map(
        functools.partial(body, ring),
        mesh=mesh,
        in_specs=(P(AXES, None), P(AXES, None)) + weights,
        out_specs=(P(AXES, None), P(AXES, None)) + weights,
        check_vma=False,
    )
```

time: 767 us -> 628 us (0.82)
  Pallas kernels: 350 us -> 592 us
  waiting for transfers between devices: 211 us -> 0 us
  starting transfers between devices: 134 us -> 0 us
  other arithmetic: 38.6 us -> 13.1 us
    pallas_call x8 -> x20, Pallas kernels: 350 us -> 592 us  [call(): pl.pallas_call(run, out_shape=list(out_shape) + [o for o, _ in lane_outs]...]
    ppermute x106 -> x0, waiting for transfers between devices: 211 us -> none  [the longest x12 75.6 us: scatter(): lax.ppermute(away, AXES, self.step_pairs(self.scatter_order, s)).astype(f32)]
    ppermute x106 -> x0, starting transfers between devices: 134 us -> none  [the longest x18 47.1 us: gather(): lax.ppermute(shard, AXES, self.narrow_pairs(k))]
    add x24 -> x0, other arithmetic: 23.9 us -> none  [the longest x6 12.7 us: scatter(): keep.astype(f32) + lax.ppermute(send, AXES, self.core_pairs()).astype(f32)]
  transfers between devices with their start and end apart: 106 -> 0, of which waited for: 36 -> 0; matrix products, arithmetic and copies ran while one was open for 7% -> 0% of each run, Pallas kernels for 28% -> 0%
where the time goes in v2:
time: 628 us; the launch traced here: 620 us
  Pallas kernels  592 us (94%)
  local copies, waits for them, and re-layouts  14.2 us (2%)
  other arithmetic  13.1 us (2%)
    pallas_call x20, Pallas kernels, call(): pl.pallas_call(run, out_shape=list(out_shape) + [o for o, _ in lane_outs]...  592 us

profile of v2, /device:TPU:0, one launch (start us, length us, event | category | flops | bytes accessed | tf_op | source)
XLA Modules:
  0.0 620.3 jit_solution(8800770848785167911)
XLA Ops:
  0.6 1.7 copy.43
  2.4 0.0 copy-start.12
  2.4 0.0 copy-start.10
  2.4 0.0 copy-start.11
  2.4 0.0 copy-start.8
  2.4 0.0 copy-start.6
  2.4 0.0 copy-start.2
  2.4 0.0 copy-start.3
  2.4 2.1 convert_bitcast_fusion.refs_0_
  4.5 0.1 reshape.75
  4.6 0.1 copy.45
  4.7 0.1 copy.47
  4.8 0.1 copy.46
  4.9 0.1 fusion.4
  5.1 0.7 pad_maximum_fusion.3.refs_0_
  5.7 17.5 %exchange.2 = bf16[4,24,3200]{2,1,0:T(8,128)(2,1)} custom-call(bf16[24,3200]{1,0:T(8,128)(2,1)} %pad_maximum_fusion.3.refs_0_), custom_call_target="tpu_custom_call" | custom-call | bytes 10000000 | tf_op jit(solution)/shard_map/exchange/pallas_call | solution.py:168
  23.2 0.7 slice_bitcast_fusion.1
  23.9 0.0 copy-done.3
  23.9 0.7 slice_bitcast_fusion
  24.7 33.4 %exchange.3 = (bf16[96,3200]{1,0:T(8,128)(2,1)}, bf16[96,3200]{1,0:T(8,128)(2,1)}, bf16[96,3200]{1,0:T(8,128)(2,1)}, bf16[96,3200]{1,0:T(8,128)(2,1)}, bf16[96,3...) custom-call(bf16[96,3200]{1,0:T(8,128)(2,1)} %bitcast.55, ...), custom_call_target="tpu_custom_call" | custom-call | bytes 10000000 | tf_op jit(solution)/shard_map/exchange/pallas_call | solution.py:168
  58.1 0.0 copy-start.9
  58.1 21.7 %project.2 = (bf16[768,1024]{1,0:T(8,128)(2,1)}, bf16[2304,1024]{1,0:T(8,128)(2,1)}, bf16[1536,64]{1,0:T(8,128)(2,1)}, f32[768,128]{1,0:T(8,128)}, bf16[96,3072]...) custom-call(f32[768,1024]{1,0:T(8,128)} %convert_bitcast_fusion.refs_0_, ...), custom_call_target="tpu_custom_call" | custom-call | flops 3800000000 | bytes 14000000 | tf_op jit(solution)/shard_map/project/pallas_call | solution.py:168
  79.8 0.1 rev.6
  79.9 0.7 fusion.1.refs_4_.refs_7_
  80.7 0.7 pad_maximum_fusion.4.refs_19_
  81.3 45.9 %attend.2 = (bf16[768,1024]{1,0:T(8,128)(2,1)}, bf16[768,1024]{1,0:T(8,128)(2,1)}, bf16[768,1024]{1,0:T(8,128)(2,1)}, f32[12,64,64]{2,1,0:T(8,128)}, f32[6,4,12,...) custom-call(f32[768,1024]{1,0:T(8,128)} %convert_bitcast_fusion.refs, ...), custom_call_target="tpu_custom_call" | custom-call | flops 3000000000 | bytes 30000000 | tf_op jit(solution)/shard_map/attend/pallas_call | solution.py:168
  127.2 0.3 fusion.5
  127.5 1.5 reshape.92.refs_2_
  129.0 31.4 %up.2 = (bf16[3072,1024]{1,0:T(8,128)(2,1)}, bf16[3072,1024]{1,0:T(8,128)(2,1)}, bf16[96,3072]{1,0:T(8,128)(2,1)}, bf16[96,3072]{1,0:T(8,128)(2,1)}, bf16[96,307...) custom-call(f32[768,1024]{1,0:T(8,128)} %get-tuple-element.167.refs_, ...), custom_call_target="tpu_custom_call" | custom-call | flops 4899999744 | bytes 24000000 | tf_op jit(solution)/shard_map/up/pallas_call | solution.py:168
  160.4 22.2 %down.2 = (f32[768,1024]{1,0:T(8,128)}, f32[8,1024]{1,0:T(8,128)}, f32[768,1024]{1,0:T(8,128)}, bf16[96,3072]{1,0:T(8,128)(2,1)}, bf16[96,3072]{1,0:T(8,128)(2,1...) custom-call(f32[768,1024]{1,0:T(8,128)} %get-tuple-element.167.refs_0_.refs_3_, ...), custom_call_target="tpu_custom_call" | custom-call | flops 4899999744 | bytes 24000000 | tf_op jit(solution)/shard_map/down/pallas_call | solution.py:168
  182.6 21.5 %project.3 = (bf16[768,1024]{1,0:T(8,128)(2,1)}, bf16[2304,1024]{1,0:T(8,128)(2,1)}, bf16[1536,64]{1,0:T(8,128)(2,1)}, bf16[96,3072]{1,0:T(8,128)(2,1)}, bf16[96...) custom-call(f32[768,1024]{1,0:T(8,128)} %get-tuple-element.186.refs_0_, ...), custom_call_target="tpu_custom_call" | custom-call | flops 3800000000 | bytes 14000000 | tf_op jit(solution)/shard_map/project/pallas_call | solution.py:168
  204.1 0.1 rev.7
  204.2 0.7 fusion.refs_4_.refs_7_
  205.0 36.0 %attend.3 = (bf16[768,1024]{1,0:T(8,128)(2,1)}, bf16[768,1024]{1,0:T(8,128)(2,1)}, bf16[768,1024]{1,0:T(8,128)(2,1)}, f32[12,64,64]{2,1,0:T(8,128)}, f32[6,4,12,...) custom-call(f32[768,1024]{1,0:T(8,128)} %get-tuple-element.186.refs_, ...), custom_call_target="tpu_custom_call" | custom-call | flops 3000000000 | bytes 30000000 | tf_op jit(solution)/shard_map/attend/pallas_call | solution.py:168
  240.9 1.5 reshape.93.refs_2_
  242.5 18.8 %up.3 = (bf16[3072,1024]{1,0:T(8,128)(2,1)}, bf16[3072,1024]{1,0:T(8,128)(2,1)}) custom-call(f32[768,1024]{1,0:T(8,128)} %get-tuple-element.198.refs_0_.refs_3_, f32[768,128]{1,0:T(8,128)} %get-tuple-element.164.refs_3_.refs_1_.refs_4_.refs_5_, f32[3072,1]{1,0:T(8,128)} %reshape.93.refs_2_, bf16[96,3072]{1,0:T(8,128)(2,1)} %bitcast.102, ...), custom_call_target="tpu_custom_call" | custom-call | flops 4899999744 | bytes 24000000 | tf_op jit(solution)/shard_map/up/pallas_call | solution.py:168
  261.3 16.0 %down.3 = (f32[768,1024]{1,0:T(8,128)}, f32[8,1024]{1,0:T(8,128)}, bf16[1024,768]{1,0:T(8,128)(2,1)}) custom-call(f32[768,1024]{1,0:T(8,128)} %get-tuple-element.198.refs_0_.refs_3_, f32[768,128]{1,0:T(8,128)} %get-tuple-element.164.refs_3_.refs_1_.refs_4_.refs_5_, bf16[3072,1024]{1,0:T(8,128)(2,1)} %get-tuple-element.203.refs_2_.refs_5_, ...), custom_call_target="tpu_custom_call" | custom-call | flops 4899999744 | bytes 24000000 | tf_op jit(solution)/shard_map/down/pallas_call | solution.py:168
  277.3 0.8 broadcast_in_dim.3.refs_0_
  278.1 24.9 %hidden.2 = (bf16[4,384,768]{2,1,0:T(8,128)(2,1)}, bf16[4,384,768]{2,1,0:T(8,128)(2,1)}, bf16[3072,1024]{1,0:T(8,128)(2,1)}, f32[768,1024]{1,0:T(8,128)}, f32[768,128]{1,0:T(8,128)}) custom-call(f32[768,128]{1,0:T(8,128)} %broadcast_in_dim.3.refs_0_, bf16[1024,768]{1,0:T(8,128)(2,1)} %refs_1_.1, f32[768,1024]{1,0:T(8,128)} %get-tuple-element.211.refs_2_, ...), custom_call_target="tpu_custom_call" | custom-call | flops 9699999744 | bytes 40000000 | tf_op jit(solution)/shard_map/hidden/pallas_call | solution.py:168
  303.0 27.9 %inner.2 = (bf16[384,3072]{1,0:T(8,128)(2,1)}, bf16[384,3072]{1,0:T(8,128)(2,1)}, f32[768,1024]{1,0:T(8,128)}, f32[768,128]{1,0:T(8,128)}, bf16[384,768]{1,0:T(8,128)(2,1)}, /*index=5*/f32[384,768]{1,0:T(8,128)}) custom-call(f32[768,128]{1,0:T(8,128)} %get-tuple-element.214.refs_0_, bf16[3072,1024]{1,0:T(8,128)(2,1)} %get-tuple-element.215.refs_1_, ...), custom_call_target="tpu_custom_call" | custom-call | flops 9699999744 | bytes 35000000 | tf_op jit(solution)/shard_map/inner/pallas_call | solution.py:168
  330.9 36.6 %values.2 = (bf16[384,768]{1,0:T(8,128)(2,1)}, bf16[384,768]{1,0:T(8,128)(2,1)}, bf16[768,1024]{1,0:T(8,128)(2,1)}, bf16[768,1024]{1,0:T(8,128)(2,1)}, f32[12,64...) custom-call(f32[768,128]{1,0:T(8,128)} %get-tuple-element.220.refs_0, ...), custom_call_target="tpu_custom_call" | custom-call | flops 5000000000 | bytes 25000000 | tf_op jit(solution)/shard_map/values/pallas_call | solution.py:168
  367.5 38.6 %scores.2 = (bf16[1536,1024]{1,0:T(8,128)(2,1)}, f32[768,128]{1,0:T(8,128)}, f32[24,3072]{1,0:T(8,128)}, f32[24,768]{1,0:T(8,128)}) custom-call(f32[768,128]{1,0:T(8,128)} %get-tuple-element.230.refs_0_, bf16[2304,1024]{1,0:T(8,128)(2,1)} %get-tuple-element.193.refs_1_.refs_2_, bf16[768,1024]{1,0:T(8,128)(2,1)} %get-tuple-element.231.refs_2_, ...), custom_call_target="tpu_custom_call" | custom-call | flops 3000000000 | bytes 30000000 | tf_op jit(solution)/shard_map/scores/pallas_call | solution.py:168
  406.1 13.2 %inputs.2 = (bf16[384,2304]{1,0:T(8,128)(2,1)}, bf16[384,2304]{1,0:T(8,128)(2,1)}, f32[768,1024]{1,0:T(8,128)}) custom-call(f32[768,1024]{1,0:T(8,128)} %get-tuple-element.221.refs_1_.refs_0_, bf16[768,1024]{1,0:T(8,128)(2,1)} %get-tuple-element.241.refs_1_, bf16[1536,1024]{1,0:T(8,128)(2,1)} %get-tuple-element.242.refs_2_, ...), custom_call_target="tpu_custom_call" | custom-call | flops 7400000000 | bytes 25000000 | tf_op jit(solution)/shard_map/inputs/pallas_call | solution.py:168
  419.2 28.0 %hidden.3 = (bf16[4,384,768]{2,1,0:T(8,128)(2,1)}, bf16[4,384,768]{2,1,0:T(8,128)(2,1)}, bf16[3072,1024]{1,0:T(8,128)(2,1)}, f32[768,1024]{1,0:T(8,128)}, f32[76...) custom-call(f32[768,128]{1,0:T(8,128)} %get-tuple-element.240.refs_0_, ...), custom_call_target="tpu_custom_call" | custom-call | flops 9699999744 | bytes 40000000 | tf_op jit(solution)/shard_map/hidden/pallas_call | solution.py:168
  447.2 32.0 %inner.3 = (bf16[384,3072]{1,0:T(8,128)(2,1)}, bf16[384,3072]{1,0:T(8,128)(2,1)}, f32[768,1024]{1,0:T(8,128)}, f32[768,128]{1,0:T(8,128)}, f32[24,2304]{1,0:T(8,...) custom-call(f32[768,128]{1,0:T(8,128)} %get-tuple-element.250.refs_0_, ...), custom_call_target="tpu_custom_call" | custom-call | flops 9699999744 | bytes 35000000 | tf_op jit(solution)/shard_map/inner/pallas_call | solution.py:168
  479.2 35.2 %values.3 = (bf16[384,768]{1,0:T(8,128)(2,1)}, bf16[384,768]{1,0:T(8,128)(2,1)}, bf16[768,1024]{1,0:T(8,128)(2,1)}, bf16[768,1024]{1,0:T(8,128)(2,1)}, f32[12,64...) custom-call(f32[768,128]{1,0:T(8,128)} %get-tuple-element.260.refs_0, ...), custom_call_target="tpu_custom_call" | custom-call | flops 5000000000 | bytes 25000000 | tf_op jit(solution)/shard_map/values/pallas_call | solution.py:168
  514.4 41.8 %scores.3 = (bf16[1536,1024]{1,0:T(8,128)(2,1)}, f32[768,128]{1,0:T(8,128)}, f32[24,3072]{1,0:T(8,128)}, f32[24,768]{1,0:T(8,128)}) custom-call(f32[768,128]{1,0:T(8,128)} %get-tuple-element.269.refs_0_, bf16[2304,1024]{1,0:T(8,128)(2,1)} %get-tuple-element.162.refs_1_.refs_2_, bf16[768,1024]{1,0:T(8,128)(2,1)} %get-tuple-element.270.refs_2_, ...), custom_call_target="tpu_custom_call" | custom-call | flops 3000000000 | bytes 30000000 | tf_op jit(solution)/shard_map/scores/pallas_call | solution.py:168
  556.2 49.2 %inputs.3 = (bf16[384,2304]{1,0:T(8,128)(2,1)}, bf16[384,2304]{1,0:T(8,128)(2,1)}, f32[1024,768]{1,0:T(8,128)}, f32[24,768]{1,0:T(8,128)}, f32[24,768]{1,0:T(8,1...) custom-call(f32[768,1024]{1,0:T(8,128)} %get-tuple-element.258.refs_1_.refs_0_, bf16[768,1024]{1,0:T(8,128)(2,1)} %get-tuple-element.259.refs_1_, ...), custom_call_target="tpu_custom_call" | custom-call | flops 7400000000 | bytes 25000000 | tf_op jit(solution)/shard_map/inputs/pallas_call | solution.py:168
  605.4 1.1 maximum_bitcast_fusion
  606.6 1.7 pad_maximum_fusion.2
  608.3 1.6 pad_maximum_fusion.5
  609.9 0.0 copy-done.5
  609.9 1.8 pad_maximum_fusion
  611.7 0.7 slice.63
  612.4 0.6 reshape.89
  613.1 1.3 constant_dynamic-slice_fusion.2
  614.4 0.0 copy-done.4
  614.4 1.8 pad_maximum_fusion.1
  616.2 0.0 copy-done.7
  616.2 0.1 constant_dynamic-slice_fusion
  616.3 0.6 copy.56
  616.9 0.7 constant_dynamic-slice_fusion.1
  617.5 0.6 copy.57
  618.2 1.7 copy.65
  (27 shorter events, 0.1 us)
Async XLA Ops:
  2.4 2.1 copy-start.12
  2.4 2.4 copy-start.10
  2.4 2.4 copy-start.11
  2.4 2.6 copy-start.8
  2.4 2.6 copy-start.6
  2.4 20.8 %copy-start.2 = (bf16[2,24,3072]{2,1,0:T(8,128)(2,1)S(1)}, bf16[2,24,3072]{2,1,0:T(8,128)(2,1)}, u32[]{:S(2)}) copy-start(bf16[2,24,3072]{2,1,0:T(8,128)(2,1)} %param.14) | copy-start | bytes 884740
  2.4 21.5 %copy-start.3 = (bf16[2,96,768]{2,1,0:T(8,128)(2,1)S(1)}, bf16[2,96,768]{2,1,0:T(8,128)(2,1)}, u32[]{:S(2)}) copy-start(bf16[2,96,768]{2,1,0:T(8,128)(2,1)} %param.16) | copy-start | bytes 884740
  58.1 21.7 %copy-start.9 = (bf16[2,12,33]{2,0,1:T(2,128)(2,1)S(1)}, bf16[2,12,33]{2,0,1:T(2,128)(2,1)}, u32[]{:S(2)}) copy-start(bf16[2,12,33]{2,0,1:T(2,128)(2,1)} %param.19) | copy-start | bytes 4756
  81.3 45.9 %copy-start = (f32[768,128]{1,0:T(8,128)S(1)}, f32[768,128]{1,0:T(8,128)}, u32[]{:S(2)}) copy-start(f32[768,128]{1,0:T(8,128)} %get-tuple-element.164.refs_3_.refs_1_.refs_4_.refs_5_) | copy-start | bytes 1179652
  556.2 53.7 %copy-start.5 = (f32[24,3072]{1,0:T(8,128)S(1)}, f32[24,3072]{1,0:T(8,128)}, u32[]{:S(2)}) copy-start(f32[24,3072]{1,0:T(8,128)} %get-tuple-element.292) | copy-start | bytes 884740
  556.2 58.2 %copy-start.4 = (f32[96,768]{1,0:T(8,128)S(1)}, f32[96,768]{1,0:T(8,128)}, u32[]{:S(2)}) copy-start(f32[96,768]{1,0:T(8,128)} %get-tuple-element.295) | copy-start | bytes 884740
  605.4 10.8 %copy-start.7 = (f32[24,896]{1,0:T(8,128)S(1)}, f32[24,896]{1,0:T(8,128)}, u32[]{:S(2)}) copy-start(f32[24,896]{1,0:T(8,128)} %get-tuple-element.293) | copy-start | bytes 258052
  605.4 12.7 %copy-start.1 = (f32[1024,768]{1,0:T(8,128)S(1)}, f32[1024,768]{1,0:T(8,128)}, u32[]{:S(2)}) copy-start(f32[1024,768]{1,0:T(8,128)} %get-tuple-element.355) | copy-start | bytes 9437188

commit v3 on v2

--- a/solution.py
+++ b/solution.py
@@ -128,6 +128,29 @@
     return out
 
 
+def sizes_of(groups, layer):
+    return [(len(g), g[0].shape[1] - (128 if layer == 0 and i == 0 else 0)) for i, g in enumerate(groups)]
+
+
+def grouped(refs, sizes):
+    groups = []
+    for n, _ in sizes:
+        groups.append(refs[:n])
+        refs = refs[n:]
+    return groups, refs
+
+
+def column_loader(groups, sizes, dst, sem, low, high):
+    out = []
+    at = 0
+    for g, (n, width) in enumerate(sizes):
+        a, b = max(low, at), min(high, at + width)
+        if b > a:
+            out += loader(groups[g], dst.at[:, pl.ds(a - low, b - a)], sem.at[g], (a - at, b - a))
+        at += width
+    return out
+
+
 def call(kernel, name, out_shape, in_specs, out_specs, scratch, args, lanes, flops, size, grid=None, trans=0):
     identity, lanes = lanes
     ins, outs = len(args), len(out_shape)
@@ -218,7 +241,7 @@
 
 class Move:
     def __init__(self, source, name, start, wait):
-        self.chained = isinstance(source, Move)
+        self.chained = not hasattr(source, "dtype")
         self.source, self.name, self.start, self.wait = source, name, start, wait
         self.shape = source.shape
         self.args = [] if self.chained else [source]
@@ -241,14 +264,15 @@
             self.copy().start()
 
     def done(self, got):
-        self.value = got[0]
+        self.value = got[0].reshape(-1, self.shape[-1])
 
 
 class Spread:
     def __init__(self, shard, start, wait):
         self.start, self.wait = start, wait
+        self.shape = (4, *shard.shape)
         self.args, self.specs = [shard], [ANY]
-        self.outs = [(sd(4, *shard.shape, t=bf16), ANY)]
+        self.outs = [(sd(*self.shape, t=bf16), ANY)]
         self.scratch = [DMA((7,))]
         self.partners = ["z1", "z2", "z3"]
 
@@ -271,8 +295,41 @@
                 copy.start()
 
     def done(self, got):
-        value = got[0]
-        self.value = value.reshape(-1, value.shape[-1])
+        self.value = got[0].reshape(-1, self.shape[-1])
+
+
+class Gather:
+    def __init__(self, block):
+        self.block, self.moves = block, {}
+
+    def at(self, name):
+        if name == "own":
+            return self.block
+        return self.moves[name]
+
+    def go(self, **turns):
+        out = []
+        fresh = {}
+        value = lambda k: fresh[k] if k in fresh else (
+            self.moves[k].value if k in self.moves else
+            self.block.value if hasattr(self.block, "value") else self.block)
+        for key, turn in turns.items():
+            if key == "a":
+                todo = [("a", "own", "a")]
+            elif key == "b":
+                todo = [("b0", "own", "b"), ("b1", "a", "b")]
+            else:
+                todo = {"core0": [("c0", "own", "core")], "core1": [("c1", "a", "core")],
+                        "core2": [("c2", "b0", "core"), ("c3", "b1", "core")]}[key]
+            for name, source, partner in todo:
+                fresh[name] = Move(value(source), partner, *turn)
+                out.append(fresh[name])
+        self.moves.update(fresh)
+        return sorted(out, key=lambda m: m.start)
+
+    def pieces(self):
+        block = self.block.value if hasattr(self.block, "value") else self.block
+        return [block] + [self.moves[k].value for k in ("a", "b0", "b1", "c0", "c1", "c2", "c3")]
 
 
 def strips(columns):
@@ -310,7 +367,7 @@
             self.keep_from, self.send = args
             self.keep = rest[0]
 
-    def use(self, keep, send):
+    def use(self, keep, send, sums):
         self.keep, self.send = keep.at[:, self.at], send.at[:, self.at]
 
     def load(self):
@@ -380,14 +437,11 @@
         if i == self.turns[1]:
             self.third().wait()
             for at in strips(self.columns):
+                value = self.own[:, at] + self.got2[:, at].astype(f32)
                 for k in range(4):
-                    block = slice(k * self.size, (k + 1) * self.size)
-                    self.sums[k, :, at] = self.own[block, at]
-                whole_block = self.got2[:, at].astype(f32)
-                for k in range(4):
-                    value = self.sums[k, :, at] + whole_block[k * self.size : (k + 1) * self.size]
-                    self.sums[k, :, at] = value
-                    self.parts[k, :, at] = value.astype(bf16)
+                    block = value[k * self.size : (k + 1) * self.size]
+                    self.sums[k, :, at] = block
+                    self.parts[k, :, at] = block.astype(bf16)
             for copy in self.last():
                 copy.start()
         if i == self.turns[2]:
@@ -404,13 +458,86 @@
         self.value = got[0]
 
 
+class Third:
+    def __init__(self, away, own, turns):
+        self.turns = turns
+        r, columns = away.shape
+        self.columns, self.size = columns, r // 4
+        self.partners = ["a"]
+        self.args, self.specs = [away, own], [ANY, whole(r, columns)]
+        shape = (4, self.size, columns)
+        self.outs = [(sd(*shape, t=bf16), whole(*shape)), (sd(*shape), whole(*shape))]
+        self.scratch = [pltpu.VMEM((r, columns), bf16), DMA((2,))]
+
+    def bind(self, args, outs, scratch):
+        self.away, self.own = args
+        self.parts, self.sums = outs
+        self.got, self.sem = scratch
+
+    def copy(self):
+        return remote(self.away, self.got, self.sem.at[0], self.sem.at[1], "a")
+
+    def turn(self, i):
+        if i == self.turns[0]:
+            self.copy().start()
+        if i == self.turns[1]:
+            self.copy().wait()
+            for at in strips(self.columns):
+                value = self.own[:, at] + self.got[:, at].astype(f32)
+                for k in range(4):
+                    block = value[k * self.size : (k + 1) * self.size]
+                    self.sums[k, :, at] = block
+                    self.parts[k, :, at] = block.astype(bf16)
+
+    def done(self, got):
+        self.value = got
+
+
+class Final:
+    def __init__(self, parts, sums, turns):
+        self.turns = turns
+        _, self.size, self.columns = shape = parts.shape
+        self.partners = ["z1", "z2", "z3"]
+        self.args, self.specs = [parts, sums], [ANY, whole(*shape)]
+        self.outs = [(sd(*shape[1:]), whole(*shape[1:]))]
+        self.scratch = [pltpu.VMEM(shape, bf16), DMA((8,))]
+
+    def bind(self, args, outs, scratch):
+        self.parts, self.sums = args
+        self.out = outs[0]
+        self.got, self.sem = scratch
+
+    def copies(self):
+        near = Near()
+        return [
+            remote(self.parts.at[near.over(k)], self.got.at[near.z], self.sem.at[2 * k], self.sem.at[2 * k + 1], f"z{k}")
+            for k in (1, 2, 3)]
+
+    def turn(self, i):
+        if i == self.turns[0]:
+            for copy in self.copies():
+                copy.start()
+        if i == self.turns[1]:
+            for copy in self.copies():
+                copy.wait()
+            near = Near()
+            for at in strips(self.columns):
+                value = self.sums[near.z, :, at]
+                for k in (1, 2, 3):
+                    value = value + self.got[near.over(k), :, at].astype(f32)
+                self.out[:, at] = value
+
+    def done(self, got):
+        self.value = got[0]
+
+
 SMALL = 24
 
 
 class Total:
-    def __init__(self, sums, taps, turns):
+    def __init__(self, taps, turns):
         self.turns = turns
-        self.args = [sums, *taps]
+        self.args = list(taps)
         self.specs = [whole(*a.shape) for a in self.args]
         shape = (SMALL, D + 128)
         self.outs = [(sd(*shape), whole(*shape))]
@@ -418,8 +545,11 @@
         self.partners = ["core", "x", "y", "z1", "z2"]
 
     def bind(self, args, outs, scratch):
-        self.small, self.out = args, outs[0]
+        self.taps, self.out = args, outs[0]
         self.held, self.got, self.sem = scratch
+
+    def use(self, keep, send, sums):
+        self.sums = sums
 
     def copy(self, s):
         return remote(self.held.at[s], self.got.at[s], self.sem.at[2 * s], self.sem.at[2 * s + 1], self.partners[s])
@@ -435,9 +565,9 @@
                     else:
                         self.out[...] = value
                 else:
-                    self.held[0, :, 0:D] = self.small[0][...].T[0:SMALL, :]
-                    self.held[0, 0:HEADS, D:] = self.small[1][...]
-                    self.held[0, HEADS : 2 * HEADS, D:] = self.small[2][...]
+                    self.held[0, :, 0:D] = self.sums[...].T[0:SMALL, :]
+                    self.held[0, 0:HEADS, D:] = self.taps[0][...]
+                    self.held[0, HEADS : 2 * HEADS, D:] = self.taps[1][...]
                 if s < 5:
                     self.copy(s).start()
 
@@ -447,7 +577,7 @@
 
 CHUNK = 768
 STEPS = FF // CHUNK
-SUB = 256
+SUB = 768
 
 
 def flip(t, stride):
@@ -491,20 +621,33 @@
     call(kernel, "exchange", [], [], [], [], (), lanes, 0, 10_000_000)
 
 
-def project_kernel(n, p, x_ref, *rest, hook):
+def attention_kernel(sizes, p, x_ref, *rest, hook):
     if p:
         par_ref, *rest = rest
-    pieces, rest = rest[:n], rest[n:]
-    if p:
-        xl_ref, mix_ref, lm_ref, w_ref, sem = rest
-        loads = []
-    else:
-        xl_ref, mix_ref, lm_ref, par_ref, w_ref, sem, low_ref, low_sem = rest
-        loads = loader(pieces, low_ref, low_sem, (4 * D, 128))
-    loads += loader(pieces, w_ref, sem, (0, 3 * D))
+    conv_ref, *rest = rest
+    groups, rest = grouped(rest, sizes)
+    xl_out, mix_out, lm_ref, *rest = rest
+    if not p:
+        par_ref, *rest = rest
+    (ctx_out, f_out, b_out, a_ref, ns_out, small_ref, xhat_ref, rstd_ref,
+     w_ref, vpad_ref, z_ref, sem, xl_ref, mix_ref, ctx_ref, f_ref, b_ref, ns_ref, out_sem, ns_sem, *rest) = rest
+    leaving = []
+
+    def leave(src, dst):
+        copy = pltpu.make_async_copy(src, dst, out_sem.at[len(leaving)])
+        copy.start()
+        leaving.append(copy)
+
+    loads = column_loader(groups, sizes, w_ref, sem, 0, 4 * D)
+    if not p:
+        low_ref, low_sem = rest
+        loads += loader(groups[0], low_ref, low_sem, (sizes[0][1], 128))
     for copy in loads:
         copy.start()
     xl_ref[...] = x_ref[...].astype(bf16)
+    leave(xl_ref, xl_out)
+    vpad_ref[:, 0:LEAD] = jnp.zeros((D, LEAD), bf16)
+    vpad_ref[:, LEAD + T :] = jnp.zeros((D, LEAD), bf16)
     hook(0)
     for copy in loads:
         copy.wait()
@@ -513,42 +656,19 @@
     for part, column in ((0, p), (1, None), (2, p + 1)):
 
         def mix_step(i, _):
-            at = rows(part * D + i * 256, 256)
+            at = rows(part * D + i * 384, 384)
             got = dot(w_ref[:, at], xl_ref[...], TN)
             if column is not None:
-                got = got + par_ref[rows(i * 256, 256), column : column + 1]
+                got = got + par_ref[rows(i * 384, 384), column : column + 1]
             mix_ref[at, :] = got.astype(bf16)
             return 0
 
-        lax.fori_loop(0, 3, mix_step, 0)
+        lax.fori_loop(0, 2, mix_step, 0)
+        leave(mix_ref.at[pl.ds(part * D, D), :], mix_out.at[pl.ds(part * D, D), :])
         hook(part + 1)
+    vpad_ref[:, LEAD : LEAD + T] = mix_ref[2 * D :, :]
     lm_ref[...] = dot(mix_ref[0 : 2 * D, :], segment_mean(), NN).astype(bf16)
-    hook(4)
-
-
-def project(x, pieces, par, layer, lanes=(None, ())):
-    n = len(pieces)
-    first = layer == 0
-    got = call(
-        functools.partial(project_kernel, n, 8 * layer), "project",
-        [sd(D, T, t=bf16), sd(3 * D, T, t=bf16), sd(2 * D, LM, t=bf16)] + [sd(D, 128)] * first,
-        [vm()] + [vm()] * (not first) + anywhere(n), [vm()] * (3 + first),
-        [pltpu.VMEM((D, 3 * D), bf16), DMA((n,))] + [pltpu.VMEM((D, 128), bf16), DMA((n,))] * first,
-        (x, *([] if first else [par]), *pieces), lanes, 3_800_000_000, 14_000_000)
-    return got if first else [*got, par]
-
-
-def attend_kernel(n, p, x_ref, mix_ref, lm_ref, par_ref, conv_ref, *rest, hook):
-    pieces = rest[:n]
-    (ctx_ref, f_ref, b_ref, a_ref, ns_ref, small_ref, xhat_ref, rstd_ref,
-     w_ref, vpad_ref, z_ref, sem) = rest[n:]
-    loads = loader(pieces, w_ref, sem, (3 * D, D))
-    for copy in loads:
-        copy.start()
-    vpad_ref[:, 0:LEAD] = jnp.zeros((D, LEAD), bf16)
-    vpad_ref[:, LEAD + T :] = jnp.zeros((D, LEAD), bf16)
-    vpad_ref[:, LEAD : LEAD + T] = mix_ref[2 * D :, :]
-    hook(0)
+
     for h in range(HEADS):
         ql = lm_ref[h * HD : (h + 1) * HD, :]
         kl = lm_ref[D + h * HD : D + (h + 1) * HD, :]
@@ -577,10 +697,13 @@
             rs[h] = split(r3)
         for h in range(HEADS):
             z_ref[h] = 0.25 * dot3(split(z_ref[h]), rs[h], NN)
+        pltpu.make_async_copy(ns_ref.at[k], ns_out.at[k], ns_sem.at[k]).start()
         return 0
 
-    lax.fori_loop(0, NS_ITERS, ns_step, 0)
-    hook(1)
+    lax.fori_loop(0, NS_ITERS // 2, ns_step, 0)
+    hook(4)
+    lax.fori_loop(NS_ITERS // 2, NS_ITERS, ns_step, 0)
+    hook(5)
 
     def head_step(h, _):
         base = h * HD
@@ -608,107 +731,80 @@
         ctx_ref[rows(base, HD), :] = (attended + unstack_blocks(conv)).astype(bf16)
         return 0
 
-    lax.fori_loop(0, HEADS // 2, head_step, 0)
-    hook(2)
-    lax.fori_loop(HEADS // 2, HEADS, head_step, 0)
-    hook(3)
-    for copy in loads:
+    for third in range(3):
+        lax.fori_loop(third * 4, third * 4 + 4, head_step, 0, unroll=2)
+        at = pl.ds(third * 4 * HD, 4 * HD)
+        for src, dst in ((f_ref, f_out), (b_ref, b_out), (ctx_ref, ctx_out)):
+            leave(src.at[at, :], dst.at[at, :])
+        hook(6 + third)
+
+    def out_step(i, _):
+        at = rows(i * 384, 384)
+        got = dot(w_ref[:, rows(3 * D + i * 384, 384)], ctx_ref[...], TN)
+        xhat_ref[at, :] = got + par_ref[at, p + 2 : p + 3] + x_ref[at, :]
+        return 0
+
+    lax.fori_loop(0, 2, out_step, 0)
+    norm_forward(xhat_ref, xhat_ref, rstd_ref)
+    for copy in leaving:
         copy.wait()
-
-    def out_step(i, _):
-        base = i * 256
-        got = dot(w_ref[:, rows(base, 256)], ctx_ref[...], TN)
-        xhat_ref[rows(base, 256), :] = got + par_ref[rows(base, 256), p + 2 : p + 3] + x_ref[rows(base, 256), :]
-        return 0
-
-    lax.fori_loop(0, 3, out_step, 0)
-    norm_forward(xhat_ref, xhat_ref, rstd_ref)
-    hook(4)
-
-
-def attend(x, mix, lm, pieces, par, conv, layer, lanes=(None, ())):
-    n = len(pieces)
-    return call(
-        functools.partial(attend_kernel, n, 8 * layer), "attend",
-        [
+    for k in range(NS_ITERS):
+        pltpu.make_async_copy(ns_ref.at[k], ns_out.at[k], ns_sem.at[k]).wait()
+    hook(9)
+    hook(10)
+
+
+def attention(x, groups, par, conv, layer, lanes=(None, ())):
+    first = layer == 0
+    sizes = sizes_of(groups, layer)
+    n = sizes[0][0]
+    got = call(
+        functools.partial(attention_kernel, sizes, 8 * layer), "attention",
+        [sd(D, T, t=bf16), sd(3 * D, T, t=bf16), sd(2 * D, LM, t=bf16)] + [sd(D, 128)] * first
+        + [
             sd(D, T, t=bf16), sd(D, T, t=bf16), sd(D, T, t=bf16), sd(HEADS, LM, LM),
             sd(NS_ITERS, 4, HEADS, LM, LM), sd(3, HEADS, LM, LM), sd(D, T), sd(8, T),
         ],
-        [vm()] * 5 + anywhere(n), [vm()] * 8,
+        [vm()] * (2 if first else 3) + anywhere(n * len(groups)),
+        [ANY, ANY, vm()] + [vm()] * first + [ANY, ANY, ANY, vm(), ANY, vm(), vm(), vm()],
         [
-            pltpu.VMEM((D, D), bf16), pltpu.VMEM((D, T + 2 * LEAD), bf16), pltpu.VMEM((HEADS, LM, LM), f32),
-            pltpu.SemaphoreType.DMA((n,)),
-        ],
-        (x, mix, lm, par, conv, *pieces), lanes, 3_000_000_000, 30_000_000, trans=2_000_000)
-
-
-def up_kernel(n, p, xhat_ref, par_ref, inb_ref, *rest, hook):
-    pieces, (a_ref, g_ref, w_ref, hl_ref, sem) = rest[:n], rest[n:]
+            pltpu.VMEM((D, 4 * D), bf16), pltpu.VMEM((D, T + 2 * LEAD), bf16), pltpu.VMEM((HEADS, LM, LM), f32),
+            DMA((len(groups), n)), pltpu.VMEM((D, T), bf16), pltpu.VMEM((3 * D, T), bf16), pltpu.VMEM((D, T), bf16),
+            pltpu.VMEM((D, T), bf16), pltpu.VMEM((D, T), bf16), pltpu.VMEM((NS_ITERS, 4, HEADS, LM, LM), f32),
+            DMA((16,)), DMA((NS_ITERS,)),
+        ] + [pltpu.VMEM((D, 128), bf16), DMA((n,))] * first,
+        (x, *([] if first else [par]), conv, *[piece for g in groups for piece in g]), lanes,
+        6_800_000_000, 40_000_000, trans=2_000_000)
+    return got if first else [*got[:3], par, *got[3:]]
+
+
+def feed_kernel(n, p, last, xhat_ref, par_ref, inb_ref, *rest, hook):
+    pieces1, pieces2, rest = rest[:n], rest[n : 2 * n], rest[2 * n :]
+    a_ref, g_ref, xhat2_ref, rstd2_ref, next_ref, w1_ref, w2_ref, hl_ref, sem = rest
     j = pl.program_id(0)
 
     @pl.when(j == 0)
     def _():
-        loads = loader(pieces, w_ref, sem)
+        loads = loader(pieces1, w1_ref, sem.at[0])
         for copy in loads:
+            copy.start()
+        later = loader(pieces2, w2_ref, sem.at[1])
+        for copy in later:
             copy.start()
         hook(0)
         h = xhat_ref[...] * par_ref[:, p + 6 : p + 7] + par_ref[:, p + 3 : p + 4]
         hl_ref[...] = h.astype(bf16)
-        for copy in loads:
+        xhat2_ref[...] = h + par_ref[:, p + 4 : p + 5]
+        for copy in loads + later:
             copy.wait()
 
-    def up_step(i, _):
-        base = i * SUB
-        at = j * CHUNK + base
-        u = dot(w_ref[:, pl.ds(pl.multiple_of(at, SUB), SUB)], hl_ref[...], TN)
-        u = u + inb_ref[rows(at, SUB), 0:1]
-        cdf = 0.5 + 0.5 * lax.erf(u * (2.0 ** -0.5))
-        pdf = jnp.exp(-0.5 * u * u) * ((2.0 * np.pi) ** -0.5)
-        a_ref[rows(base, SUB), :] = (u * cdf).astype(bf16)
-        g_ref[rows(base, SUB), :] = (cdf + u * pdf).astype(bf16)
-        return 0
-
-    lax.fori_loop(0, CHUNK // SUB, up_step, 0)
-    for i in range(STEPS):
-
-        @pl.when(j == i)
-        def _():
-            hook(i + 1)
-
-
-def up(xhat, pieces, par, inb, layer, lanes=(None, ())):
-    n = len(pieces)
-    chunk = pl.BlockSpec((CHUNK, T), lambda j: (j, 0))
-    return call(
-        functools.partial(up_kernel, n, 8 * layer), "up",
-        [sd(FF, T, t=bf16), sd(FF, T, t=bf16)],
-        [whole(D, T), whole(D, 128), whole(FF, 1)] + anywhere(n), [chunk, chunk],
-        [pltpu.VMEM((D, FF), bf16), pltpu.VMEM((D, T), bf16), pltpu.SemaphoreType.DMA((n,))],
-        (xhat, par, inb, *pieces), lanes, 4_900_000_000, 24_000_000, (STEPS,), 6_000_000)
-
-
-def down_kernel(n, p, last, xhat_ref, par_ref, a_ref, *rest, hook):
-    pieces, (xhat2_ref, rstd2_ref, next_ref, w_ref, sem) = rest[:n], rest[n:]
-    j = pl.program_id(0)
-
-    @pl.when(j == 0)
-    def _():
-        loads = loader(pieces, w_ref, sem)
-        for copy in loads:
-            copy.start()
-        hook(0)
-        h = xhat_ref[...] * par_ref[:, p + 6 : p + 7] + par_ref[:, p + 3 : p + 4]
-        xhat2_ref[...] = h + par_ref[:, p + 4 : p + 5]
-        for copy in loads:
-            copy.wait()
-
-    def down_step(i, _):
-        base = i * SUB
-        xhat2_ref[rows(base, SUB), :] += dot(
-            w_ref[rows(j * CHUNK, CHUNK), pl.ds(pl.multiple_of(base, SUB), SUB)], a_ref[...], TN)
-        return 0
-
-    lax.fori_loop(0, D // SUB, down_step, 0)
+    u = dot(w1_ref[:, rows(j * CHUNK, CHUNK)], hl_ref[...], TN)
+    u = u + inb_ref[rows(j * CHUNK, CHUNK), 0:1]
+    cdf = 0.5 + 0.5 * lax.erf(u * (2.0 ** -0.5))
+    pdf = jnp.exp(-0.5 * u * u) * ((2.0 * np.pi) ** -0.5)
+    a_ref[...] = (u * cdf).astype(bf16)
+    g_ref[...] = (cdf + u * pdf).astype(bf16)
+    xhat2_ref[...] += dot(w2_ref[rows(j * CHUNK, CHUNK), :], a_ref[...], TN)
 
     @pl.when(j == STEPS - 1)
     def _():
@@ -718,6 +814,7 @@
             next_ref[...] = y.T.astype(bf16)
         else:
             next_ref[...] = y
+
     for i in range(STEPS):
 
         @pl.when(j == i)
@@ -725,16 +822,17 @@
             hook(i + 1)
 
 
-def down(xhat, a, pieces, par, layer, last, lanes=(None, ())):
-    n = len(pieces)
+def feed(xhat, pieces1, pieces2, par, inb, layer, last, lanes=(None, ())):
+    n = len(pieces1)
+    chunk = pl.BlockSpec((CHUNK, T), lambda j: (j, 0))
     next_shape = (T, D) if last else (D, T)
     return call(
-        functools.partial(down_kernel, n, 8 * layer, last), "down",
-        [sd(D, T), sd(8, T), sd(*next_shape, t=bf16 if last else f32)],
-        [whole(D, T), whole(D, 128), pl.BlockSpec((CHUNK, T), lambda j: (j, 0))] + anywhere(n),
-        [whole(D, T), whole(8, T), whole(*next_shape)],
-        [pltpu.VMEM((FF, D), bf16), pltpu.SemaphoreType.DMA((n,))],
-        (xhat, par, a, *pieces), lanes, 4_900_000_000, 24_000_000, (STEPS,))
+        functools.partial(feed_kernel, n, 8 * layer, last), "feed",
+        [sd(FF, T, t=bf16), sd(FF, T, t=bf16), sd(D, T), sd(8, T), sd(*next_shape, t=bf16 if last else f32)],
+        [whole(D, T), whole(D, 128), whole(FF, 1)] + anywhere(2 * n),
+        [chunk, chunk, whole(D, T), whole(8, T), whole(*next_shape)],
+        [pltpu.VMEM((D, FF), bf16), pltpu.VMEM((FF, D), bf16), pltpu.VMEM((D, T), bf16), DMA((2, n))],
+        (xhat, par, inb, *pieces1, *pieces2), lanes, 9_800_000_000, 40_000_000, (STEPS,), 6_000_000)
 
 
 def norm_backward(dy_ref, xhat_ref, rstd_ref, gain, out_ref, grads_ref, gain_col, shift_col, width=128):
@@ -886,33 +984,54 @@
         (sums, du, dr, xhat, rstd, par, *pieces), lanes, 9_700_000_000, 35_000_000, (STEPS,))
 
 
-def values_kernel(n, p, sums_in, dr1_ref, v_ref, ctx_ref, f_ref, b_ref, small_ref, conv_ref, *rest, hook):
-    order = Order(n)
-    pieces = rest[:n]
-    (keep_ref, send_ref, dctx_ref, dv_ref, dz_ref, dbv_ref, taps_ref, cols_ref,
-     w_ref, dp_ref, perm_ref, vpad_ref, dpad_ref, sem) = rest[n:]
-    loads = loader(pieces, w_ref, sem, (3 * D, D))
-    for copy in loads:
+def row_loader(src, dst, order, sem):
+    block = D // 8
+    return [
+        pltpu.make_async_copy(
+            src.at[rows(order.target(i) * block, block), :], dst.at[pl.ds(i * block, block), :], sem.at[i])
+        for i in range(8)]
+
+
+def values_kernel(sizes, p, sums_in, dr1_ref, mix_from, ctx_from, f_from, b_from, xl_from, small_ref, conv_ref,
+                  *rest, hook):
+    order = Order(sizes[0][0])
+    groups, rest = grouped(rest, sizes)
+    (keep_ref, send_ref, dctx_out, dv_ref, dz_ref, dbv_ref, taps_ref, cols_ref,
+     w_ref, dp_ref, perm_ref, vpad_ref, dpad_ref, dctx_ref, f_ref, b_ref, v_ref, xperm_ref,
+     sem, perm_sem, late_sem) = rest
+    early = column_loader(groups, sizes, w_ref, sem, 3 * D, 4 * D)
+    perms = row_loader(ctx_from, perm_ref, order, perm_sem.at[0])
+    late = [pltpu.make_async_copy(mix_from.at[pl.ds(2 * D, D), :], v_ref, late_sem.at[0]),
+            pltpu.make_async_copy(f_from, f_ref, late_sem.at[1]),
+            pltpu.make_async_copy(b_from, b_ref, late_sem.at[2])]
+    last = row_loader(xl_from, xperm_ref, order, perm_sem.at[1])
+    for copy in early + perms + late + last:
         copy.start()
     for ref in (vpad_ref, dpad_ref):
         ref[:, 0:LEAD] = jnp.zeros((D, LEAD), bf16)
         ref[:, LEAD + T :] = jnp.zeros((D, LEAD), bf16)
+    dp_ref[...] = dr1_ref[...].astype(bf16)
+    hook(0)
+    for copy in early:
+        copy.wait()
+
+    def dctx_step(i, _):
+        at = rows(i * 384, 384)
+        got = dot(w_ref[at, :], dp_ref[...], NN).astype(bf16)
+        dctx_ref[at, :] = got
+        dpad_ref[at, LEAD : LEAD + T] = got
+        return 0
+
+    lax.fori_loop(0, 2, dctx_step, 0)
+    leave = pltpu.make_async_copy(dctx_ref, dctx_out, late_sem.at[3])
+    leave.start()
+    for copy in perms:
+        copy.wait()
+    for i, ref in enumerate((keep_ref, send_ref)):
+        ref[:, 0:D] = dot(perm_ref[i * (D // 2) : (i + 1) * (D // 2), :], dp_ref[...], NT).astype(bf16)
+    for copy in late:
+        copy.wait()
     vpad_ref[:, LEAD : LEAD + T] = v_ref[...]
-    dp_ref[...] = dr1_ref[...].astype(bf16)
-    permute_rows(perm_ref, ctx_ref, order, D // 8)
-    hook(0)
-    for i, ref in enumerate((keep_ref, send_ref)):
-        ref[...] = dot(perm_ref[i * (D // 2) : (i + 1) * (D // 2), :], dp_ref[...], NT).astype(bf16)
-    for copy in loads:
-        copy.wait()
-
-    def dctx_step(i, _):
-        got = dot(w_ref[rows(i * SUB, SUB), :], dp_ref[...], NN).astype(bf16)
-        dctx_ref[rows(i * SUB, SUB), :] = got
-        dpad_ref[rows(i * SUB, SUB), LEAD : LEAD + T] = got
-        return 0
-
-    lax.fori_loop(0, D // SUB, dctx_step, 0)
     hook(1)
     flip = jnp.where(
         lax.broadcasted_iota(jnp.int32, (CONV_N, CONV_N), 0)
@@ -935,44 +1054,83 @@
         taps_ref[pl.ds(h, 1), :] = jnp.sum(g[:, 0:128], axis=0, keepdims=True)
         return 0
 
-    lax.fori_loop(0, HEADS // 2, value_step, 0)
+    lax.fori_loop(0, HEADS // 2, value_step, 0, unroll=2)
     hook(2)
-    lax.fori_loop(HEADS // 2, HEADS, value_step, 0)
+    lax.fori_loop(HEADS // 2, HEADS, value_step, 0, unroll=2)
+    hook(3)
+    for copy in last:
+        copy.wait()
+    for i, ref in enumerate((keep_ref, send_ref)):
+        ref[:, D:] = dot(xperm_ref[i * (D // 2) : (i + 1) * (D // 2), :], dv_ref[...], NT).astype(bf16)
     cols_ref[...] = sums_in[...]
     cols_ref[:, p + 1 : p + 2] = lane_sum(dv_ref[...])
-    hook(3)
+    leave.wait()
     hook(4)
 
 
-def values(sums, dr1, mix, ctx, f, b, small, conv, pieces, layer, lanes=(None, ())):
-    n = len(pieces)
+def values(sums, dr1, mix, ctx, f, b, xl, small, conv, groups, layer, lanes=(None, ())):
+    sizes = sizes_of(groups, layer)
+    n = sizes[0][0]
     return call(
-        functools.partial(values_kernel, n, 8 * layer), "values",
+        functools.partial(values_kernel, sizes, 8 * layer), "values",
         [
-            sd(D // 2, D, t=bf16), sd(D // 2, D, t=bf16), sd(D, T, t=bf16), sd(D, T, t=bf16),
+            sd(D // 2, 2 * D, t=bf16), sd(D // 2, 2 * D, t=bf16), sd(D, T, t=bf16), sd(D, T, t=bf16),
             sd(HEADS, LM, LM), sd(HEADS, LM, LM, t=bf16), sd(HEADS, 128), sd(D, 128),
         ],
-        [whole(D, 128), whole(D, T), pl.BlockSpec((D, T), lambda *_: (2, 0)), whole(D, T), whole(D, T), whole(D, T),
-         whole(*small.shape), whole(*conv.shape)] + anywhere(n),
-        [whole(D // 2, D), whole(D // 2, D), whole(D, T), whole(D, T), whole(HEADS, LM, LM), whole(HEADS, LM, LM),
-         whole(HEADS, 128), whole(D, 128)],
+        [vm(), vm()] + [ANY] * 5 + [vm(), vm()] + anywhere(n * len(groups)),
+        [vm(), vm(), ANY] + [vm()] * 5,
         [
             pltpu.VMEM((D, D), bf16), pltpu.VMEM((D, T), bf16), pltpu.VMEM((D, T), bf16),
-            pltpu.VMEM((D, T + 2 * LEAD), bf16), pltpu.VMEM((D, T + 2 * LEAD), bf16), pltpu.SemaphoreType.DMA((n,)),
-        ],
-        (sums, dr1, mix, ctx, f, b, small, conv, *pieces), lanes, 5_000_000_000, 25_000_000, (1,))
-
-
-def scores_kernel(p, sums_in, mix_ref, dctx_ref, f_ref, b_ref, lm_ref, a_ref, ns_ref, small_ref, dz0_ref, dbv_ref,
-                  dqk_ref, cols_ref, dz_ref, da_ref, *, hook):
+            pltpu.VMEM((D, T + 2 * LEAD), bf16), pltpu.VMEM((D, T + 2 * LEAD), bf16),
+        ] + [pltpu.VMEM((D, T), bf16)] * 5 + [DMA((len(groups), n)), DMA((2, 8)), DMA((4,))],
+        (sums, dr1, mix, ctx, f, b, xl, small, conv, *[piece for g in groups for piece in g]), lanes,
+        6_200_000_000, 25_000_000)
+
+
+QK = 2 * D
+TURNS = 20
+
+
+def back_kernel(sizes, p, out, tail, sums_in, ns_from, mix_from, dctx_from, f_from, b_from, dv_from, xl_from, dr1_from,
+                lm_ref, a_ref, small_ref, dz0_ref, dbv_ref, *rest, hook):
+    order = Order(sizes[0][0])
+    groups, rest = grouped(rest, sizes)
+    if out:
+        keep_ref, send_ref, *rest = rest
+    dx_ref, cols_ref, *rest = rest
+    if not out:
+        keep_ref, send_ref, *rest = rest
+    (w_ref, ns_ref, mix_ref, dctx_ref, f_ref, b_ref, dv_ref, perm_ref, dr1_ref, dz_ref, da_ref,
+     sem, ns_sem, late_sem, perm_sem) = rest
+
+    def load_ns(i):
+        return pltpu.make_async_copy(
+            ns_from.at[NS_ITERS - 1 - i], ns_ref.at[lax.rem(i, 2)], ns_sem.at[lax.rem(i, 2)])
+
+    load_ns(0).start()
+    late = [
+        pltpu.make_async_copy(src, dst, late_sem.at[i]) for i, (src, dst) in enumerate((
+            (mix_from, mix_ref), (dctx_from, dctx_ref), (f_from, f_ref), (b_from, b_ref), (dv_from, dv_ref),
+            (dr1_from, dr1_ref)))]
+    late += row_loader(xl_from, perm_ref, order, perm_sem)
+    late += column_loader(groups, sizes, w_ref, sem, 0, 3 * D)
+    for lane in tail:
+        lane.use(keep_ref, send_ref, cols_ref)
+    for copy in late:
+        copy.start()
     hook(0)
-    spread = segment_spread()
     for h in range(HEADS):
         da_ref[h] = jnp.zeros((LM, LM), f32)
         dz_ref[h] = dz0_ref[h]
 
     def ns_step(i, _):
-        k = NS_ITERS - 1 - i
+        k = lax.rem(i, 2)
+        load_ns(i).wait()
+
+        @pl.when(i + 1 < NS_ITERS)
+        def _():
+            load_ns(i + 1).start()
+
         d3, dzs, dps, d2 = [], [], [], []
         for h in range(HEADS):
             dzn = split(0.25 * dz_ref[h])
@@ -995,7 +1153,10 @@
     lax.fori_loop(0, NS_ITERS // 2, ns_step, 0)
     hook(1)
     lax.fori_loop(NS_ITERS // 2, NS_ITERS, ns_step, 0)
+    for copy in late:
+        copy.wait()
     hook(2)
+    spread = segment_spread()
 
     def score_step(h, _):
         base = h * HD
@@ -1018,72 +1179,56 @@
         dql = dot(kl, dsa, NT) + dot(k, dsb, NT)
         dq = dot(kl, dsf, NN) + dot((dql * (1.0 / SEG)).astype(bf16), spread, NN)
         dk = dot(ql, dsb, NN) + dot((dkl * (1.0 / SEG)).astype(bf16), spread, NN)
-        dqk_ref[rows(base, HD), :] = dq.astype(bf16)
-        dqk_ref[rows(D + base, HD), :] = dk.astype(bf16)
+        mix_ref[rows(base, HD), :] = dq.astype(bf16)
+        mix_ref[rows(D + base, HD), :] = dk.astype(bf16)
         return 0
 
-    lax.fori_loop(0, HEADS // 2, score_step, 0)
-    hook(3)
-    lax.fori_loop(HEADS // 2, HEADS, score_step, 0)
+    half = D // 2
+    for part in range(2):
+        for quarter in range(2):
+            start = (2 * part + quarter) * (HEADS // 4)
+            lax.fori_loop(start, start + HEADS // 4, score_step, 0)
+            if quarter == 0:
+                hook(3 + 2 * part)
+        for side, ref in ((1, send_ref), (0, keep_ref)):
+            mine = perm_ref[side * half : (side + 1) * half, :]
+            for k in range(2):
+                at = part * D + k * half
+                d = mix_ref[k * D + part * half : k * D + (part + 1) * half, :]
+                ref[:, at : at + half] = dot(mine, d, NT).astype(bf16)
+        hook(4 + 2 * part)
     cols_ref[...] = sums_in[...]
-    cols_ref[:, p : p + 1] = lane_sum(dqk_ref[0:D, :])
-    hook(4)
-
-
-def scores(sums, mix, dctx, f, b, lm, a, ns, small, dz0, dbv, layer, lanes=(None, ())):
-    return call(
-        functools.partial(scores_kernel, 8 * layer), "scores", [sd(2 * D, T, t=bf16), sd(D, 128)], [vm()] * 11,
-        [vm()] * 2, [pltpu.VMEM((HEADS, LM, LM), f32), pltpu.VMEM((HEADS, LM, LM), f32)],
-        (sums, mix, dctx, f, b, lm, a, ns, small, dz0, dbv), lanes, 3_000_000_000, 30_000_000)
-
-
-def inputs_kernel(n, first, tail, dr1_ref, xl_ref, dqk_ref, dv_ref, *rest, hook):
-    order = Order(n)
-    pieces, (keep_ref, send_ref, dx_ref, w_ref, perm_ref, sem) = rest[:n], rest[n:]
-    loads = loader(pieces, w_ref, sem, (0, 3 * D))
-    for copy in loads:
-        copy.start()
-    permute_rows(perm_ref, xl_ref, order, D // 8)
-    for lane in tail:
-        lane.use(keep_ref, send_ref)
-    hook(0)
+    cols_ref[:, p : p + 1] = lane_sum(mix_ref[0:D, :])
     for i in range(3):
-        d = dqk_ref[i * D : (i + 1) * D, :] if i < 2 else dv_ref[...]
-        for part, ref in enumerate((send_ref, keep_ref)):
-            mine = perm_ref[(1 - part) * (D // 2) : (2 - part) * (D // 2), :]
-            ref[:, i * D : (i + 1) * D] = dot(mine, d, NT).astype(bf16)
-        hook(i + 1)
-    for copy in loads:
-        copy.wait()
-
-    def dx_step(i, _):
-        at = rows(i * SUB, SUB)
-        got = dr1_ref[at, :] + dot(w_ref[at, 0 : 2 * D], dqk_ref[...], NN)
-        got = got + dot(w_ref[at, 2 * D :], dv_ref[...], NN)
-        if first:
+        at = slice(i * 256, (i + 1) * 256)
+        got = dr1_ref[at, :] + dot(w_ref[at, 0:QK], mix_ref[0:QK, :], NN) + dot(w_ref[at, QK:], dv_ref[...], NN)
+        if p:
+            dx_ref[at, :] = got
+        else:
             dx_ref[:, at] = got.T
-        else:
-            dx_ref[at, :] = got
-        return 0
-
-    for i in range(D // SUB):
-        dx_step(i, 0)
-        hook(i + 4)
-    for i in range(7, TURNS):
+        hook(7 + i)
+    for i in range(10, TURNS):
         hook(i)
 
 
-TURNS = 16
-
-
-def inputs(dr1, xl, dqk, dv, pieces, first, lanes=(None, ()), tail=()):
-    n = len(pieces)
-    return call(
-        functools.partial(inputs_kernel, n, first, tail), "inputs",
-        [sd(D // 2, 3 * D, t=bf16), sd(D // 2, 3 * D, t=bf16), sd(*((T, D) if first else (D, T)))],
-        [vm()] * 4 + anywhere(n), [vm()] * 3,
-        [pltpu.VMEM((D, 3 * D), bf16), pltpu.VMEM((D, T), bf16), pltpu.SemaphoreType.DMA((n,))],
-        (dr1, xl, dqk, dv, *pieces), lanes, 7_400_000_000, 25_000_000)
+def back(sums, ns, mix, dctx, f, b, dv, xl, dr1, lm, a, small, dz0, dbv, groups, layer, lanes=(None, ()), tail=(), on=False):
+    sizes = sizes_of(groups, layer)
+    n = sizes[0][0]
+    halves = [(D // 2, QK)] * 2
+    out = 0 if on and layer == 0 else 1
+    got = call(
+        functools.partial(back_kernel, sizes, 8 * layer, out, tail), "back",
+        [sd(*h, t=bf16) for h in halves] * out + [sd(*((D, T) if layer else (T, D))), sd(D, 128)],
+        [vm()] + [ANY] * 8 + [vm()] * 5 + anywhere(n * len(groups)), [vm()] * (2 + 2 * out),
+        [pltpu.VMEM(h, bf16) for h in halves] * (1 - out) + [
+            pltpu.VMEM((D, 3 * D), bf16), pltpu.VMEM((2, 4, HEADS, LM, LM), f32), pltpu.VMEM((3 * D, T), bf16),
+        ] + [pltpu.VMEM((D, T), bf16)] * 5 + [
+            pltpu.VMEM((D, T), f32), pltpu.VMEM((HEADS, LM, LM), f32), pltpu.VMEM((HEADS, LM, LM), f32),
+            DMA((len(groups), n)), DMA((2,)), DMA((6,)), DMA((8,)),
+        ],
+        (sums, ns, mix, dctx, f, b, dv, xl, dr1, lm, a, small, dz0, dbv, *[piece for g in groups for piece in g]),
+        lanes, 10_000_000_000, 50_000_000)
+    return got if out else [None, None, *got]
 
 
 class Ring:
@@ -1268,172 +1413,152 @@
         return (self.count, list(lanes))
 
 
-def pieces_of(block, a, b, c):
-    return [block, a.value] + [m.value for m in b] + [m.value for m in c]
-
-
 def body(ring, tokens, cotangent, qkv_w, out_w, in_w, in_b, out2_w, bias_rows, gain_rows, conv_w):
     layers = qkv_w.shape[0]
     size = qkv_w.shape[1]
     small = small_shard(in_b, bias_rows, gain_rows)
-    shards = [
-        jnp.concatenate([qkv_w[layer], out_w[layer]] + ([small] if layer == 0 else []), axis=1)
-        for layer in range(layers)]
     plan = Plan()
     none = (None, ())
     on = ring.exact and layers == 2
     x = tokens.T.astype(f32)
     conv = [conv_rows(conv_w[layer]) for layer in range(layers)]
-    lanes = {name: [none] * layers for name in ("project", "attend", "up", "down")}
-
+    on_attention, on_feed = [none] * layers, [none] * layers
+    qkvo = [jnp.concatenate([qkv_w[layer], out_w[layer]], axis=1) for layer in range(layers)]
     if on:
-        spread = Spread(shards[0], 0, 1)
-        exchange(plan.lanes(spread), 2)
-        u1 = spread.value
-        a1 = Move(u1, "a", 0, 1)
-        b1 = [Move(u1, "b", 1, 2), Move(a1, "b", 1, 2)]
-        c1 = [Move(u1, "core", 0, 3), Move(a1, "core", 1, 3)] + [Move(b, "core", 2, 3) for b in b1]
-        s2, s3 = Spread(in_w[0], 0, 3), Spread(out2_w[0], 0, 3)
-        exchange(plan.lanes(a1, *b1, *c1, s2, s3), 4)
-        att = [pieces_of(u1, a1, b1, c1), None]
-        win, wout = [None, None], [None, None]
+        s1 = Spread(jnp.concatenate([qkvo[0][:, : 2 * D], small], axis=1), 0, 1)
+        s2 = Spread(qkvo[0][:, 2 * D :], 1, 3)
+        g1, g2 = Gather(s1), Gather(s2)
+        s3 = Spread(in_w[0], 3, 8)
+        m1 = g1.go(a=(1, 2), b=(2, 4), core0=(1, 8), core1=(2, 8), core2=(4, 8))
+        m2 = g2.go(a=(3, 5), b=(5, 7), core0=(3, 8), core1=(5, 8), core2=(7, 8))
+        exchange(plan.lanes(s1, s2, *m1, *m2, s3), 9)
+        att = [[g1.pieces(), g2.pieces()], None]
+        win, wout = [None] * 2, [None] * 2
+        g3 = Gather(s3)
+        s4, s5 = Spread(out2_w[0], 0, 4), Spread(qkvo[1], 4, 9)
+        g4 = Gather(s4)
+        m3 = g3.go(a=(0, 2), b=(2, 6), core0=(0, 3), core1=(2, 5), core2=(6, 9))
+        m4 = g4.go(a=(4, 6), b=(6, 9), core0=(4, 7), core1=(6, 9), core2=(9, 10))
+        on_attention[0] = plan.lanes(s4, *m3, *m4, s5)
     else:
+        shards = [jnp.concatenate([qkvo[0], small], axis=1)] + qkvo[1:]
         att, win, wout = gather_all(ring, shards, in_w, out2_w)
+        att = [[pieces] for pieces in att]
 
     kept = []
     par = None
     for layer in range(layers):
         final = layer == layers - 1
+        xl, mix, lm, par, ctx, f, b, a, ns, sm, xhat1, rstd1 = attention(
+            x, att[layer], par, conv[layer], layer, on_attention[layer])
         if on and layer == 0:
-            u2, u3 = s2.value, s3.value
-            a2, a3 = Move(u2, "a", 0, 4), Move(u3, "a", 0, 4)
-            c2, c3 = [Move(u2, "core", 0, 4)], [Move(u3, "core", 0, 4)]
-            lanes["project"][0] = plan.lanes(a2, c2[0], a3, c3[0])
+            win[0], wout[0] = g3.pieces(), g4.pieces()
+            s6, s7 = Spread(in_w[1], 0, 2), Spread(out2_w[1], 2, 4)
+            g5, g6, g7 = Gather(s5), Gather(s6), Gather(s7)
+            m5 = g5.go(a=(0, 1), b=(1, 3), core0=(0, 1), core1=(1, 3), core2=(3, 4))
+            m6 = g6.go(a=(3, 4))
+            on_feed[0] = plan.lanes(*m5, s6, s7, *m6)
         if on and layer == 1:
-            b5 = [Move(u5, "b", 0, 4), Move(a5.value, "b", 0, 4)]
-            c5 = [Move(u5, "core", 0, 4), Move(a5.value, "core", 0, 4)]
-            lanes["project"][1] = plan.lanes(*b5, *c5)
-        xl, mix, lm, par = project(x, att[layer], par, layer, lanes["project"][layer])
-        if on and layer == 0:
-            b2 = [Move(u2, "b", 0, 1), Move(a2.value, "b", 0, 1)]
-            b3 = [Move(u3, "b", 1, 3), Move(a3.value, "b", 1, 3)]
-            c2 += [Move(a2.value, "core", 0, 1)] + [Move(b, "core", 1, 4) for b in b2]
-            c3 += [Move(a3.value, "core", 0, 1)] + [Move(b, "core", 3, 4) for b in b3]
-            s4 = Spread(shards[1], 0, 4)
-            lanes["attend"][0] = plan.lanes(*b2, *b3, *c2[1:], *c3[1:], s4)
-        if on and layer == 1:
-            b6 = [Move(u6, "b", 0, 2), Move(a6.value, "b", 0, 2)]
-            c6 = [Move(u6, "core", 0, 1), Move(a6.value, "core", 0, 1)] + [Move(b, "core", 2, 4) for b in b6]
-            c5 += [Move(b.value, "core", 0, 4) for b in b5]
-            lanes["attend"][1] = plan.lanes(*b6, *c6, *c5[2:])
-        ctx, f, b, a, ns, sm, xhat1, rstd1 = attend(
-            x, mix, lm, att[layer], par, conv[layer], layer, lanes["attend"][layer])
-        if on and layer == 0:
-            win[0], wout[0] = pieces_of(u2, a2, b2, c2), pieces_of(u3, a3, b3, c3)
-            u4 = s4.value
-            a4 = Move(u4, "a", 0, 1)
-            b4 = [Move(u4, "b", 1, 4), Move(a4, "b", 1, 4)]
-            c4 = [Move(u4, "core", 0, 1), Move(a4, "core", 1, 4)]
-            s5, s6 = Spread(in_w[1], 0, 4), Spread(out2_w[1], 0, 4)
-            lanes["up"][0] = plan.lanes(a4, *b4, *c4, s5, s6)
-        if on and layer == 1:
-            win[1], wout[1] = pieces_of(u5, a5, b5, c5), pieces_of(u6, a6, b6, c6)
+            win[1], wout[1] = g6.pieces(), g7.pieces()
         at = 8 * layers + FF // D * layer
         inb = par[:, at : at + FF // D].reshape(FF, 1)
-        act, slope = up(xhat1, win[layer], par, inb, layer, lanes["up"][layer])
+        act, slope, xhat2, rstd2, x = feed(
+            xhat1, win[layer], wout[layer], par, inb, layer, final, on_feed[layer])
         if on and layer == 0:
-            c4 += [Move(b.value, "core", 0, 4) for b in b4]
-            u5, u6 = s5.value, s6.value
-            a5, a6 = Move(u5, "a", 0, 4), Move(u6, "a", 0, 4)
-            lanes["down"][0] = plan.lanes(*c4[2:], a5, a6)
-        xhat2, rstd2, x = down(xhat1, act, wout[layer], par, layer, final, lanes["down"][layer])
-        if on and layer == 0:
-            att[1] = pieces_of(u4, a4, b4, c4)
+            att[1] = [g5.pieces()]
+            m6 = g6.go(b=(0, 4), core0=(0, 3), core1=(0, 3), core2=(4, 9))
+            m7 = g7.go(a=(0, 2), b=(4, 8), core0=(0, 3), core1=(2, 5), core2=(8, 10))
+            on_attention[1] = plan.lanes(*m6, *m7)
         kept.append((xl, mix, lm, ctx, f, b, a, ns, sm, xhat1, rstd1, act, slope, xhat2, rstd2))
     output = x
 
     dy = cotangent
     sums = jnp.zeros((D, 128), f32)
     taps = [None] * layers
-    grads = [[None] * 4 for _ in range(layers)]
-    waiting = []
-
-    def sum_first(keep, send, turns, layer, place, **more):
-        lane = ReduceFirst(keep, send, turns, **more)
-        waiting.append((lane, layer, place))
+    grads = [{} for _ in range(layers)]
+    firsts, thirds, ends = {}, {}, []
+
+    def sum_first(keep, send, turns, layer, place):
+        firsts[layer, place] = ReduceFirst(keep, send, turns)
+        return firsts[layer, place]
+
+    def sum_third(layer, place, turns):
+        thirds[layer, place] = Third(*firsts[layer, place].value, turns)
+        return thirds[layer, place]
+
+    def ending(lane, layer, place):
+        ends.append((lane, layer, place))
         return lane
 
-    def sum_last(turns, chained=False):
-        lane, layer, place = waiting.pop(0)
-        if chained:
-            last = ReduceLast(None, None, turns, inside=lane)
-        else:
-            last = ReduceLast(*lane.value, turns)
-        ends.append((last, layer, place))
-        return last
-
-    ends = []
+    def sum_final(layer, place, turns):
+        return ending(Final(*thirds[layer, place].value, turns), layer, place)
+
+    def sum_last(layer, place, turns):
+        return ending(ReduceLast(*firsts[layer, place].value, turns), layer, place)
+
     halves = None
     for layer in reversed(range(layers)):
         xl, mix, lm, ctx, f, b, a, ns, sm, xhat1, rstd1, act, slope, xhat2, rstd2 = kept[layer]
-        lane = plan.lanes(sum_first(*halves, (0, 1, 4), 1, 0)) if on and halves else none
+        above = layer + 1 < layers
+        lane = none
+        if on and above:
+            lane = plan.lanes(sum_first(*halves, (0, 1, 4), layer + 1, "qk"), sum_last(layer + 1, "ov", (0, 1, 4)))
         keep, send, du, dr2, sums = hidden(
-            sums, dy, xhat2, rstd2, par, act, slope, wout[layer], layer, layer == layers - 1, lane)
+            sums, dy, xhat2, rstd2, par, act, slope, wout[layer], layer, not above, lane)
         if on:
-            out2 = (keep.reshape(-1, D), send.reshape(-1, D))
-            lane = [sum_last((0, 1, 4))] if waiting else []
-            lane = plan.lanes(*lane, sum_first(*out2, (0, 1, 4), layer, 3))
+            lane = [sum_first(keep.reshape(-1, D), send.reshape(-1, D), (0, 1, 4), layer, "out2")]
+            lane += [sum_last(layer + 1, "qk", (0, 1, 4))] if above else []
+            lane = plan.lanes(*lane)
         else:
-            keep, send = natural_halves(keep, send)
-            grads[layer][3] = ring.sum(keep, send)
+            grads[layer]["out2"] = ring.sum(*natural_halves(keep, send))
         keep, send, dr1, sums = inner(sums, du, dr2, xhat1, rstd1, par, win[layer], layer, lane)
         if on:
-            lane = plan.lanes(sum_last((0, 1, 4)), sum_first(keep, send, (0, 1, 4), layer, 2))
+            lane = plan.lanes(sum_third(layer, "out2", (0, 1)), sum_first(keep, send, (0, 1, 4), layer, "in"))
         else:
-            grads[layer][2] = ring.sum(keep, send)
+            grads[layer]["in"] = ring.sum(keep, send)
         keep, send, dctx, dv, dz, dbv, taps[layer], sums = values(
-            sums, dr1, mix, ctx, f, b, sm, conv[layer], att[layer], layer, lane)
+            sums, dr1, mix, ctx, f, b, xl, sm, conv[layer], att[layer], layer, lane)
+        tail = []
         if on:
-            last = sum_last((0, 1, 4))
-            lead = sum_first(keep, send, (0, 1, 2), layer, 1, chained=True)
-            lane = plan.lanes(last, lead, sum_last((2, 3, 4), chained=True))
+            lane = [sum_final(layer, "out2", (0, 2)), sum_last(layer, "in", (0, 1, 6))]
+            if layer:
+                lane.append(sum_first(keep, send, (0, 1, 3), layer, "ov"))
+            else:
+                lead = ReduceFirst(keep, send, (0, 1, 3), chained=True)
+                lane += [lead, ending(ReduceLast(None, None, (3, 4, 10), inside=lead), 0, "ov")]
+                for part, (go, end) in enumerate((((4, 5, 7), (7, 9, 12)), ((6, 7, 9), (9, 11, 13)))):
+                    lead = ReduceFirst(None, None, go, chained=True, columns=slice(part * D, (part + 1) * D))
+                    tail.append(lead)
+                    lane += [lead, ending(ReduceLast(None, None, end, inside=lead), 0, f"qk{part}")]
+                total = Total(taps, (7, 8, 9, 10, 11, 12))
+                tail.append(total)
+                lane.append(total)
+            lane = plan.lanes(*lane)
         else:
-            grads[layer][1] = ring.sum(keep, send)
-        dqk, sums = scores(sums, mix, dctx, f, b, lm, a, ns, sm, dz, dbv, layer, lane)
-        tail = []
-        if on and layer == 0:
-            turns = [(1, 4, 7), (2, 5, 9), (3, 6, 11)]
-            lane = []
-            for part in range(3):
-                lead = ReduceFirst(
-                    None, None, turns[part], chained=True, columns=slice(part * D, (part + 1) * D))
-                after = turns[part][2]
-                last = ReduceLast(None, None, (after, after + 2, after + 4), inside=lead)
-                tail.append(lead)
-                ends.append((last, 0, part))
-                lane += [lead, last]
-            total = Total(sums, taps, (0, 1, 2, 3, 4, 5))
-            lane = plan.lanes(*lane, total)
-        else:
-            lane = none
-        keep, send, dy = inputs(dr1, xl, dqk, dv, att[layer], layer == 0, lane, tuple(tail))
+            grads[layer]["ov"] = ring.sum(keep, send)
+        keep, send, dy, sums = back(
+            sums, ns, mix, dctx, f, b, dv, xl, dr1, lm, a, sm, dz, dbv, att[layer], layer, lane, tuple(tail), on)
         halves = (keep, send)
         if not on:
-            grads[layer][0] = ring.sum(keep, send)
+            grads[layer]["qk"] = ring.sum(keep, send)
     if on:
-        qkv = [None] * 3
         for lane, layer, place in ends:
-            if layer == 0 and lane.columns == D and lane.inside is not None and lane.inside.at is not None:
-                qkv[place] = lane.value
-            else:
-                grads[layer][place] = lane.value
-        grads[0][0] = jnp.concatenate(qkv, axis=1)
+            grads[layer][place] = lane.value
+        grads[0]["qk"] = jnp.concatenate([grads[0]["qk0"], grads[0]["qk1"]], axis=1)
         total = total.value
     else:
         flat = jnp.concatenate([sums.T[:SMALL], jnp.concatenate(taps, axis=0)], axis=1)
         total = ring.total(flat)
     gbias, ggain, ginb, gtaps = small_outputs(ring, total, size, in_b.shape[1])
-    stacked = [jnp.stack([grads[layer][i] for layer in range(layers)]) for i in range(4)]
+    half = D // 2
+    stacked = [
+        jnp.stack([
+            jnp.concatenate([
+                g["qk"][:, :half], g["qk"][:, D : D + half], g["qk"][:, half:D], g["qk"][:, D + half :],
+                g["ov"][:, D:]], axis=1) for g in grads]),
+        jnp.stack([g["ov"][:, :D] for g in grads]),
+        jnp.stack([g["in"] for g in grads]),
+        jnp.stack([g["out2"] for g in grads])]
     return (output, dy, stacked[0], stacked[1], stacked[2], ginb, stacked[3], gbias, ggain, gtaps)
 
 

time: 628 us -> 536 us (0.85)
  Pallas kernels: 592 us -> 497 us
    pallas_call x20 -> x13, Pallas kernels: 592 us -> 497 us  [call(): pl.pallas_call(run, out_shape=list(out_shape) + [o for o, _ in lane_outs]...]
where the time goes in v3:
time: 536 us; the launch traced here: 527 us
  Pallas kernels  497 us (93%)
  local copies, waits for them, and re-layouts  18.7 us (3%)
  other arithmetic  9.71 us (2%)
    pallas_call x13, Pallas kernels, call(): pl.pallas_call(run, out_shape=list(out_shape) + [o for o, _ in lane_outs]...  497 us

profile of v3, /device:TPU:0, one launch (start us, length us, event | category | flops | bytes accessed | tf_op | source)
XLA Modules:
  0.0 526.9 jit_solution(6807433524983384078)
XLA Ops:
  0.6 1.7 copy.43
  2.4 0.0 copy-start.11
  2.4 0.0 copy-start.14
  2.4 0.0 copy-start.12
  2.4 0.0 copy-start.13
  2.4 0.0 copy-start.10
  2.4 0.0 copy-start.6
  2.4 0.0 copy-start.1
  2.4 2.1 convert_bitcast_fusion.refs_0_
  4.5 0.0 copy-done.11
  4.5 0.1 rev.6
  4.7 0.7 fusion.1.refs_1_.refs_8_
  5.4 0.0 copy-done.14
  5.4 0.1 reshape.144
  5.5 0.1 copy.48
  5.6 0.1 copy.50
  5.7 0.0 copy-done.12
  5.7 0.1 copy.49
  5.8 0.1 fusion.4
  5.9 0.0 copy-done.10
  5.9 0.0 copy-done.6
  5.9 0.6 pad_maximum_fusion.6
  6.6 0.6 pad_maximum_fusion.5.refs_0_
  7.2 0.7 slice_bitcast_fusion.1
  8.0 41.5 %exchange.1 = (bf16[4,24,1664]{2,1,0:T(8,128)(2,1)}, bf16[4,24,1536]{2,1,0:T(8,128)(2,1)}, bf16[4,24,1664]{2,1,0:T(8,128)(2,1)}, bf16[4,24,1664]{2,1,0:T(8,128)(...) custom-call(bf16[24,1664]{1,0:T(8,128)(2,1)} %pad_maximum_fusion.5.r, ...), custom_call_target="tpu_custom_call" | custom-call | bytes 10000000 | tf_op jit(solution)/shard_map/exchange/pallas_call | solution.py:191
  49.5 0.7 slice_bitcast_fusion
  50.2 0.7 pad_maximum_fusion.3.refs_22_
  50.9 59.0 %attention.2 = (bf16[768,1024]{1,0:T(8,128)(2,1)}, bf16[2304,1024]{1,0:T(8,128)(2,1)}, bf16[1536,64]{1,0:T(8,128)(2,1)}, f32[768,128]{1,0:T(8,128)}, bf16[768,10...) custom-call(f32[768,1024]{1,0:T(8,128)} %convert_bitcast_fusion.refs, ...), custom_call_target="tpu_custom_call" | custom-call | flops 6800000000 | bytes 40000000 | tf_op jit(solution)/shard_map/attention/pallas_call | solution.py:191
  109.9 1.4 fusion.5
  111.3 1.5 reshape.184.refs_2_
  112.8 43.2 %feed.2 = (bf16[3072,1024]{1,0:T(8,128)(2,1)}, bf16[3072,1024]{1,0:T(8,128)(2,1)}, f32[768,1024]{1,0:T(8,128)}, f32[8,1024]{1,0:T(8,128)}, f32[768,1024]{1,0:T(8...) custom-call(f32[768,1024]{1,0:T(8,128)} %get-tuple-element.181.refs_, ...), custom_call_target="tpu_custom_call" | custom-call | flops 9799999488 | bytes 40000000 | tf_op jit(solution)/shard_map/feed/pallas_call | solution.py:191
  156.0 0.1 rev.7
  156.2 0.7 fusion.refs_2_.refs_8_
  156.9 45.7 %attention.3 = (bf16[768,1024]{1,0:T(8,128)(2,1)}, bf16[2304,1024]{1,0:T(8,128)(2,1)}, bf16[1536,64]{1,0:T(8,128)(2,1)}, bf16[768,1024]{1,0:T(8,128)(2,1)}, bf16...) custom-call(f32[768,1024]{1,0:T(8,128)} %get-tuple-element.199.refs_, ...), custom_call_target="tpu_custom_call" | custom-call | flops 6800000000 | bytes 40000000 | tf_op jit(solution)/shard_map/attention/pallas_call | solution.py:191
  202.7 1.5 reshape.185.refs_2_
  204.2 24.8 %feed.3 = (bf16[3072,1024]{1,0:T(8,128)(2,1)}, bf16[3072,1024]{1,0:T(8,128)(2,1)}, f32[768,1024]{1,0:T(8,128)}, f32[8,1024]{1,0:T(8,128)}, bf16[1024,768]{1,0:T(8,128)(2,1)}) custom-call(f32[768,1024]{1,0:T(8,128)} %get-tuple-element.210.refs_0_.refs_3_, f32[768,128]{1,0:T(8,128)} %get-tuple-element.182.refs_1_.refs_4_.refs_5_, f32[3072,1]{1,0:T(8,128)} %reshape.185.refs_2_, ...), custom_call_target="tpu_custom_call" | custom-call | flops 9799999488 | bytes 40000000 | tf_op jit(solution)/shard_map/feed/pallas_call | solution.py:191
  229.0 0.8 broadcast_in_dim.3.refs_0_
  229.8 22.1 %hidden.2 = (bf16[4,384,768]{2,1,0:T(8,128)(2,1)}, bf16[4,384,768]{2,1,0:T(8,128)(2,1)}, bf16[3072,1024]{1,0:T(8,128)(2,1)}, f32[768,1024]{1,0:T(8,128)}, f32[768,128]{1,0:T(8,128)}) custom-call(f32[768,128]{1,0:T(8,128)} %broadcast_in_dim.3.refs_0_, bf16[1024,768]{1,0:T(8,128)(2,1)} %refs_1_.1, f32[768,1024]{1,0:T(8,128)} %get-tuple-element.225.refs_2_, ...), custom_call_target="tpu_custom_call" | custom-call | flops 9699999744 | bytes 40000000 | tf_op jit(solution)/shard_map/hidden/pallas_call | solution.py:191
  251.9 27.8 %inner.2 = (bf16[384,3072]{1,0:T(8,128)(2,1)}, bf16[384,3072]{1,0:T(8,128)(2,1)}, f32[768,1024]{1,0:T(8,128)}, f32[768,128]{1,0:T(8,128)}, bf16[384,768]{1,0:T(8,128)(2,1)}, /*index=5*/f32[384,768]{1,0:T(8,128)}) custom-call(f32[768,128]{1,0:T(8,128)} %get-tuple-element.229.refs_0_, bf16[3072,1024]{1,0:T(8,128)(2,1)} %get-tuple-element.230.refs_1_, ...), custom_call_target="tpu_custom_call" | custom-call | flops 9699999744 | bytes 35000000 | tf_op jit(solution)/shard_map/inner/pallas_call | solution.py:191
  279.7 32.4 %values.2 = (bf16[384,1536]{1,0:T(8,128)(2,1)}, bf16[384,1536]{1,0:T(8,128)(2,1)}, bf16[768,1024]{1,0:T(8,128)(2,1)}, bf16[768,1024]{1,0:T(8,128)(2,1)}, f32[12,...) custom-call(f32[768,128]{1,0:T(8,128)} %get-tuple-element.235.refs_0, ...), custom_call_target="tpu_custom_call" | custom-call | flops 6200000000 | bytes 25000000 | tf_op jit(solution)/shard_map/values/pallas_call | solution.py:191
  312.1 41.9 %back.2 = (bf16[384,1536]{1,0:T(8,128)(2,1)}, bf16[384,1536]{1,0:T(8,128)(2,1)}, f32[768,1024]{1,0:T(8,128)}, f32[768,128]{1,0:T(8,128)}, f32[96,768]{1,0:T(8,12...) custom-call(f32[768,128]{1,0:T(8,128)} %get-tuple-element.247.refs_0_, ...), custom_call_target="tpu_custom_call" | custom-call | flops 10000000000 | bytes 50000000 | tf_op jit(solution)/shard_map/back/pallas_call | solution.py:191
  354.1 30.4 %hidden.3 = (bf16[4,384,768]{2,1,0:T(8,128)(2,1)}, bf16[4,384,768]{2,1,0:T(8,128)(2,1)}, bf16[3072,1024]{1,0:T(8,128)(2,1)}, f32[768,1024]{1,0:T(8,128)}, f32[76...) custom-call(f32[768,128]{1,0:T(8,128)} %get-tuple-element.261.refs_0_, ...), custom_call_target="tpu_custom_call" | custom-call | flops 9699999744 | bytes 40000000 | tf_op jit(solution)/shard_map/hidden/pallas_call | solution.py:191
  384.5 28.9 %inner.3 = (bf16[384,3072]{1,0:T(8,128)(2,1)}, bf16[384,3072]{1,0:T(8,128)(2,1)}, f32[768,1024]{1,0:T(8,128)}, f32[768,128]{1,0:T(8,128)}, bf16[384,768]{1,0:T(8...) custom-call(f32[768,128]{1,0:T(8,128)} %get-tuple-element.271.refs_0_, ...), custom_call_target="tpu_custom_call" | custom-call | flops 9699999744 | bytes 35000000 | tf_op jit(solution)/shard_map/inner/pallas_call | solution.py:191
  413.4 32.2 %values.3 = (bf16[384,1536]{1,0:T(8,128)(2,1)}, bf16[384,1536]{1,0:T(8,128)(2,1)}, bf16[768,1024]{1,0:T(8,128)(2,1)}, bf16[768,1024]{1,0:T(8,128)(2,1)}, f32[12,...) custom-call(f32[768,128]{1,0:T(8,128)} %get-tuple-element.279.refs_0, ...), custom_call_target="tpu_custom_call" | custom-call | flops 6200000000 | bytes 25000000 | tf_op jit(solution)/shard_map/values/pallas_call | solution.py:191
  445.6 66.9 %back.3 = (f32[1024,768]{1,0:T(8,128)}, f32[768,128]{1,0:T(8,128)}, f32[96,768]{1,0:T(8,128)}, f32[24,3072]{1,0:T(8,128)}, f32[24,1536]{1,0:T(8,128)}, /*index=5...) custom-call(f32[768,128]{1,0:T(8,128)} %get-tuple-element.291.refs_0_, ...), custom_call_target="tpu_custom_call" | custom-call | flops 10000000000 | bytes 50000000 | tf_op jit(solution)/shard_map/back/pallas_call | solution.py:191
  512.6 0.0 copy-start.3
  512.6 0.8 slice_dynamic-update-slice_fusion.9
  513.5 0.8 slice_dynamic-update-slice_fusion.8
  514.3 0.8 slice_dynamic-update-slice_fusion.7
  515.0 0.8 slice_dynamic-update-slice_fusion.6
  515.8 0.9 slice_bitcast_fusion.7
  516.7 0.0 copy-start
  516.7 0.8 pad_maximum_fusion.2
  517.5 0.7 pad_maximum_fusion.4
  518.2 0.9 pad_maximum_fusion
  519.1 0.0 copy-done.9
  519.1 0.6 reshape.181
  519.7 1.3 constant_dynamic-slice_fusion.2
  521.0 1.8 pad_maximum_fusion.1
  522.8 0.1 constant_dynamic-slice_fusion
  522.9 0.6 copy.56
  523.5 0.7 constant_dynamic-slice_fusion.1
  524.2 0.6 copy.57
  524.8 1.7 copy.73
  (34 shorter events, 0.2 us)
Async XLA Ops:
  2.4 2.1 copy-start.11
  2.4 3.0 copy-start.14
  2.4 3.3 copy-start.12
  2.4 3.3 copy-start.13
  2.4 3.5 copy-start.10
  2.4 3.5 copy-start.6
  2.4 4.8 copy-start.1
  4.5 45.0 %copy-start.2 = (bf16[2,96,768]{2,1,0:T(8,128)(2,1)S(1)}, bf16[2,96,768]{2,1,0:T(8,128)(2,1)}, u32[]{:S(2)}) copy-start(bf16[2,96,768]{2,1,0:T(8,128)(2,1)} %param.16) | copy-start | bytes 884740
  445.6 66.9 %copy-start.8 = (f32[24,1536]{1,0:T(8,128)S(1)}, f32[24,1536]{1,0:T(8,128)}, u32[]{:S(2)}) copy-start(f32[24,1536]{1,0:T(8,128)} %get-tuple-element.311) | copy-start | bytes 442372
  445.6 67.0 %copy-start.7 = (f32[24,1536]{1,0:T(8,128)S(1)}, f32[24,1536]{1,0:T(8,128)}, u32[]{:S(2)}) copy-start(f32[24,1536]{1,0:T(8,128)} %get-tuple-element.312) | copy-start | bytes 442372
  512.5 5.7 %copy-start.4 = (f32[24,3072]{1,0:T(8,128)S(1)}, f32[24,3072]{1,0:T(8,128)}, u32[]{:S(2)}) copy-start(f32[24,3072]{1,0:T(8,128)} %get-tuple-element.314) | copy-start | bytes 884740
  512.5 5.7 %copy-start.5 = (f32[24,3072]{1,0:T(8,128)S(1)}, f32[24,3072]{1,0:T(8,128)}, u32[]{:S(2)}) copy-start(f32[24,3072]{1,0:T(8,128)} %get-tuple-element.313) | copy-start | bytes 884740
  512.6 6.5 %copy-start.9 = (f32[24,896]{1,0:T(8,128)S(1)}, f32[24,896]{1,0:T(8,128)}, u32[]{:S(2)}) copy-start(f32[24,896]{1,0:T(8,128)} %get-tuple-element.315) | copy-start | bytes 258052
  512.6 8.4 %copy-start.3 = (f32[96,768]{1,0:T(8,128)S(1)}, f32[96,768]{1,0:T(8,128)}, u32[]{:S(2)}) copy-start(f32[96,768]{1,0:T(8,128)} %get-tuple-element.317) | copy-start | bytes 884740
  516.7 8.1 %copy-start = (f32[1024,768]{1,0:T(8,128)S(1)}, f32[1024,768]{1,0:T(8,128)}, u32[]{:S(2)}) copy-start(f32[1024,768]{1,0:T(8,128)} %get-tuple-element.383) | copy-start | bytes 9437188

commit v4 on v3

--- a/solution.py
+++ b/solution.py
@@ -307,7 +307,7 @@
             return self.block
         return self.moves[name]
 
-    def go(self, **turns):
+    def go(self, apart=0, **turns):
         out = []
         fresh = {}
         value = lambda k: fresh[k] if k in fresh else (
@@ -322,7 +322,12 @@
                 todo = {"core0": [("c0", "own", "core")], "core1": [("c1", "a", "core")],
                         "core2": [("c2", "b0", "core"), ("c3", "b1", "core")]}[key]
             for name, source, partner in todo:
-                fresh[name] = Move(value(source), partner, *turn)
+                start, wait = turn
+                if name == "b1":
+                    wait += apart
+                if name == "c3":
+                    start += apart
+                fresh[name] = Move(value(source), partner, start, wait)
                 out.append(fresh[name])
         self.moves.update(fresh)
         return sorted(out, key=lambda m: m.start)
@@ -333,7 +338,7 @@
 
 
 def strips(columns):
-    width = 384 if columns % 384 == 0 else columns
+    width = 384 if columns % 384 == 0 else 512 if columns % 512 == 0 else columns
     return [slice(c, c + width) for c in range(0, columns, width)]
 
 
@@ -349,7 +354,7 @@
         self.specs = [ANY] * len(self.args)
         self.outs = [] if chained else [(sd(*shape, t=bf16), whole(*shape)), (sd(*shape), whole(*shape))]
         self.scratch = [pltpu.VMEM((2 * r, self.columns), bf16), pltpu.VMEM((2 * r, self.columns), bf16),
-                        pltpu.VMEM((4 * r, self.columns), bf16), DMA((5,))]
+                        pltpu.VMEM((4 * r, self.columns), bf16), DMA((7,))]
         if chained:
             self.scratch += [pltpu.VMEM(shape, bf16), pltpu.VMEM(shape, f32)]
         if columns is None:
@@ -373,8 +378,10 @@
     def load(self):
         return pltpu.make_async_copy(self.keep_from, self.keep, self.sem.at[4])
 
-    def first(self):
-        return remote(self.send, self.got0, self.sem.at[0], self.sem.at[1], "core")
+    def first(self, half):
+        at = pl.ds(2 * self.r * half, 2 * self.r)
+        k = 5 if half == 0 else 0
+        return remote(self.send.at[at, :], self.got0.at[at, :], self.sem.at[k], self.sem.at[k + 1], "core")
 
     def second(self):
         return remote(self.away1, self.got1, self.sem.at[2], self.sem.at[3], "b")
@@ -382,17 +389,19 @@
     def turn(self, i):
         r = self.r
         if i == self.turns[0]:
-            self.first().start()
+            self.first(1).start()
             if self.at is None:
                 self.load().start()
+            self.first(0).start()
         if i == self.turns[1]:
             if self.at is None:
                 self.load().wait()
-            self.first().wait()
+            self.first(1).wait()
             for at in strips(self.columns):
                 self.away1[:, at] = self.keep[2 * r :, at] + self.got0[2 * r :, at]
             self.second().start()
         if i == self.turns[2]:
+            self.first(0).wait()
             self.second().wait()
             for at in strips(self.columns):
                 for k, out in ((0, self.own2), (1, self.away2)):
@@ -458,19 +467,90 @@
         self.value = got[0]
 
 
+class Core:
+    def __init__(self, keep, send, turns):
+        self.turns = turns
+        r, columns = send.shape[0] // 2, send.shape[1]
+        self.r, self.columns = r, columns
+        self.partners = ["core"]
+        self.args, self.specs = [keep, send], [ANY, ANY]
+        self.outs = [(sd(r, columns, t=bf16), whole(r, columns))] * 2
+        self.scratch = [pltpu.VMEM((2 * r, columns), bf16), pltpu.VMEM((2 * r, columns), bf16), DMA((3,))]
+
+    def bind(self, args, outs, scratch):
+        self.keep_from, self.send = args
+        self.away, self.own = outs
+        self.keep, self.got, self.sem = scratch
+
+    def copies(self):
+        return [pltpu.make_async_copy(self.keep_from, self.keep, self.sem.at[2]),
+                remote(self.send, self.got, self.sem.at[0], self.sem.at[1], "core")]
+
+    def turn(self, i):
+        if i == self.turns[0]:
+            for copy in self.copies():
+                copy.start()
+        if i == self.turns[1]:
+            for copy in self.copies():
+                copy.wait()
+            for at in strips(self.columns):
+                self.away[:, at] = self.keep[self.r :, at] + self.got[self.r :, at]
+                self.own[:, at] = self.keep[: self.r, at] + self.got[: self.r, at]
+
+    def done(self, got):
+        self.value = got
+
+
+class Plane:
+    def __init__(self, away, own, turns, chained=False):
+        self.turns, self.chained = turns, chained
+        rows2, self.columns = away.shape
+        self.r = rows2 // 2
+        shape = (self.r, self.columns)
+        self.partners = ["b"]
+        self.args, self.specs = [away, own], [ANY, whole(rows2, self.columns)]
+        self.outs = [] if chained else [(sd(*shape, t=bf16), whole(*shape)), (sd(*shape), whole(*shape))]
+        self.scratch = [pltpu.VMEM((rows2, self.columns), bf16), DMA((2,))]
+        if chained:
+            self.scratch += [pltpu.VMEM(shape, bf16), pltpu.VMEM(shape, f32)]
+
+    def bind(self, args, outs, scratch):
+        self.away1, self.own1 = args
+        self.got, self.sem = scratch[:2]
+        self.away2, self.own2 = scratch[2:] if self.chained else outs
+
+    def copy(self):
+        return remote(self.away1, self.got, self.sem.at[0], self.sem.at[1], "b")
+
+    def turn(self, i):
+        r = self.r
+        if i == self.turns[0]:
+            self.copy().start()
+        if i == self.turns[1]:
+            self.copy().wait()
+            for at in strips(self.columns):
+                for block, out in ((slice(0, r), self.own2), (slice(r, 2 * r), self.away2)):
+                    value = self.own1[block, at].astype(f32) + self.got[block, at].astype(f32)
+                    out[:, at] = value.astype(out.dtype)
+
+    def done(self, got):
+        self.value = got
+
+
 class Third:
-    def __init__(self, away, own, turns):
-        self.turns = turns
-        r, columns = away.shape
+    def __init__(self, away, own, turns, inside=None):
+        self.turns, self.inside = turns, inside
+        r, columns = (inside.r, inside.columns) if inside else away.shape
         self.columns, self.size = columns, r // 4
         self.partners = ["a"]
-        self.args, self.specs = [away, own], [ANY, whole(r, columns)]
+        self.args = [] if inside else [away, own]
+        self.specs = [] if inside else [ANY, whole(r, columns)]
         shape = (4, self.size, columns)
         self.outs = [(sd(*shape, t=bf16), whole(*shape)), (sd(*shape), whole(*shape))]
         self.scratch = [pltpu.VMEM((r, columns), bf16), DMA((2,))]
 
     def bind(self, args, outs, scratch):
-        self.away, self.own = args
+        self.away, self.own = (self.inside.away2, self.inside.own2) if self.inside else args
         self.parts, self.sums = outs
         self.got, self.sem = scratch
 
@@ -535,17 +615,16 @@
 
 
 class Total:
-    def __init__(self, taps, turns):
+    def __init__(self, packed, turns):
         self.turns = turns
-        self.args = list(taps)
-        self.specs = [whole(*a.shape) for a in self.args]
-        shape = (SMALL, D + 128)
+        self.args, self.specs = [packed], [whole(*packed.shape)]
+        shape = packed.shape
         self.outs = [(sd(*shape), whole(*shape))]
         self.scratch = [pltpu.VMEM((5, *shape), f32), pltpu.VMEM((5, *shape), f32), DMA((10,))]
         self.partners = ["core", "x", "y", "z1", "z2"]
 
     def bind(self, args, outs, scratch):
-        self.taps, self.out = args, outs[0]
+        self.packed, self.out = args[0], outs[0]
         self.held, self.got, self.sem = scratch
 
     def use(self, keep, send, sums):
@@ -566,8 +645,7 @@
                         self.out[...] = value
                 else:
                     self.held[0, :, 0:D] = self.sums[...].T[0:SMALL, :]
-                    self.held[0, 0:HEADS, D:] = self.taps[0][...]
-                    self.held[0, HEADS : 2 * HEADS, D:] = self.taps[1][...]
+                    self.held[0, :, D:] = self.packed[:, D:]
                 if s < 5:
                     self.copy(s).start()
 
@@ -732,7 +810,7 @@
         return 0
 
     for third in range(3):
-        lax.fori_loop(third * 4, third * 4 + 4, head_step, 0, unroll=2)
+        lax.fori_loop(third * 4, third * 4 + 4, head_step, 0, unroll=4)
         at = pl.ds(third * 4 * HD, 4 * HD)
         for src, dst in ((f_ref, f_out), (b_ref, b_out), (ctx_ref, ctx_out)):
             leave(src.at[at, :], dst.at[at, :])
@@ -750,8 +828,8 @@
         copy.wait()
     for k in range(NS_ITERS):
         pltpu.make_async_copy(ns_ref.at[k], ns_out.at[k], ns_sem.at[k]).wait()
-    hook(9)
-    hook(10)
+    for i in range(9, 13):
+        hook(i)
 
 
 def attention(x, groups, par, conv, layer, lanes=(None, ())):
@@ -821,6 +899,10 @@
         def _():
             hook(i + 1)
 
+    @pl.when(j == STEPS - 1)
+    def _():
+        hook(STEPS + 1)
+
 
 def feed(xhat, pieces1, pieces2, par, inb, layer, last, lanes=(None, ())):
     n = len(pieces1)
@@ -881,6 +963,7 @@
         norm_backward(dy, xhat_ref, rstd_ref, par_ref[:, p + 7 : p + 8], dr_ref, cols_ref, p + 7, p + 5)
         dz_ref[...] = dr_ref[...].astype(bf16)
         cols_ref[:, p + 4 : p + 5] = lane_sum(dz_ref[...])
+        hook(1)
         for copy in loads:
             copy.wait()
 
@@ -907,7 +990,7 @@
         def _():
             column = 2 * 8 + p // 2 + i
             cols_ref[:, column : column + 1] = inb_ref[...]
-            hook(i + 1)
+            hook(i + 2)
 
 
 def hidden(sums, dy, xhat, rstd, par, a, g, pieces, layer, first, lanes=(None, ())):
@@ -992,12 +1075,12 @@
         for i in range(8)]
 
 
-def values_kernel(sizes, p, sums_in, dr1_ref, mix_from, ctx_from, f_from, b_from, xl_from, small_ref, conv_ref,
+def values_kernel(sizes, p, small_in, sums_in, dr1_ref, mix_from, ctx_from, f_from, b_from, xl_from, small_ref, conv_ref,
                   *rest, hook):
     order = Order(sizes[0][0])
     groups, rest = grouped(rest, sizes)
-    (keep_ref, send_ref, dctx_out, dv_ref, dz_ref, dbv_ref, taps_ref, cols_ref,
-     w_ref, dp_ref, perm_ref, vpad_ref, dpad_ref, dctx_ref, f_ref, b_ref, v_ref, xperm_ref,
+    (keep_ref, send_ref, dctx_out, dv_ref, dz_ref, dbv_ref, small_out, cols_ref,
+     w_ref, dp_ref, perm_ref, vpad_ref, dpad_ref, dctx_ref, f_ref, b_ref, v_ref, xperm_ref, taps_ref,
      sem, perm_sem, late_sem) = rest
     early = column_loader(groups, sizes, w_ref, sem, 3 * D, 4 * D)
     perms = row_loader(ctx_from, perm_ref, order, perm_sem.at[0])
@@ -1023,6 +1106,7 @@
         return 0
 
     lax.fori_loop(0, 2, dctx_step, 0)
+    hook(1)
     leave = pltpu.make_async_copy(dctx_ref, dctx_out, late_sem.at[3])
     leave.start()
     for copy in perms:
@@ -1032,7 +1116,7 @@
     for copy in late:
         copy.wait()
     vpad_ref[:, LEAD : LEAD + T] = v_ref[...]
-    hook(1)
+    hook(2)
     flip = jnp.where(
         lax.broadcasted_iota(jnp.int32, (CONV_N, CONV_N), 0)
         + lax.broadcasted_iota(jnp.int32, (CONV_N, CONV_N), 1) == CONV_N - 1, 1.0, 0.0).astype(bf16)
@@ -1055,39 +1139,44 @@
         return 0
 
     lax.fori_loop(0, HEADS // 2, value_step, 0, unroll=2)
-    hook(2)
+    hook(3)
     lax.fori_loop(HEADS // 2, HEADS, value_step, 0, unroll=2)
-    hook(3)
+    hook(4)
     for copy in last:
         copy.wait()
     for i, ref in enumerate((keep_ref, send_ref)):
         ref[:, D:] = dot(xperm_ref[i * (D // 2) : (i + 1) * (D // 2), :], dv_ref[...], NT).astype(bf16)
     cols_ref[...] = sums_in[...]
     cols_ref[:, p + 1 : p + 2] = lane_sum(dv_ref[...])
+    first = p // 8 * HEADS
+    small_out[...] = small_in[...]
+    small_out[:, 0:D] = cols_ref[...].T[0:SMALL, :]
+    small_out[first : first + HEADS, D:] = taps_ref[...]
     leave.wait()
-    hook(4)
-
-
-def values(sums, dr1, mix, ctx, f, b, xl, small, conv, groups, layer, lanes=(None, ())):
+    hook(5)
+
+
+def values(total, sums, dr1, mix, ctx, f, b, xl, small, conv, groups, layer, lanes=(None, ())):
     sizes = sizes_of(groups, layer)
     n = sizes[0][0]
     return call(
         functools.partial(values_kernel, sizes, 8 * layer), "values",
         [
             sd(D // 2, 2 * D, t=bf16), sd(D // 2, 2 * D, t=bf16), sd(D, T, t=bf16), sd(D, T, t=bf16),
-            sd(HEADS, LM, LM), sd(HEADS, LM, LM, t=bf16), sd(HEADS, 128), sd(D, 128),
+            sd(HEADS, LM, LM), sd(HEADS, LM, LM, t=bf16), sd(SMALL, D + 128), sd(D, 128),
         ],
-        [vm(), vm()] + [ANY] * 5 + [vm(), vm()] + anywhere(n * len(groups)),
+        [vm(), vm(), vm()] + [ANY] * 5 + [vm(), vm()] + anywhere(n * len(groups)),
         [vm(), vm(), ANY] + [vm()] * 5,
         [
             pltpu.VMEM((D, D), bf16), pltpu.VMEM((D, T), bf16), pltpu.VMEM((D, T), bf16),
             pltpu.VMEM((D, T + 2 * LEAD), bf16), pltpu.VMEM((D, T + 2 * LEAD), bf16),
-        ] + [pltpu.VMEM((D, T), bf16)] * 5 + [DMA((len(groups), n)), DMA((2, 8)), DMA((4,))],
-        (sums, dr1, mix, ctx, f, b, xl, small, conv, *[piece for g in groups for piece in g]), lanes,
+        ] + [pltpu.VMEM((D, T), bf16)] * 5 + [pltpu.VMEM((HEADS, 128), f32), DMA((len(groups), n)), DMA((2, 8)), DMA((4,))],
+        (total, sums, dr1, mix, ctx, f, b, xl, small, conv, *[piece for g in groups for piece in g]), lanes,
         6_200_000_000, 25_000_000)
 
 
 QK = 2 * D
+QK_HEADS = ((0, 8), (8, 4))
 TURNS = 20
 
 
@@ -1184,21 +1273,23 @@
         return 0
 
     half = D // 2
-    for part in range(2):
-        for quarter in range(2):
-            start = (2 * part + quarter) * (HEADS // 4)
-            lax.fori_loop(start, start + HEADS // 4, score_step, 0)
-            if quarter == 0:
-                hook(3 + 2 * part)
-        for side, ref in ((1, send_ref), (0, keep_ref)):
-            mine = perm_ref[side * half : (side + 1) * half, :]
-            for k in range(2):
-                at = part * D + k * half
-                d = mix_ref[k * D + part * half : k * D + (part + 1) * half, :]
-                ref[:, at : at + half] = dot(mine, d, NT).astype(bf16)
+    at = 0
+    for part, (head, heads) in enumerate(QK_HEADS):
+        middle = head + heads // 2
+        lax.fori_loop(head, middle, score_step, 0, unroll=heads // 2)
+        hook(3 + 2 * part)
+        lax.fori_loop(middle, head + heads, score_step, 0, unroll=heads // 2)
+        if head + heads == HEADS:
+            cols_ref[...] = sums_in[...]
+            cols_ref[:, p : p + 1] = lane_sum(mix_ref[0:D, :])
+        width = heads * HD
+        for k in range(2):
+            d = mix_ref[k * D + head * HD : k * D + head * HD + width, :]
+            for side, ref in ((1, send_ref), (0, keep_ref)):
+                mine = perm_ref[side * half : (side + 1) * half, :]
+                ref[:, at : at + width] = dot(mine, d, NT).astype(bf16)
+            at += width
         hook(4 + 2 * part)
-    cols_ref[...] = sums_in[...]
-    cols_ref[:, p : p + 1] = lane_sum(mix_ref[0:D, :])
     for i in range(3):
         at = slice(i * 256, (i + 1) * 256)
         got = dr1_ref[at, :] + dot(w_ref[at, 0:QK], mix_ref[0:QK, :], NN) + dot(w_ref[at, QK:], dv_ref[...], NN)
@@ -1429,17 +1520,19 @@
         s2 = Spread(qkvo[0][:, 2 * D :], 1, 3)
         g1, g2 = Gather(s1), Gather(s2)
         s3 = Spread(in_w[0], 3, 8)
+        g3 = Gather(s3)
         m1 = g1.go(a=(1, 2), b=(2, 4), core0=(1, 8), core1=(2, 8), core2=(4, 8))
-        m2 = g2.go(a=(3, 5), b=(5, 7), core0=(3, 8), core1=(5, 8), core2=(7, 8))
-        exchange(plan.lanes(s1, s2, *m1, *m2, s3), 9)
+        m2 = g2.go(apart=1, a=(3, 5), b=(5, 7), core0=(3, 9), core1=(5, 9), core2=(7, 9))
+        exchange(plan.lanes(s1, s2, *m1, *m2, s3), 10)
         att = [[g1.pieces(), g2.pieces()], None]
         win, wout = [None] * 2, [None] * 2
-        g3 = Gather(s3)
-        s4, s5 = Spread(out2_w[0], 0, 4), Spread(qkvo[1], 4, 9)
+        s4, s5 = Spread(out2_w[0], 0, 6), Spread(qkvo[1], 6, 10)
         g4 = Gather(s4)
-        m3 = g3.go(a=(0, 2), b=(2, 6), core0=(0, 3), core1=(2, 5), core2=(6, 9))
-        m4 = g4.go(a=(4, 6), b=(6, 9), core0=(4, 7), core1=(6, 9), core2=(9, 10))
-        on_attention[0] = plan.lanes(s4, *m3, *m4, s5)
+        m3 = g3.go(a=(0, 4), b=(4, 9), core0=(0, 4), core1=(4, 9), core2=(9, 11))
+        m4 = g4.go(apart=1, a=(6, 8), b=(8, 10), core0=(6, 9), core1=(8, 10), core2=(10, 12))
+        g5 = Gather(s5)
+        m5 = g5.go(a=(10, 12))
+        on_attention[0] = plan.lanes(s4, *m3, *m4, s5, *m5)
     else:
         shards = [jnp.concatenate([qkvo[0], small], axis=1)] + qkvo[1:]
         att, win, wout = gather_all(ring, shards, in_w, out2_w)
@@ -1453,10 +1546,10 @@
             x, att[layer], par, conv[layer], layer, on_attention[layer])
         if on and layer == 0:
             win[0], wout[0] = g3.pieces(), g4.pieces()
-            s6, s7 = Spread(in_w[1], 0, 2), Spread(out2_w[1], 2, 4)
-            g5, g6, g7 = Gather(s5), Gather(s6), Gather(s7)
-            m5 = g5.go(a=(0, 1), b=(1, 3), core0=(0, 1), core1=(1, 3), core2=(3, 4))
-            m6 = g6.go(a=(3, 4))
+            s6, s7 = Spread(in_w[1], 0, 3), Spread(out2_w[1], 3, 5)
+            g6, g7 = Gather(s6), Gather(s7)
+            m5 = g5.go(b=(0, 3), core0=(0, 3), core1=(0, 3), core2=(3, 5))
+            m6 = g6.go(a=(3, 5))
             on_feed[0] = plan.lanes(*m5, s6, s7, *m6)
         if on and layer == 1:
             win[1], wout[1] = g6.pieces(), g7.pieces()
@@ -1466,15 +1559,15 @@
             xhat1, win[layer], wout[layer], par, inb, layer, final, on_feed[layer])
         if on and layer == 0:
             att[1] = [g5.pieces()]
-            m6 = g6.go(b=(0, 4), core0=(0, 3), core1=(0, 3), core2=(4, 9))
-            m7 = g7.go(a=(0, 2), b=(4, 8), core0=(0, 3), core1=(2, 5), core2=(8, 10))
+            m6 = g6.go(b=(0, 6), core0=(0, 6), core1=(0, 6), core2=(6, 11))
+            m7 = g7.go(apart=1, a=(0, 6), b=(6, 10), core0=(0, 6), core1=(6, 10), core2=(10, 12))
             on_attention[1] = plan.lanes(*m6, *m7)
         kept.append((xl, mix, lm, ctx, f, b, a, ns, sm, xhat1, rstd1, act, slope, xhat2, rstd2))
     output = x
 
     dy = cotangent
     sums = jnp.zeros((D, 128), f32)
-    taps = [None] * layers
+    total = jnp.zeros((SMALL, D + 128), f32)
     grads = [{} for _ in range(layers)]
     firsts, thirds, ends = {}, {}, []
 
@@ -1502,37 +1595,59 @@
         above = layer + 1 < layers
         lane = none
         if on and above:
-            lane = plan.lanes(sum_first(*halves, (0, 1, 4), layer + 1, "qk"), sum_last(layer + 1, "ov", (0, 1, 4)))
+            firsts[layer + 1, "ov"] = Plane(*core_ov.value, (0, 5))
+            lane = plan.lanes(
+                sum_first(*halves, (0, 1, 5), layer + 1, "qk"), firsts[layer + 1, "ov"],
+                sum_final(layer + 1, "in", (0, 5)))
         keep, send, du, dr2, sums = hidden(
             sums, dy, xhat2, rstd2, par, act, slope, wout[layer], layer, not above, lane)
         if on:
-            lane = [sum_first(keep.reshape(-1, D), send.reshape(-1, D), (0, 1, 4), layer, "out2")]
-            lane += [sum_last(layer + 1, "qk", (0, 1, 4))] if above else []
+            out2 = (keep.reshape(-1, D), send.reshape(-1, D))
+            if above:
+                lane = [
+                    sum_first(*out2, (0, 1, 4), layer, "out2"),
+                    sum_third(layer + 1, "qk", (0, 3)), sum_third(layer + 1, "ov", (0, 3))]
+            else:
+                core2 = Core(*out2, (0, 2))
+                lane = [core2]
             lane = plan.lanes(*lane)
         else:
             grads[layer]["out2"] = ring.sum(*natural_halves(keep, send))
         keep, send, dr1, sums = inner(sums, du, dr2, xhat1, rstd1, par, win[layer], layer, lane)
         if on:
-            lane = plan.lanes(sum_third(layer, "out2", (0, 1)), sum_first(keep, send, (0, 1, 4), layer, "in"))
+            core1 = Core(keep, send, (0, 3))
+            if above:
+                lane = [
+                    sum_third(layer, "out2", (0, 5)), sum_first(keep, send, (0, 1, 5), layer, "in"),
+                    sum_final(layer + 1, "qk", (0, 5)), sum_final(layer + 1, "ov", (0, 5))]
+            else:
+                core1 = Core(keep, send, (0, 3))
+                firsts[layer, "out2"] = Plane(*core2.value, (0, 5))
+                lane = [firsts[layer, "out2"], core1]
+            lane = plan.lanes(*lane)
         else:
             grads[layer]["in"] = ring.sum(keep, send)
-        keep, send, dctx, dv, dz, dbv, taps[layer], sums = values(
-            sums, dr1, mix, ctx, f, b, xl, sm, conv[layer], att[layer], layer, lane)
+        keep, send, dctx, dv, dz, dbv, total, sums = values(
+            total, sums, dr1, mix, ctx, f, b, xl, sm, conv[layer], att[layer], layer, lane)
         tail = []
         if on:
-            lane = [sum_final(layer, "out2", (0, 2)), sum_last(layer, "in", (0, 1, 6))]
             if layer:
-                lane.append(sum_first(keep, send, (0, 1, 3), layer, "ov"))
+                core_ov = Core(keep, send, (0, 2))
+                lead = Plane(*core1.value, (0, 4), chained=True)
+                thirds[layer, "in"] = Third(None, None, (4, 10), inside=lead)
+                lane = [sum_last(layer, "out2", (0, 3, 10)), lead, thirds[layer, "in"], core_ov]
             else:
+                late = Total(total, (6, 8, 10, 11, 13, 15))
+                lane, tail = [late], [late]
+                starts = (0, 2 * QK_HEADS[0][1] * HD, QK)
+                for part, (go, end) in enumerate((((4, 5, 8), (8, 11, 14)), ((6, 9, 11), (11, 13, 15)))):
+                    lead = ReduceFirst(None, None, go, chained=True, columns=slice(starts[part], starts[part + 1]))
+                    tail.append(lead)
+                    lane = [lead, ending(ReduceLast(None, None, end, inside=lead), 0, f"qk{part}")] + lane
                 lead = ReduceFirst(keep, send, (0, 1, 3), chained=True)
-                lane += [lead, ending(ReduceLast(None, None, (3, 4, 10), inside=lead), 0, "ov")]
-                for part, (go, end) in enumerate((((4, 5, 7), (7, 9, 12)), ((6, 7, 9), (9, 11, 13)))):
-                    lead = ReduceFirst(None, None, go, chained=True, columns=slice(part * D, (part + 1) * D))
-                    tail.append(lead)
-                    lane += [lead, ending(ReduceLast(None, None, end, inside=lead), 0, f"qk{part}")]
-                total = Total(taps, (7, 8, 9, 10, 11, 12))
-                tail.append(total)
-                lane.append(total)
+                lane += [
+                    sum_final(0, "out2", (0, 4)), sum_last(0, "in", (0, 2, 6)), lead,
+                    ending(ReduceLast(None, None, (3, 4, 10), inside=lead), 0, "ov")]
             lane = plan.lanes(*lane)
         else:
             grads[layer]["ov"] = ring.sum(keep, send)
@@ -1545,16 +1660,16 @@
         for lane, layer, place in ends:
             grads[layer][place] = lane.value
         grads[0]["qk"] = jnp.concatenate([grads[0]["qk0"], grads[0]["qk1"]], axis=1)
-        total = total.value
+        total = late.value
     else:
-        flat = jnp.concatenate([sums.T[:SMALL], jnp.concatenate(taps, axis=0)], axis=1)
-        total = ring.total(flat)
+        total = ring.total(jnp.concatenate([sums.T[:SMALL], total[:, D:]], axis=1))
     gbias, ggain, ginb, gtaps = small_outputs(ring, total, size, in_b.shape[1])
-    half = D // 2
+    first = 2 * QK_HEADS[0][1] * HD
+    cut, rest = first // 2, (QK - first) // 2
     stacked = [
         jnp.stack([
             jnp.concatenate([
-                g["qk"][:, :half], g["qk"][:, D : D + half], g["qk"][:, half:D], g["qk"][:, D + half :],
+                g["qk"][:, :cut], g["qk"][:, first : first + rest], g["qk"][:, cut:first], g["qk"][:, first + rest :],
                 g["ov"][:, D:]], axis=1) for g in grads]),
         jnp.stack([g["ov"][:, :D] for g in grads]),
         jnp.stack([g["in"] for g in grads]),

time: 536 us -> 516 us (0.963)
  Pallas kernels: 497 us -> 476 us
    pallas_call x13, Pallas kernels: 497 us -> 476 us  [call(): pl.pallas_call(run, out_shape=list(out_shape) + [o for o, _ in lane_outs]...]
where the time goes in v4:
time: 516 us; the launch traced here: 506 us
  Pallas kernels  476 us (92%)
  local copies, waits for them, and re-layouts  17.3 us (3%)
  other arithmetic  11.6 us (2%)
    pallas_call x13, Pallas kernels, call(): pl.pallas_call(run, out_shape=list(out_shape) + [o for o, _ in lane_outs]...  476 us

profile of v4, /device:TPU:0, one launch (start us, length us, event | category | flops | bytes accessed | tf_op | source)
XLA Modules:
  0.0 505.8 jit_solution(3271920185246460798)
XLA Ops:
  0.6 0.0 copy-start.11
  0.7 0.0 copy-start.2
  0.7 0.0 copy-start.1
  0.7 1.1 slice_bitcast_fusion.4
  1.8 0.8 slice_bitcast_fusion.9
  2.6 0.6 pad_maximum_fusion.6
  3.2 0.8 reshape.147
  4.0 0.1 copy.48
  4.1 0.1 copy.50
  4.2 0.7 copy.47
  4.9 0.7 maximum_bitcast_fusion
  5.5 0.1 copy.49
  5.6 0.1 fusion.4
  5.7 0.6 pad_maximum_fusion.5.refs_0_
  6.4 1.7 slice_bitcast_fusion.1
  8.1 41.1 %exchange.1 = (bf16[4,24,1664]{2,1,0:T(8,128)(2,1)}, bf16[4,24,1536]{2,1,0:T(8,128)(2,1)}, bf16[4,24,1664]{2,1,0:T(8,128)(2,1)}, bf16[4,24,1664]{2,1,0:T(8,128)(...) custom-call(bf16[24,1664]{1,0:T(8,128)(2,1)} %pad_maximum_fusion.5.r, ...), custom_call_target="tpu_custom_call" | custom-call | bytes 10000000 | tf_op jit(solution)/shard_map/exchange/pallas_call | solution.py:191
  49.2 0.0 copy-done.11
  49.2 0.1 rev.6
  49.3 0.7 fusion.1.refs_1_.refs_9_
  50.1 0.7 pad_maximum_fusion.3.refs_22_
  50.8 0.0 copy-done.2
  50.8 0.7 slice_bitcast_fusion
  51.5 0.0 copy-done.1
  51.5 0.7 copy.43
  52.2 2.1 convert_bitcast_fusion.refs_0_
  54.3 64.1 %attention.2 = (bf16[768,1024]{1,0:T(8,128)(2,1)}, bf16[2304,1024]{1,0:T(8,128)(2,1)}, bf16[1536,64]{1,0:T(8,128)(2,1)}, f32[768,128]{1,0:T(8,128)}, bf16[768,10...) custom-call(f32[768,1024]{1,0:T(8,128)} %convert_bitcast_fusion.refs, ...), custom_call_target="tpu_custom_call" | custom-call | flops 6800000000 | bytes 40000000 | tf_op jit(solution)/shard_map/attention/pallas_call | solution.py:191
  118.4 1.4 fusion.5
  119.8 1.5 reshape.188.refs_2_
  121.3 37.0 %feed.2 = (bf16[3072,1024]{1,0:T(8,128)(2,1)}, bf16[3072,1024]{1,0:T(8,128)(2,1)}, f32[768,1024]{1,0:T(8,128)}, f32[8,1024]{1,0:T(8,128)}, f32[768,1024]{1,0:T(8...) custom-call(f32[768,1024]{1,0:T(8,128)} %get-tuple-element.189.refs_, ...), custom_call_target="tpu_custom_call" | custom-call | flops 9799999488 | bytes 40000000 | tf_op jit(solution)/shard_map/feed/pallas_call | solution.py:191
  158.3 0.1 rev.7
  158.4 0.7 fusion.refs_2_.refs_9_
  159.2 44.2 %attention.3 = (bf16[768,1024]{1,0:T(8,128)(2,1)}, bf16[2304,1024]{1,0:T(8,128)(2,1)}, bf16[1536,64]{1,0:T(8,128)(2,1)}, bf16[768,1024]{1,0:T(8,128)(2,1)}, bf16...) custom-call(f32[768,1024]{1,0:T(8,128)} %get-tuple-element.208.refs_, ...), custom_call_target="tpu_custom_call" | custom-call | flops 6800000000 | bytes 40000000 | tf_op jit(solution)/shard_map/attention/pallas_call | solution.py:191
  203.4 1.5 reshape.189.refs_2_
  204.9 25.0 %feed.3 = (bf16[3072,1024]{1,0:T(8,128)(2,1)}, bf16[3072,1024]{1,0:T(8,128)(2,1)}, f32[768,1024]{1,0:T(8,128)}, f32[8,1024]{1,0:T(8,128)}, bf16[1024,768]{1,0:T(8,128)(2,1)}) custom-call(f32[768,1024]{1,0:T(8,128)} %get-tuple-element.218.refs_0_.refs_3_, f32[768,128]{1,0:T(8,128)} %get-tuple-element.190.refs_1_.refs_4_.refs_5_, f32[3072,1]{1,0:T(8,128)} %reshape.189.refs_2_, ...), custom_call_target="tpu_custom_call" | custom-call | flops 9799999488 | bytes 40000000 | tf_op jit(solution)/shard_map/feed/pallas_call | solution.py:191
  229.9 0.8 broadcast_in_dim.7.refs_0_
  230.7 21.9 %hidden.2 = (bf16[4,384,768]{2,1,0:T(8,128)(2,1)}, bf16[4,384,768]{2,1,0:T(8,128)(2,1)}, bf16[3072,1024]{1,0:T(8,128)(2,1)}, f32[768,1024]{1,0:T(8,128)}, f32[768,128]{1,0:T(8,128)}) custom-call(f32[768,128]{1,0:T(8,128)} %broadcast_in_dim.7.refs_0_, bf16[1024,768]{1,0:T(8,128)(2,1)} %refs_1_.1, f32[768,1024]{1,0:T(8,128)} %get-tuple-element.233.refs_2_, ...), custom_call_target="tpu_custom_call" | custom-call | flops 9699999744 | bytes 40000000 | tf_op jit(solution)/shard_map/hidden/pallas_call | solution.py:191
  252.7 23.0 %inner.2 = (bf16[384,3072]{1,0:T(8,128)(2,1)}, bf16[384,3072]{1,0:T(8,128)(2,1)}, f32[768,1024]{1,0:T(8,128)}, f32[768,128]{1,0:T(8,128)}, bf16[768,768]{1,0:T(8,128)(2,1)}, /*index=5*/bf16[768,768]{1,0:T(8,128)(2,1)}) custom-call(f32[768,128]{1,0:T(8,128)} %get-tuple-element.237.refs_0_, bf16[3072,1024]{1,0:T(8,128)(2,1)} %get-tuple-element.238.refs_1_, ...), custom_call_target="tpu_custom_call" | custom-call | flops 9699999744 | bytes 35000000 | tf_op jit(solution)/shard_map/inner/pallas_call | solution.py:191
  275.6 0.6 broadcast_in_dim.6.refs_0_
  276.3 23.8 %values.2 = (bf16[384,1536]{1,0:T(8,128)(2,1)}, bf16[384,1536]{1,0:T(8,128)(2,1)}, bf16[768,1024]{1,0:T(8,128)(2,1)}, bf16[768,1024]{1,0:T(8,128)(2,1)}, f32[12,...) custom-call(f32[24,896]{1,0:T(8,128)} %broadcast_in_dim.6.refs_0_, ...), custom_call_target="tpu_custom_call" | custom-call | flops 6200000000 | bytes 25000000 | tf_op jit(solution)/shard_map/values/pallas_call | solution.py:191
  300.1 42.4 %back.2 = (bf16[384,1536]{1,0:T(8,128)(2,1)}, bf16[384,1536]{1,0:T(8,128)(2,1)}, f32[768,1024]{1,0:T(8,128)}, f32[768,128]{1,0:T(8,128)}, f32[96,768]{1,0:T(8,12...) custom-call(f32[768,128]{1,0:T(8,128)} %get-tuple-element.256.refs_0, ...), custom_call_target="tpu_custom_call" | custom-call | flops 10000000000 | bytes 50000000 | tf_op jit(solution)/shard_map/back/pallas_call | solution.py:191
  342.5 28.6 %hidden.3 = (bf16[4,384,768]{2,1,0:T(8,128)(2,1)}, bf16[4,384,768]{2,1,0:T(8,128)(2,1)}, bf16[3072,1024]{1,0:T(8,128)(2,1)}, f32[768,1024]{1,0:T(8,128)}, f32[76...) custom-call(f32[768,128]{1,0:T(8,128)} %get-tuple-element.270.refs_0, ...), custom_call_target="tpu_custom_call" | custom-call | flops 9699999744 | bytes 40000000 | tf_op jit(solution)/shard_map/hidden/pallas_call | solution.py:191
  371.1 30.1 %inner.3 = (bf16[384,3072]{1,0:T(8,128)(2,1)}, bf16[384,3072]{1,0:T(8,128)(2,1)}, f32[768,1024]{1,0:T(8,128)}, f32[768,128]{1,0:T(8,128)}, bf16[384,768]{1,0:T(8...) custom-call(f32[768,128]{1,0:T(8,128)} %get-tuple-element.282.refs_0, ...), custom_call_target="tpu_custom_call" | custom-call | flops 9699999744 | bytes 35000000 | tf_op jit(solution)/shard_map/inner/pallas_call | solution.py:191
  401.3 31.3 %values.3 = (bf16[384,1536]{1,0:T(8,128)(2,1)}, bf16[384,1536]{1,0:T(8,128)(2,1)}, bf16[768,1024]{1,0:T(8,128)(2,1)}, bf16[768,1024]{1,0:T(8,128)(2,1)}, f32[12,...) custom-call(f32[24,896]{1,0:T(8,128)} %get-tuple-element.255.refs_0_, ...), custom_call_target="tpu_custom_call" | custom-call | flops 6200000000 | bytes 25000000 | tf_op jit(solution)/shard_map/values/pallas_call | solution.py:191
  432.6 0.0 copy-start.3
  432.6 0.0 copy-start.4
  432.6 63.1 %back.3 = (f32[1024,768]{1,0:T(8,128)}, f32[768,128]{1,0:T(8,128)}, f32[24,512]{1,0:T(8,128)}, f32[24,1024]{1,0:T(8,128)}, f32[24,896]{1,0:T(8,128)}, /*index=5*...) custom-call(f32[768,128]{1,0:T(8,128)} %get-tuple-element.308.refs_0_, ...), custom_call_target="tpu_custom_call" | custom-call | flops 10000000000 | bytes 50000000 | tf_op jit(solution)/shard_map/back/pallas_call | solution.py:191
  495.7 0.0 copy-start.8
  495.7 0.0 copy-start.10
  495.7 0.0 copy-start.7
  495.8 0.0 copy-start.5
  495.8 0.0 copy-done.3
  495.8 1.9 pad_maximum_fusion.1
  497.7 2.0 pad_maximum_fusion
  499.7 0.0 copy-done.8
  499.7 0.0 copy-done.5
  499.8 0.0 copy-done.6
  499.8 0.7 pad_maximum_fusion.4
  500.5 0.8 pad_maximum_fusion.2
  501.3 0.1 constant_dynamic-slice_fusion
  501.4 0.6 copy.56
  502.0 0.7 constant_dynamic-slice_fusion.1
  502.7 0.6 constant_dynamic-slice_fusion.2
  503.3 0.6 copy.57
  503.9 1.7 copy.73
  (29 shorter events, 0.2 us)
Async XLA Ops:
  0.6 48.6 %copy-start.11 = (bf16[2,12,33]{2,0,1:T(2,128)(2,1)S(1)}, bf16[2,12,33]{2,0,1:T(2,128)(2,1)}, u32[]{:S(2)}) copy-start(bf16[2,12,33]{2,0,1:T(2,128)(2,1)} %param.19) | copy-start | bytes 4756
  0.7 50.1 %copy-start.2 = (bf16[2,96,768]{2,1,0:T(8,128)(2,1)S(1)}, bf16[2,96,768]{2,1,0:T(8,128)(2,1)}, u32[]{:S(2)}) copy-start(bf16[2,96,768]{2,1,0:T(8,128)(2,1)} %param.16) | copy-start | bytes 884740
  0.7 50.8 %copy-start.1 = (bf16[1024,768]{1,0:T(8,128)(2,1)S(1)}, bf16[1024,768]{1,0:T(8,128)(2,1)}, u32[]{:S(2)}) copy-start(bf16[1024,768]{1,0:T(8,128)(2,1)} %param.10) | copy-start | bytes 4718596
  432.6 63.2 %copy-start.3 = (f32[96,768]{1,0:T(8,128)S(1)}, f32[96,768]{1,0:T(8,128)}, u32[]{:S(2)}) copy-start(f32[96,768]{1,0:T(8,128)} %get-tuple-element.333) | copy-start | bytes 884740
  432.6 65.1 %copy-start.4 = (f32[24,3072]{1,0:T(8,128)S(1)}, f32[24,3072]{1,0:T(8,128)}, u32[]{:S(2)}) copy-start(f32[24,3072]{1,0:T(8,128)} %get-tuple-element.330) | copy-start | bytes 884740
  495.7 3.9 copy-start.8
  495.7 3.9 copy-start.10
  495.7 4.0 copy-start.7
  495.8 4.0 copy-start.5
  495.8 4.0 copy-start.6
  497.7 3.6 copy-start.9
  497.7 6.3 %copy-start = (f32[1024,768]{1,0:T(8,128)S(1)}, f32[1024,768]{1,0:T(8,128)}, u32[]{:S(2)}) copy-start(f32[1024,768]{1,0:T(8,128)} %get-tuple-element.399) | copy-start | bytes 9437188

commit v5 on v4

--- a/solution.py
+++ b/solution.py
@@ -42,7 +42,10 @@
 
 
 def dot3(a, b, dims):
-    return dot(a[0], b[0], dims) + (dot(a[0], b[1], dims) + dot(a[1], b[0], dims))
+    if dims is NN:
+        return dot(a[0], b[0], dims) + (dot(a[0], b[1], dims) + dot(a[1], b[0], dims))
+    (i,), (j,) = dims[0]
+    return dot(jnp.concatenate([a[0], a[0], a[1]], axis=i), jnp.concatenate([b[0], b[1], b[0]], axis=j), dims)
 
 
 def rows(start, size):

time: 516 us -> 507 us (0.983)
  Pallas kernels: 476 us -> 466 us
    pallas_call x13, Pallas kernels: 476 us -> 466 us  [call(): pl.pallas_call(run, out_shape=list(out_shape) + [o for o, _ in lane_outs]...]
where the time goes in v5:
time: 507 us; the launch traced here: 497 us
  Pallas kernels  466 us (92%)
  local copies, waits for them, and re-layouts  17.3 us (3%)
  other arithmetic  11.6 us (2%)
    pallas_call x13, Pallas kernels, call(): pl.pallas_call(run, out_shape=list(out_shape) + [o for o, _ in lane_outs]...  466 us

profile of v5, /device:TPU:0, one launch (start us, length us, event | category | flops | bytes accessed | tf_op | source)
XLA Modules:
  0.0 496.7 jit_solution(10003365634633620602)
XLA Ops:
  0.6 0.0 copy-start.11
  0.7 0.0 copy-start.2
  0.7 0.0 copy-start.1
  0.7 1.1 slice_bitcast_fusion.4
  1.8 0.8 slice_bitcast_fusion.9
  2.6 0.6 pad_maximum_fusion.6
  3.2 0.8 reshape.147
  4.0 0.1 copy.48
  4.1 0.1 copy.50
  4.2 0.7 copy.47
  4.9 0.7 maximum_bitcast_fusion
  5.5 0.1 copy.49
  5.6 0.1 fusion.4
  5.7 0.6 pad_maximum_fusion.5.refs_0_
  6.4 1.7 slice_bitcast_fusion.1
  8.1 41.1 %exchange.1 = (bf16[4,24,1664]{2,1,0:T(8,128)(2,1)}, bf16[4,24,1536]{2,1,0:T(8,128)(2,1)}, bf16[4,24,1664]{2,1,0:T(8,128)(2,1)}, bf16[4,24,1664]{2,1,0:T(8,128)(...) custom-call(bf16[24,1664]{1,0:T(8,128)(2,1)} %pad_maximum_fusion.5.r, ...), custom_call_target="tpu_custom_call" | custom-call | bytes 10000000 | tf_op jit(solution)/shard_map/exchange/pallas_call | solution.py:194
  49.2 0.0 copy-done.11
  49.2 0.1 rev.6
  49.3 0.7 fusion.1.refs_1_.refs_9_
  50.1 0.7 pad_maximum_fusion.3.refs_22_
  50.8 0.0 copy-done.2
  50.8 0.7 slice_bitcast_fusion
  51.5 0.0 copy-done.1
  51.5 0.7 copy.43
  52.2 2.1 convert_bitcast_fusion.refs_0_
  54.3 64.1 %attention.2 = (bf16[768,1024]{1,0:T(8,128)(2,1)}, bf16[2304,1024]{1,0:T(8,128)(2,1)}, bf16[1536,64]{1,0:T(8,128)(2,1)}, f32[768,128]{1,0:T(8,128)}, bf16[768,10...) custom-call(f32[768,1024]{1,0:T(8,128)} %convert_bitcast_fusion.refs, ...), custom_call_target="tpu_custom_call" | custom-call | flops 6800000000 | bytes 40000000 | tf_op jit(solution)/shard_map/attention/pallas_call | solution.py:194
  118.4 1.4 fusion.5
  119.8 1.5 reshape.188.refs_2_
  121.3 37.0 %feed.2 = (bf16[3072,1024]{1,0:T(8,128)(2,1)}, bf16[3072,1024]{1,0:T(8,128)(2,1)}, f32[768,1024]{1,0:T(8,128)}, f32[8,1024]{1,0:T(8,128)}, f32[768,1024]{1,0:T(8...) custom-call(f32[768,1024]{1,0:T(8,128)} %get-tuple-element.189.refs_, ...), custom_call_target="tpu_custom_call" | custom-call | flops 9799999488 | bytes 40000000 | tf_op jit(solution)/shard_map/feed/pallas_call | solution.py:194
  158.3 0.1 rev.7
  158.4 0.7 fusion.refs_2_.refs_9_
  159.2 44.2 %attention.3 = (bf16[768,1024]{1,0:T(8,128)(2,1)}, bf16[2304,1024]{1,0:T(8,128)(2,1)}, bf16[1536,64]{1,0:T(8,128)(2,1)}, bf16[768,1024]{1,0:T(8,128)(2,1)}, bf16...) custom-call(f32[768,1024]{1,0:T(8,128)} %get-tuple-element.208.refs_, ...), custom_call_target="tpu_custom_call" | custom-call | flops 6800000000 | bytes 40000000 | tf_op jit(solution)/shard_map/attention/pallas_call | solution.py:194
  203.4 1.5 reshape.189.refs_2_
  204.9 25.0 %feed.3 = (bf16[3072,1024]{1,0:T(8,128)(2,1)}, bf16[3072,1024]{1,0:T(8,128)(2,1)}, f32[768,1024]{1,0:T(8,128)}, f32[8,1024]{1,0:T(8,128)}, bf16[1024,768]{1,0:T(8,128)(2,1)}) custom-call(f32[768,1024]{1,0:T(8,128)} %get-tuple-element.218.refs_0_.refs_3_, f32[768,128]{1,0:T(8,128)} %get-tuple-element.190.refs_1_.refs_4_.refs_5_, f32[3072,1]{1,0:T(8,128)} %reshape.189.refs_2_, ...), custom_call_target="tpu_custom_call" | custom-call | flops 9799999488 | bytes 40000000 | tf_op jit(solution)/shard_map/feed/pallas_call | solution.py:194
  229.9 0.8 broadcast_in_dim.7.refs_0_
  230.7 21.9 %hidden.2 = (bf16[4,384,768]{2,1,0:T(8,128)(2,1)}, bf16[4,384,768]{2,1,0:T(8,128)(2,1)}, bf16[3072,1024]{1,0:T(8,128)(2,1)}, f32[768,1024]{1,0:T(8,128)}, f32[768,128]{1,0:T(8,128)}) custom-call(f32[768,128]{1,0:T(8,128)} %broadcast_in_dim.7.refs_0_, bf16[1024,768]{1,0:T(8,128)(2,1)} %refs_1_.1, f32[768,1024]{1,0:T(8,128)} %get-tuple-element.233.refs_2_, ...), custom_call_target="tpu_custom_call" | custom-call | flops 9699999744 | bytes 40000000 | tf_op jit(solution)/shard_map/hidden/pallas_call | solution.py:194
  252.7 22.8 %inner.2 = (bf16[384,3072]{1,0:T(8,128)(2,1)}, bf16[384,3072]{1,0:T(8,128)(2,1)}, f32[768,1024]{1,0:T(8,128)}, f32[768,128]{1,0:T(8,128)}, bf16[768,768]{1,0:T(8,128)(2,1)}, /*index=5*/bf16[768,768]{1,0:T(8,128)(2,1)}) custom-call(f32[768,128]{1,0:T(8,128)} %get-tuple-element.237.refs_0_, bf16[3072,1024]{1,0:T(8,128)(2,1)} %get-tuple-element.238.refs_1_, ...), custom_call_target="tpu_custom_call" | custom-call | flops 9699999744 | bytes 35000000 | tf_op jit(solution)/shard_map/inner/pallas_call | solution.py:194
  275.5 0.6 broadcast_in_dim.6.refs_0_
  276.1 23.3 %values.2 = (bf16[384,1536]{1,0:T(8,128)(2,1)}, bf16[384,1536]{1,0:T(8,128)(2,1)}, bf16[768,1024]{1,0:T(8,128)(2,1)}, bf16[768,1024]{1,0:T(8,128)(2,1)}, f32[12,...) custom-call(f32[24,896]{1,0:T(8,128)} %broadcast_in_dim.6.refs_0_, ...), custom_call_target="tpu_custom_call" | custom-call | flops 6200000000 | bytes 25000000 | tf_op jit(solution)/shard_map/values/pallas_call | solution.py:194
  299.4 38.6 %back.2 = (bf16[384,1536]{1,0:T(8,128)(2,1)}, bf16[384,1536]{1,0:T(8,128)(2,1)}, f32[768,1024]{1,0:T(8,128)}, f32[768,128]{1,0:T(8,128)}, f32[96,768]{1,0:T(8,12...) custom-call(f32[768,128]{1,0:T(8,128)} %get-tuple-element.256.refs_0, ...), custom_call_target="tpu_custom_call" | custom-call | flops 10000000000 | bytes 50000000 | tf_op jit(solution)/shard_map/back/pallas_call | solution.py:194
  338.1 27.6 %hidden.3 = (bf16[4,384,768]{2,1,0:T(8,128)(2,1)}, bf16[4,384,768]{2,1,0:T(8,128)(2,1)}, bf16[3072,1024]{1,0:T(8,128)(2,1)}, f32[768,1024]{1,0:T(8,128)}, f32[76...) custom-call(f32[768,128]{1,0:T(8,128)} %get-tuple-element.270.refs_0, ...), custom_call_target="tpu_custom_call" | custom-call | flops 9699999744 | bytes 40000000 | tf_op jit(solution)/shard_map/hidden/pallas_call | solution.py:194
  365.7 30.1 %inner.3 = (bf16[384,3072]{1,0:T(8,128)(2,1)}, bf16[384,3072]{1,0:T(8,128)(2,1)}, f32[768,1024]{1,0:T(8,128)}, f32[768,128]{1,0:T(8,128)}, bf16[384,768]{1,0:T(8...) custom-call(f32[768,128]{1,0:T(8,128)} %get-tuple-element.282.refs_0, ...), custom_call_target="tpu_custom_call" | custom-call | flops 9699999744 | bytes 35000000 | tf_op jit(solution)/shard_map/inner/pallas_call | solution.py:194
  395.8 31.3 %values.3 = (bf16[384,1536]{1,0:T(8,128)(2,1)}, bf16[384,1536]{1,0:T(8,128)(2,1)}, bf16[768,1024]{1,0:T(8,128)(2,1)}, bf16[768,1024]{1,0:T(8,128)(2,1)}, f32[12,...) custom-call(f32[24,896]{1,0:T(8,128)} %get-tuple-element.255.refs_0_, ...), custom_call_target="tpu_custom_call" | custom-call | flops 6200000000 | bytes 25000000 | tf_op jit(solution)/shard_map/values/pallas_call | solution.py:194
  427.1 0.0 copy-start.3
  427.1 0.0 copy-start.4
  427.1 59.2 %back.3 = (f32[1024,768]{1,0:T(8,128)}, f32[768,128]{1,0:T(8,128)}, f32[24,512]{1,0:T(8,128)}, f32[24,1024]{1,0:T(8,128)}, f32[24,896]{1,0:T(8,128)}, /*index=5*...) custom-call(f32[768,128]{1,0:T(8,128)} %get-tuple-element.308.refs_0_, ...), custom_call_target="tpu_custom_call" | custom-call | flops 10000000000 | bytes 50000000 | tf_op jit(solution)/shard_map/back/pallas_call | solution.py:194
  486.4 0.0 copy-start.8
  486.4 0.0 copy-start.10
  486.4 0.0 copy-start.7
  486.4 0.0 copy-start.5
  486.4 0.0 copy-done.3
  486.4 0.0 copy-start.6
  486.4 1.9 pad_maximum_fusion.1
  488.3 2.0 pad_maximum_fusion
  490.3 0.0 copy-done.7
  490.5 0.7 pad_maximum_fusion.4
  491.1 0.8 pad_maximum_fusion.2
  491.9 0.0 copy-done.9
  491.9 0.1 constant_dynamic-slice_fusion
  492.0 0.6 copy.56
  492.6 0.7 constant_dynamic-slice_fusion.1
  493.3 0.6 constant_dynamic-slice_fusion.2
  494.0 0.6 copy.57
  494.6 1.7 copy.73
  (29 shorter events, 0.2 us)
Async XLA Ops:
  0.6 48.6 %copy-start.11 = (bf16[2,12,33]{2,0,1:T(2,128)(2,1)S(1)}, bf16[2,12,33]{2,0,1:T(2,128)(2,1)}, u32[]{:S(2)}) copy-start(bf16[2,12,33]{2,0,1:T(2,128)(2,1)} %param.19) | copy-start | bytes 4756
  0.7 50.1 %copy-start.2 = (bf16[2,96,768]{2,1,0:T(8,128)(2,1)S(1)}, bf16[2,96,768]{2,1,0:T(8,128)(2,1)}, u32[]{:S(2)}) copy-start(bf16[2,96,768]{2,1,0:T(8,128)(2,1)} %param.16) | copy-start | bytes 884740
  0.7 50.8 %copy-start.1 = (bf16[1024,768]{1,0:T(8,128)(2,1)S(1)}, bf16[1024,768]{1,0:T(8,128)(2,1)}, u32[]{:S(2)}) copy-start(bf16[1024,768]{1,0:T(8,128)(2,1)} %param.10) | copy-start | bytes 4718596
  427.1 59.3 %copy-start.3 = (f32[96,768]{1,0:T(8,128)S(1)}, f32[96,768]{1,0:T(8,128)}, u32[]{:S(2)}) copy-start(f32[96,768]{1,0:T(8,128)} %get-tuple-element.333) | copy-start | bytes 884740
  427.1 61.2 %copy-start.4 = (f32[24,3072]{1,0:T(8,128)S(1)}, f32[24,3072]{1,0:T(8,128)}, u32[]{:S(2)}) copy-start(f32[24,3072]{1,0:T(8,128)} %get-tuple-element.330) | copy-start | bytes 884740
  486.4 3.9 copy-start.8
  486.4 3.9 copy-start.10
  486.4 4.0 copy-start.7
  486.4 4.0 copy-start.5
  486.4 4.0 copy-start.6
  488.3 3.6 copy-start.9
  488.3 6.3 %copy-start = (f32[1024,768]{1,0:T(8,128)S(1)}, f32[1024,768]{1,0:T(8,128)}, u32[]{:S(2)}) copy-start(f32[1024,768]{1,0:T(8,128)} %get-tuple-element.399) | copy-start | bytes 9437188

commit v6 on v5

--- a/solution.py
+++ b/solution.py
@@ -694,12 +694,22 @@
         return dx * (1 + core) + dy * (2 - core)
 
 
-def exchange(lanes, turns):
-    def kernel(hook):
-        for i in range(turns):
+def exchange(tokens, lanes, turns):
+    def kernel(tokens_from, x_out, tokens_ref, x_ref, sem, hook):
+        load = pltpu.make_async_copy(tokens_from, tokens_ref, sem.at[0])
+        load.start()
+        hook(0)
+        load.wait()
+        x_ref[...] = tokens_ref[...].astype(f32).T
+        leave = pltpu.make_async_copy(x_ref, x_out, sem.at[1])
+        leave.start()
+        for i in range(1, turns):
             hook(i)
-
-    call(kernel, "exchange", [], [], [], [], (), lanes, 0, 10_000_000)
+        leave.wait()
+
+    return call(
+        kernel, "exchange", [sd(D, T)], [ANY], [ANY],
+        [pltpu.VMEM((T, D), bf16), pltpu.VMEM((D, T), f32), DMA((2,))], (tokens,), lanes, 0, 10_000_000)[0]
 
 
 def attention_kernel(sizes, p, x_ref, *rest, hook):
@@ -1514,7 +1524,6 @@
     plan = Plan()
     none = (None, ())
     on = ring.exact and layers == 2
-    x = tokens.T.astype(f32)
     conv = [conv_rows(conv_w[layer]) for layer in range(layers)]
     on_attention, on_feed = [none] * layers, [none] * layers
     qkvo = [jnp.concatenate([qkv_w[layer], out_w[layer]], axis=1) for layer in range(layers)]
@@ -1526,7 +1535,7 @@
         g3 = Gather(s3)
         m1 = g1.go(a=(1, 2), b=(2, 4), core0=(1, 8), core1=(2, 8), core2=(4, 8))
         m2 = g2.go(apart=1, a=(3, 5), b=(5, 7), core0=(3, 9), core1=(5, 9), core2=(7, 9))
-        exchange(plan.lanes(s1, s2, *m1, *m2, s3), 10)
+        x = exchange(tokens, plan.lanes(s1, s2, *m1, *m2, s3), 10)
         att = [[g1.pieces(), g2.pieces()], None]
         win, wout = [None] * 2, [None] * 2
         s4, s5 = Spread(out2_w[0], 0, 6), Spread(qkvo[1], 6, 10)
@@ -1537,6 +1546,7 @@
         m5 = g5.go(a=(10, 12))
         on_attention[0] = plan.lanes(s4, *m3, *m4, s5, *m5)
     else:
+        x = tokens.T.astype(f32)
         shards = [jnp.concatenate([qkvo[0], small], axis=1)] + qkvo[1:]
         att, win, wout = gather_all(ring, shards, in_w, out2_w)
         att = [[pieces] for pieces in att]
@@ -1551,7 +1561,7 @@
             win[0], wout[0] = g3.pieces(), g4.pieces()
             s6, s7 = Spread(in_w[1], 0, 3), Spread(out2_w[1], 3, 5)
             g6, g7 = Gather(s6), Gather(s7)
-            m5 = g5.go(b=(0, 3), core0=(0, 3), core1=(0, 3), core2=(3, 5))
+            m5 = g5.go(apart=1, b=(0, 3), core0=(0, 3), core1=(0, 3), core2=(3, 5))
             m6 = g6.go(a=(3, 5))
             on_feed[0] = plan.lanes(*m5, s6, s7, *m6)
         if on and layer == 1:

time: 507 us -> 503 us (level)
  no operation moved by 1% of the time
where the time goes in v6:
time: 503 us; the launch traced here: 493 us
  Pallas kernels  466 us (93%)
  local copies, waits for them, and re-layouts  16.4 us (3%)
  other arithmetic  9.55 us (2%)
    pallas_call x13, Pallas kernels, call(): pl.pallas_call(run, out_shape=list(out_shape) + [o for o, _ in lane_outs]...  466 us

profile of v6, /device:TPU:0, one launch (start us, length us, event | category | flops | bytes accessed | tf_op | source)
XLA Modules:
  0.0 493.1 jit_solution(14618948432117680138)
XLA Ops:
  0.6 1.0 slice_bitcast_fusion.4
  1.6 0.8 slice_bitcast_fusion.9
  2.4 0.6 pad_maximum_fusion.6
  3.1 0.8 reshape.147
  3.8 0.1 copy.42
  3.9 0.1 copy.44
  4.0 0.7 copy.41
  4.7 0.7 maximum_bitcast_fusion
  5.4 0.1 copy.43
  5.5 0.1 fusion.4
  5.6 0.6 pad_maximum_fusion.5.refs_1_
  6.2 1.7 slice_bitcast_fusion.1
  7.9 41.1 %exchange.1 = (f32[768,1024]{1,0:T(8,128)}, bf16[4,24,1664]{2,1,0:T(8,128)(2,1)}, bf16[4,24,1536]{2,1,0:T(8,128)(2,1)}, bf16[4,24,1664]{2,1,0:T(8,128)(2,1)}, bf...) custom-call(bf16[1024,768]{1,0:T(8,128)(2,1)} %refs_0_.1, ...), custom_call_target="tpu_custom_call" | custom-call | bytes 10000000 | tf_op jit(solution)/shard_map/exchange/pallas_call | solution.py:194
  49.1 0.0 copy-done.10
  49.1 0.1 rev.6
  49.2 0.7 fusion.1.refs_1_.refs_9_
  49.9 0.7 pad_maximum_fusion.3.refs_22_
  50.6 0.0 copy-done.1
  50.6 0.7 slice_bitcast_fusion
  51.3 64.1 %attention.2 = (bf16[768,1024]{1,0:T(8,128)(2,1)}, bf16[2304,1024]{1,0:T(8,128)(2,1)}, bf16[1536,64]{1,0:T(8,128)(2,1)}, f32[768,128]{1,0:T(8,128)}, bf16[768,10...) custom-call(f32[768,1024]{1,0:T(8,128)} %get-tuple-element.173.refs_, ...), custom_call_target="tpu_custom_call" | custom-call | flops 6800000000 | bytes 40000000 | tf_op jit(solution)/shard_map/attention/pallas_call | solution.py:194
  115.4 1.4 fusion.5
  116.8 1.5 reshape.188.refs_2_
  118.3 36.2 %feed.2 = (bf16[3072,1024]{1,0:T(8,128)(2,1)}, bf16[3072,1024]{1,0:T(8,128)(2,1)}, f32[768,1024]{1,0:T(8,128)}, f32[8,1024]{1,0:T(8,128)}, f32[768,1024]{1,0:T(8...) custom-call(f32[768,1024]{1,0:T(8,128)} %get-tuple-element.191.refs_, ...), custom_call_target="tpu_custom_call" | custom-call | flops 9799999488 | bytes 40000000 | tf_op jit(solution)/shard_map/feed/pallas_call | solution.py:194
  154.5 0.1 rev.7
  154.6 0.7 fusion.refs_2_.refs_9_
  155.4 44.2 %attention.3 = (bf16[768,1024]{1,0:T(8,128)(2,1)}, bf16[2304,1024]{1,0:T(8,128)(2,1)}, bf16[1536,64]{1,0:T(8,128)(2,1)}, bf16[768,1024]{1,0:T(8,128)(2,1)}, bf16...) custom-call(f32[768,1024]{1,0:T(8,128)} %get-tuple-element.210.refs_, ...), custom_call_target="tpu_custom_call" | custom-call | flops 6800000000 | bytes 40000000 | tf_op jit(solution)/shard_map/attention/pallas_call | solution.py:194
  199.6 1.5 reshape.189.refs_2_
  201.1 25.0 %feed.3 = (bf16[3072,1024]{1,0:T(8,128)(2,1)}, bf16[3072,1024]{1,0:T(8,128)(2,1)}, f32[768,1024]{1,0:T(8,128)}, f32[8,1024]{1,0:T(8,128)}, bf16[1024,768]{1,0:T(8,128)(2,1)}) custom-call(f32[768,1024]{1,0:T(8,128)} %get-tuple-element.220.refs_0_.refs_3_, f32[768,128]{1,0:T(8,128)} %get-tuple-element.192.refs_1_.refs_4_.refs_5_, f32[3072,1]{1,0:T(8,128)} %reshape.189.refs_2_, ...), custom_call_target="tpu_custom_call" | custom-call | flops 9799999488 | bytes 40000000 | tf_op jit(solution)/shard_map/feed/pallas_call | solution.py:194
  226.1 0.8 broadcast_in_dim.7.refs_0_
  226.9 21.9 %hidden.2 = (bf16[4,384,768]{2,1,0:T(8,128)(2,1)}, bf16[4,384,768]{2,1,0:T(8,128)(2,1)}, bf16[3072,1024]{1,0:T(8,128)(2,1)}, f32[768,1024]{1,0:T(8,128)}, f32[768,128]{1,0:T(8,128)}) custom-call(f32[768,128]{1,0:T(8,128)} %broadcast_in_dim.7.refs_0_, bf16[1024,768]{1,0:T(8,128)(2,1)} %refs_1_.1, f32[768,1024]{1,0:T(8,128)} %get-tuple-element.235.refs_2_, ...), custom_call_target="tpu_custom_call" | custom-call | flops 9699999744 | bytes 40000000 | tf_op jit(solution)/shard_map/hidden/pallas_call | solution.py:194
  248.9 22.8 %inner.2 = (bf16[384,3072]{1,0:T(8,128)(2,1)}, bf16[384,3072]{1,0:T(8,128)(2,1)}, f32[768,1024]{1,0:T(8,128)}, f32[768,128]{1,0:T(8,128)}, bf16[768,768]{1,0:T(8,128)(2,1)}, /*index=5*/bf16[768,768]{1,0:T(8,128)(2,1)}) custom-call(f32[768,128]{1,0:T(8,128)} %get-tuple-element.239.refs_0_, bf16[3072,1024]{1,0:T(8,128)(2,1)} %get-tuple-element.240.refs_1_, ...), custom_call_target="tpu_custom_call" | custom-call | flops 9699999744 | bytes 35000000 | tf_op jit(solution)/shard_map/inner/pallas_call | solution.py:194
  271.6 0.6 broadcast_in_dim.6.refs_0_
  272.3 23.3 %values.2 = (bf16[384,1536]{1,0:T(8,128)(2,1)}, bf16[384,1536]{1,0:T(8,128)(2,1)}, bf16[768,1024]{1,0:T(8,128)(2,1)}, bf16[768,1024]{1,0:T(8,128)(2,1)}, f32[12,...) custom-call(f32[24,896]{1,0:T(8,128)} %broadcast_in_dim.6.refs_0_, ...), custom_call_target="tpu_custom_call" | custom-call | flops 6200000000 | bytes 25000000 | tf_op jit(solution)/shard_map/values/pallas_call | solution.py:194
  295.6 38.9 %back.2 = (bf16[384,1536]{1,0:T(8,128)(2,1)}, bf16[384,1536]{1,0:T(8,128)(2,1)}, f32[768,1024]{1,0:T(8,128)}, f32[768,128]{1,0:T(8,128)}, f32[96,768]{1,0:T(8,12...) custom-call(f32[768,128]{1,0:T(8,128)} %get-tuple-element.258.refs_0, ...), custom_call_target="tpu_custom_call" | custom-call | flops 10000000000 | bytes 50000000 | tf_op jit(solution)/shard_map/back/pallas_call | solution.py:194
  334.5 27.4 %hidden.3 = (bf16[4,384,768]{2,1,0:T(8,128)(2,1)}, bf16[4,384,768]{2,1,0:T(8,128)(2,1)}, bf16[3072,1024]{1,0:T(8,128)(2,1)}, f32[768,1024]{1,0:T(8,128)}, f32[76...) custom-call(f32[768,128]{1,0:T(8,128)} %get-tuple-element.272.refs_0, ...), custom_call_target="tpu_custom_call" | custom-call | flops 9699999744 | bytes 40000000 | tf_op jit(solution)/shard_map/hidden/pallas_call | solution.py:194
  361.9 30.3 %inner.3 = (bf16[384,3072]{1,0:T(8,128)(2,1)}, bf16[384,3072]{1,0:T(8,128)(2,1)}, f32[768,1024]{1,0:T(8,128)}, f32[768,128]{1,0:T(8,128)}, bf16[384,768]{1,0:T(8...) custom-call(f32[768,128]{1,0:T(8,128)} %get-tuple-element.284.refs_0, ...), custom_call_target="tpu_custom_call" | custom-call | flops 9699999744 | bytes 35000000 | tf_op jit(solution)/shard_map/inner/pallas_call | solution.py:194
  392.2 31.2 %values.3 = (bf16[384,1536]{1,0:T(8,128)(2,1)}, bf16[384,1536]{1,0:T(8,128)(2,1)}, bf16[768,1024]{1,0:T(8,128)(2,1)}, bf16[768,1024]{1,0:T(8,128)(2,1)}, f32[12,...) custom-call(f32[24,896]{1,0:T(8,128)} %get-tuple-element.257.refs_0_, ...), custom_call_target="tpu_custom_call" | custom-call | flops 6200000000 | bytes 25000000 | tf_op jit(solution)/shard_map/values/pallas_call | solution.py:194
  423.5 0.0 copy-start.2
  423.5 0.0 copy-start.3
  423.5 59.3 %back.3 = (f32[1024,768]{1,0:T(8,128)}, f32[768,128]{1,0:T(8,128)}, f32[24,512]{1,0:T(8,128)}, f32[24,1024]{1,0:T(8,128)}, f32[24,896]{1,0:T(8,128)}, /*index=5*...) custom-call(f32[768,128]{1,0:T(8,128)} %get-tuple-element.310.refs_0_, ...), custom_call_target="tpu_custom_call" | custom-call | flops 10000000000 | bytes 50000000 | tf_op jit(solution)/shard_map/back/pallas_call | solution.py:194
  482.8 0.0 copy-start.7
  482.8 0.0 copy-start.9
  482.8 0.0 copy-start.6
  482.8 0.0 copy-start.4
  482.8 0.0 copy-done.2
  482.8 0.0 copy-start.5
  482.8 1.9 pad_maximum_fusion.1
  484.7 0.0 copy-done.3
  484.7 2.0 pad_maximum_fusion
  486.7 0.0 copy-done.7
  486.7 0.0 copy-done.9
  486.7 0.0 copy-done.6
  486.8 0.0 copy-done.4
  486.8 0.0 copy-done.5
  486.9 0.7 pad_maximum_fusion.4
  487.5 0.8 pad_maximum_fusion.2
  488.3 0.0 copy-done.8
  488.4 0.1 constant_dynamic-slice_fusion
  488.4 0.6 copy.53
  489.0 0.7 constant_dynamic-slice_fusion.1
  489.7 0.6 constant_dynamic-slice_fusion.2
  490.4 0.6 copy.54
  491.0 0.0 copy-done
  491.0 1.7 copy.70
  (25 shorter events, 0.2 us)
Async XLA Ops:
  2.4 46.6 %copy-start.10 = (bf16[2,12,33]{2,0,1:T(2,128)(2,1)S(1)}, bf16[2,12,33]{2,0,1:T(2,128)(2,1)}, u32[]{:S(2)}) copy-start(bf16[2,12,33]{2,0,1:T(2,128)(2,1)} %param.19) | copy-start | bytes 4756
  5.6 45.1 %copy-start.1 = (bf16[2,96,768]{2,1,0:T(8,128)(2,1)S(1)}, bf16[2,96,768]{2,1,0:T(8,128)(2,1)}, u32[]{:S(2)}) copy-start(bf16[2,96,768]{2,1,0:T(8,128)(2,1)} %param.16) | copy-start | bytes 884740
  423.5 59.3 %copy-start.2 = (f32[96,768]{1,0:T(8,128)S(1)}, f32[96,768]{1,0:T(8,128)}, u32[]{:S(2)}) copy-start(f32[96,768]{1,0:T(8,128)} %get-tuple-element.335) | copy-start | bytes 884740
  423.5 61.3 %copy-start.3 = (f32[24,3072]{1,0:T(8,128)S(1)}, f32[24,3072]{1,0:T(8,128)}, u32[]{:S(2)}) copy-start(f32[24,3072]{1,0:T(8,128)} %get-tuple-element.332) | copy-start | bytes 884740
  482.8 3.9 copy-start.7
  482.8 3.9 copy-start.9
  482.8 4.0 copy-start.6
  482.8 4.0 copy-start.4
  482.8 4.0 copy-start.5
  484.7 3.6 copy-start.8
  484.7 6.3 %copy-start = (f32[1024,768]{1,0:T(8,128)S(1)}, f32[1024,768]{1,0:T(8,128)}, u32[]{:S(2)}) copy-start(f32[1024,768]{1,0:T(8,128)} %get-tuple-element.401) | copy-start | bytes 9437188
